TPU v7x, 32 devices: a whole 2x2x4 slice. The times are simulated.
32 devices in a mesh: grp: 4 (over y, x), blk: 8 (over z, core).
Axes of the slice: x: 2, y: 2, z: 4, core: 2. Of those that a mesh axis runs over, the one named last changes fastest.
Arguments:
- tokens: bfloat16 [2048, 4096], P(('blk', 'grp')), may hold values from -16 to 16
- w_query: bfloat16 [4096, 4096], P(None, 'grp'), may hold values from -0.09375 to 0.09375
- key_weight: bfloat16 [4096, 1024], P(None, 'grp'), may hold values from -0.09375 to 0.09375
- value_weight: bfloat16 [4096, 1024], P(None, 'grp'), may hold values from -0.09375 to 0.09375
- w_output: bfloat16 [4096, 4096], P('grp'), may hold values from -0.09375 to 0.09375
- block_mask: int32 [16, 16], P('blk'), may hold values from 0 to 1, as said below
- positions: int32 [2048], P('blk'), may hold values from 0 to 69629, as said below
Outputs:
- attended: bfloat16 [2048, 4096], P(('blk', 'grp'))
Inputs may be any that keep to these rules, and one draw needn't show every extreme that they name: block_mask[i, j] is 1 exactly where |i - j| <= 1, where i < 1 or j < 1, or where j is one of 3 distinct blocks drawn for row i; so query blocks below 1 attend every key block. A sequence block is a run of 256 tokens from a multiple of 256. The drawn blocks of a row never lie in its own sequence block, in the two sequence blocks beside it (the last and the first count as beside each other) or in the first sequence block. Over the query blocks of one sequence block, other than those below 1, the live key blocks that lie outside that sequence block, are not the block just before or just after it, and are not below 1, number at most 2 in any one other sequence block. positions rise along the sequence by 1 or 2 per token; the last token's position is the most.
All inputs are finite; a program needn't handle non-finite values.
Results may differ from a plain program's by a relative error of at most 0.017.
Values may be sent and summed in bfloat16 or wider, within the bound.
No kernel may reach another device: no remote copies, remote signals or barrier semaphores. Data moves between devices by JAX's collectives and lax.ppermute only.
A program may use at most 64 MiB of HBM per device.

v0:
```python
import jax
import jax.numpy as jnp
from jax import lax
from jax.sharding import PartitionSpec as P

HEAD_WIDTH = 128
MASK_BLOCK_TOKENS = 128


NEG_FILL = -1e30


def rotary_position(projected, positions, heads):
    half = HEAD_WIDTH // 2
    inverse = jnp.power(
        jnp.float32(500000.0), -(2.0 * jnp.arange(half, dtype=jnp.float32)) / HEAD_WIDTH
    )
    angles = positions.astype(jnp.float32)[:, None] * inverse[None, :]
    cosine = jnp.cos(angles)[:, None, :]
    sine = jnp.sin(angles)[:, None, :]
    shaped = projected.reshape(projected.shape[0], heads, HEAD_WIDTH)
    first = shaped[..., :half]
    second = shaped[..., half:]
    turned = jnp.concatenate(
        [first * cosine - second * sine, second * cosine + first * sine], axis=-1
    )
    return turned.reshape(projected.shape[0], heads * HEAD_WIDTH)


def attend(state, query_tile, key_tile, value_tile, column_live):
    top_old, total_old, accum_old = state
    scores = jnp.einsum(
        "crd,gcd->crg", query_tile, key_tile, preferred_element_type=jnp.float32
    ) * HEAD_WIDTH ** (-0.5)
    scores = jnp.where(column_live[None, None, :], scores, NEG_FILL)
    top_new = jnp.maximum(top_old, jnp.max(scores, axis=-1))
    weights = jnp.where(column_live[None, None, :], jnp.exp(scores - top_new[..., None]), 0.0)
    factor = jnp.exp(top_old - top_new)
    total_new = total_old * factor + jnp.sum(weights, axis=-1)
    product = jnp.einsum(
        "crg,gcd->crd", weights.astype(jnp.bfloat16), value_tile, preferred_element_type=jnp.float32
    )
    return (top_new, total_new, accum_old * factor[..., None] + product)


def fold_tiles(fold_state, query_tiles, key_tile, value_tile, live_cols):

    def over_query(unused, query_items):
        query_tile, top_old, total_old, accum_old, live_blocks = query_items
        column_live = jnp.repeat(live_blocks, MASK_BLOCK_TOKENS)
        updated = lax.cond(
            jnp.any(live_blocks),
            lambda: attend(
                (top_old, total_old, accum_old), query_tile, key_tile, value_tile, column_live
            ),
            lambda: (top_old, total_old, accum_old),
        )
        return (unused, updated)

    unused, new_state = lax.scan(
        over_query, 0, (query_tiles, fold_state[0], fold_state[1], fold_state[2], live_cols)
    )
    return new_state


def body(tokens, w_query, key_weight, value_weight, w_output, block_mask, positions):
    query_cols = w_query.shape[1]
    key_cols = key_weight.shape[1]
    query_heads = query_cols // HEAD_WIDTH
    kv_heads = key_cols // HEAD_WIDTH
    head_repeat_count = query_heads // kv_heads
    tile_rows = head_repeat_count * MASK_BLOCK_TOKENS
    piece = lax.all_gather(tokens, "grp", axis=0, tiled=True)
    projected = jnp.concatenate(
        [
            jnp.dot(piece, w_query, preferred_element_type=jnp.float32),
            jnp.dot(piece, key_weight, preferred_element_type=jnp.float32),
            jnp.dot(piece, value_weight, preferred_element_type=jnp.float32),
        ],
        axis=1,
    )
    block_rows = projected.shape[0]
    query_rows = rotary_position(projected[:, :query_cols], positions, query_heads).astype(
        jnp.bfloat16
    )
    key_rows = rotary_position(
        projected[:, query_cols : query_cols + key_cols], positions, kv_heads
    ).astype(jnp.bfloat16)
    value_rows = projected[:, query_cols + key_cols :].astype(jnp.bfloat16)
    query_block_rows = block_rows // MASK_BLOCK_TOKENS
    query_tiles = query_rows.reshape(
        query_block_rows, MASK_BLOCK_TOKENS, kv_heads, head_repeat_count, HEAD_WIDTH
    )
    query_tiles = query_tiles.transpose(0, 2, 3, 1, 4).reshape(
        query_block_rows, kv_heads, tile_rows, HEAD_WIDTH
    )
    live_rows = block_mask != 0
    initial = (
        jnp.full((query_block_rows, kv_heads, tile_rows), NEG_FILL, jnp.float32),
        jnp.zeros((query_block_rows, kv_heads, tile_rows), jnp.float32),
        jnp.zeros((query_block_rows, kv_heads, tile_rows, HEAD_WIDTH), jnp.float32),
    )
    key_piece = lax.all_gather(key_rows, "blk", axis=0, tiled=True)
    value_piece = lax.all_gather(value_rows, "blk", axis=0, tiled=True)
    piece_rows = key_piece.shape[0]
    group_count = piece_rows // block_rows
    key_groups = key_piece.reshape(group_count, block_rows, kv_heads, HEAD_WIDTH)
    value_groups = value_piece.reshape(group_count, block_rows, kv_heads, HEAD_WIDTH)

    def over_group(fold_state, group_items):
        key_tile, value_tile, group_index = group_items
        first_key_block = group_index * block_rows // MASK_BLOCK_TOKENS
        live_cols = lax.dynamic_slice(
            live_rows,
            (jnp.int32(0), first_key_block),
            (query_block_rows, block_rows // MASK_BLOCK_TOKENS),
        )
        return (fold_tiles(fold_state, query_tiles, key_tile, value_tile, live_cols), 0)

    result, unused = lax.scan(
        over_group, initial, (key_groups, value_groups, jnp.arange(group_count))
    )
    top_all, total_all, accum_all = result
    safe_total = jnp.where(total_all > 0, total_all, 1.0)
    mixed_tiles = accum_all / safe_total[..., None]
    mixed = mixed_tiles.reshape(
        query_block_rows, kv_heads, head_repeat_count, MASK_BLOCK_TOKENS, HEAD_WIDTH
    )
    mixed = mixed.transpose(0, 3, 1, 2, 4).reshape(block_rows, query_cols).astype(jnp.bfloat16)
    term = jnp.dot(mixed, w_output, preferred_element_type=jnp.float32)
    return lax.psum_scatter(
        lax.optimization_barrier(term.astype(jnp.bfloat16))
        .astype(jnp.float32)
        .astype(jnp.bfloat16),
        "grp",
        scatter_dimension=0,
        tiled=True,
    )


def solution(mesh):
    return jax.shard_map(
        body,
        mesh=mesh,
        in_specs=(
            P(("blk", "grp"), None),
            P(None, "grp"),
            P(None, "grp"),
            P(None, "grp"),
            P("grp", None),
            P("blk", None),
            P("blk"),
        ),
        out_specs=P(("blk", "grp"), None),
        check_vma=False,
    )
```

profile of v0, /device:TPU:0, one launch (start us, length us, event | category | flops | bytes accessed | tf_op | source)
XLA Modules:
  0.0 311.8 jit_solution(14614113315192506937)
XLA Ops:
  8.3 38.9 %all-gather.4.cloned.1.call-done = bf16[256,4096]{1,0:T(8,128)(2,1)} async-done(((bf16[64,4096]{1,0:T(8,128)(2,1)}), bf16[256,4096]{1,0:T(8,128)(2,1)}) %all-gather.4.cloned.1.call-update) | async-done | bytes 2097168 | tf_op jit(solution)/shard_map/all_gather | solution.py:73
  47.3 2.5 fusion.14
  50.6 3.6 %convolution_convert_fusion.1 = bf16[256,256]{1,0:T(8,128)(2,1)} fusion(bf16[256,4096]{1,0:T(8,128)(2,1)} %all-gather.4.cloned.1.call-done, bf16[4096,256]{1,0:T(8,128)(2,1)} %param.16), kind=kOutput, calls=%fused_computation.30 | convolution fusion | flops 536936448 | bytes 4325376 | tf_op jit(solution)/shard_map/dot_general | solution.py:78
  54.5 6.5 %convolution_bitcast_fusion = f32[32,8,8,128]{3,1,2,0:T(8,128)S(1)} fusion(bf16[256,4096]{1,0:T(8,128)(2,1)} %all-gather.4.cloned.1.call-done, bf16[4096,1024]{1,0:T(8,128)(2,1)} %param.14), kind=kOutput, calls=%fused_computation.29 | convolution fusion | flops 2147483648 | bytes 11534336 | tf_op jit(solution)/shard_map/dot_general | solution.py:76
  62.0 12.6 %all-gather.6.cloned.1.call-done = bf16[2048,256]{0,1:T(8,128)(2,1)} async-done(((bf16[256,256]{0,1:T(8,128)(2,1)}), bf16[2048,256]{0,1:T(8,128)(2,1)}) %all-gather.6.cloned.1.call-update) | async-done | bytes 1048592 | tf_op jit(solution)/shard_map/all_gather | solution.py:103
  74.6 2.5 copy.22
  77.2 2.7 copy.17
  79.8 17.2 %all-gather.8.cloned.1.call-done = bf16[2048,256]{1,0:T(8,128)(2,1)} async-done(((bf16[256,256]{1,0:T(8,128)(2,1)}), bf16[2048,256]{1,0:T(8,128)(2,1)}) %all-gather.8.cloned.1.call-update) | async-done | bytes 1048592 | tf_op jit(solution)/shard_map/all_gather | solution.py:104
  100.2 162.1 %while.41 = (s32[]{:T(128)}, f32[2,2,512]{2,1,0:T(2,128)S(1)}, f32[2,2,512]{2,1,0:T(2,128)S(1)}, f32[2,2,512,128]{3,2,1,0:T(8,128)}, s32[8]{0:T(128)S(1)}, /*ind...) while((s32[]{:T(128)}, f32[2,2,512]{2,1,0:T(2,128)S(1)}, ...), condition=%wide.region_8.9_spmd, body=%wide.region_0.8_spmd.sunk | while | flops 136841232 | bytes 7702978 | solution.py:120
  103.5 18.4 %while.42 = (s32[]{:T(128)}, f32[2,2,512]{2,1,0:T(2,128)S(1)}, f32[2,2,512]{2,1,0:T(2,128)S(1)}, f32[2,2,512,128]{3,2,1,0:T(8,128)}, pred[2,2]{1,0:T(4,128)(4,1)...) while((s32[]{:T(128)}, f32[2,2,512]{2,1,0:T(2,128)S(1)}, ...), condition=%wide.region_7.7_spmd.clone, body=%wide.region_1.6_spmd.clone.sunk | while | flops 136841216 | bytes 6916081 | solution.py:60
  107.3 3.9 %conditional.3 = (f32[1,2,512]{2,1,0:T(2,128)}, f32[1,2,512]{2,1,0:T(2,128)S(1)}, f32[1,2,512,128]{3,2,1,0:T(8,128)S(1)}) conditional(s32[]{:T(128)} %convert_element_type.56, (f32[2,512]{1,0:T(2,128)}, f32[2,512]{1,0:T(2,128)S(1)}, f32[2,512,128]{2,1,0:T(8,128)S(1)}) %tuple.108, (pred[1,2]{1,0:T(4,128)(4,1)S(1)}, ...), branch_computations={%region_3.2_spmd, %region_4.5_spmd} | conditional | flops 136841216 | bytes 4777246 | solution.py:51
  116.5 3.9 %conditional.3 = (f32[1,2,512]{2,1,0:T(2,128)}, f32[1,2,512]{2,1,0:T(2,128)S(1)}, f32[1,2,512,128]{3,2,1,0:T(8,128)S(1)}) conditional(s32[]{:T(128)} %convert_element_type.56, (f32[2,512]{1,0:T(2,128)}, f32[2,512]{1,0:T(2,128)S(1)}, f32[2,512,128]{2,1,0:T(8,128)S(1)}) %tuple.108, (pred[1,2]{1,0:T(4,128)(4,1)S(1)}, ...), branch_computations={%region_3.2_spmd, %region_4.5_spmd} | conditional | flops 136841216 | bytes 4777246 | solution.py:51
  125.2 18.4 %while.42 = (s32[]{:T(128)}, f32[2,2,512]{2,1,0:T(2,128)S(1)}, f32[2,2,512]{2,1,0:T(2,128)S(1)}, f32[2,2,512,128]{3,2,1,0:T(8,128)}, pred[2,2]{1,0:T(4,128)(4,1)...) while((s32[]{:T(128)}, f32[2,2,512]{2,1,0:T(2,128)S(1)}, ...), condition=%wide.region_7.7_spmd.clone, body=%wide.region_1.6_spmd.clone.sunk | while | flops 136841216 | bytes 6916081 | solution.py:60
  129.0 3.9 %conditional.3 = (f32[1,2,512]{2,1,0:T(2,128)}, f32[1,2,512]{2,1,0:T(2,128)S(1)}, f32[1,2,512,128]{3,2,1,0:T(8,128)S(1)}) conditional(s32[]{:T(128)} %convert_element_type.56, (f32[2,512]{1,0:T(2,128)}, f32[2,512]{1,0:T(2,128)S(1)}, f32[2,512,128]{2,1,0:T(8,128)S(1)}) %tuple.108, (pred[1,2]{1,0:T(4,128)(4,1)S(1)}, ...), branch_computations={%region_3.2_spmd, %region_4.5_spmd} | conditional | flops 136841216 | bytes 4777246 | solution.py:51
  138.2 3.9 %conditional.3 = (f32[1,2,512]{2,1,0:T(2,128)}, f32[1,2,512]{2,1,0:T(2,128)S(1)}, f32[1,2,512,128]{3,2,1,0:T(8,128)S(1)}) conditional(s32[]{:T(128)} %convert_element_type.56, (f32[2,512]{1,0:T(2,128)}, f32[2,512]{1,0:T(2,128)S(1)}, f32[2,512,128]{2,1,0:T(8,128)S(1)}) %tuple.108, (pred[1,2]{1,0:T(4,128)(4,1)S(1)}, ...), branch_computations={%region_3.2_spmd, %region_4.5_spmd} | conditional | flops 136841216 | bytes 4777246 | solution.py:51
  146.9 18.4 %while.42 = (s32[]{:T(128)}, f32[2,2,512]{2,1,0:T(2,128)S(1)}, f32[2,2,512]{2,1,0:T(2,128)S(1)}, f32[2,2,512,128]{3,2,1,0:T(8,128)}, pred[2,2]{1,0:T(4,128)(4,1)...) while((s32[]{:T(128)}, f32[2,2,512]{2,1,0:T(2,128)S(1)}, ...), condition=%wide.region_7.7_spmd.clone, body=%wide.region_1.6_spmd.clone.sunk | while | flops 136841216 | bytes 6916081 | solution.py:60
  150.7 3.9 %conditional.3 = (f32[1,2,512]{2,1,0:T(2,128)}, f32[1,2,512]{2,1,0:T(2,128)S(1)}, f32[1,2,512,128]{3,2,1,0:T(8,128)S(1)}) conditional(s32[]{:T(128)} %convert_element_type.56, (f32[2,512]{1,0:T(2,128)}, f32[2,512]{1,0:T(2,128)S(1)}, f32[2,512,128]{2,1,0:T(8,128)S(1)}) %tuple.108, (pred[1,2]{1,0:T(4,128)(4,1)S(1)}, ...), branch_computations={%region_3.2_spmd, %region_4.5_spmd} | conditional | flops 136841216 | bytes 4777246 | solution.py:51
  159.9 3.9 %conditional.3 = (f32[1,2,512]{2,1,0:T(2,128)}, f32[1,2,512]{2,1,0:T(2,128)S(1)}, f32[1,2,512,128]{3,2,1,0:T(8,128)S(1)}) conditional(s32[]{:T(128)} %convert_element_type.56, (f32[2,512]{1,0:T(2,128)}, f32[2,512]{1,0:T(2,128)S(1)}, f32[2,512,128]{2,1,0:T(8,128)S(1)}) %tuple.108, (pred[1,2]{1,0:T(4,128)(4,1)S(1)}, ...), branch_computations={%region_3.2_spmd, %region_4.5_spmd} | conditional | flops 136841216 | bytes 4777246 | solution.py:51
  168.6 18.4 %while.42 = (s32[]{:T(128)}, f32[2,2,512]{2,1,0:T(2,128)S(1)}, f32[2,2,512]{2,1,0:T(2,128)S(1)}, f32[2,2,512,128]{3,2,1,0:T(8,128)}, pred[2,2]{1,0:T(4,128)(4,1)...) while((s32[]{:T(128)}, f32[2,2,512]{2,1,0:T(2,128)S(1)}, ...), condition=%wide.region_7.7_spmd.clone, body=%wide.region_1.6_spmd.clone.sunk | while | flops 136841216 | bytes 6916081 | solution.py:60
  172.4 3.9 %conditional.3 = (f32[1,2,512]{2,1,0:T(2,128)}, f32[1,2,512]{2,1,0:T(2,128)S(1)}, f32[1,2,512,128]{3,2,1,0:T(8,128)S(1)}) conditional(s32[]{:T(128)} %convert_element_type.56, (f32[2,512]{1,0:T(2,128)}, f32[2,512]{1,0:T(2,128)S(1)}, f32[2,512,128]{2,1,0:T(8,128)S(1)}) %tuple.108, (pred[1,2]{1,0:T(4,128)(4,1)S(1)}, ...), branch_computations={%region_3.2_spmd, %region_4.5_spmd} | conditional | flops 136841216 | bytes 4777246 | solution.py:51
  181.6 3.9 %conditional.3 = (f32[1,2,512]{2,1,0:T(2,128)}, f32[1,2,512]{2,1,0:T(2,128)S(1)}, f32[1,2,512,128]{3,2,1,0:T(8,128)S(1)}) conditional(s32[]{:T(128)} %convert_element_type.56, (f32[2,512]{1,0:T(2,128)}, f32[2,512]{1,0:T(2,128)S(1)}, f32[2,512,128]{2,1,0:T(8,128)S(1)}) %tuple.108, (pred[1,2]{1,0:T(4,128)(4,1)S(1)}, ...), branch_computations={%region_3.2_spmd, %region_4.5_spmd} | conditional | flops 136841216 | bytes 4777246 | solution.py:51
  190.4 14.6 %while.42 = (s32[]{:T(128)}, f32[2,2,512]{2,1,0:T(2,128)S(1)}, f32[2,2,512]{2,1,0:T(2,128)S(1)}, f32[2,2,512,128]{3,2,1,0:T(8,128)}, pred[2,2]{1,0:T(4,128)(4,1)...) while((s32[]{:T(128)}, f32[2,2,512]{2,1,0:T(2,128)S(1)}, ...), condition=%wide.region_7.7_spmd.clone, body=%wide.region_1.6_spmd.clone.sunk | while | flops 136841216 | bytes 6916081 | solution.py:60
  194.2 3.9 %conditional.3 = (f32[1,2,512]{2,1,0:T(2,128)}, f32[1,2,512]{2,1,0:T(2,128)S(1)}, f32[1,2,512,128]{3,2,1,0:T(8,128)S(1)}) conditional(s32[]{:T(128)} %convert_element_type.56, (f32[2,512]{1,0:T(2,128)}, f32[2,512]{1,0:T(2,128)S(1)}, f32[2,512,128]{2,1,0:T(8,128)S(1)}) %tuple.108, (pred[1,2]{1,0:T(4,128)(4,1)S(1)}, ...), branch_computations={%region_3.2_spmd, %region_4.5_spmd} | conditional | flops 136841216 | bytes 4777246 | solution.py:51
  208.2 18.4 %while.42 = (s32[]{:T(128)}, f32[2,2,512]{2,1,0:T(2,128)S(1)}, f32[2,2,512]{2,1,0:T(2,128)S(1)}, f32[2,2,512,128]{3,2,1,0:T(8,128)}, pred[2,2]{1,0:T(4,128)(4,1)...) while((s32[]{:T(128)}, f32[2,2,512]{2,1,0:T(2,128)S(1)}, ...), condition=%wide.region_7.7_spmd.clone, body=%wide.region_1.6_spmd.clone.sunk | while | flops 136841216 | bytes 6916081 | solution.py:60
  212.0 3.9 %conditional.3 = (f32[1,2,512]{2,1,0:T(2,128)}, f32[1,2,512]{2,1,0:T(2,128)S(1)}, f32[1,2,512,128]{3,2,1,0:T(8,128)S(1)}) conditional(s32[]{:T(128)} %convert_element_type.56, (f32[2,512]{1,0:T(2,128)}, f32[2,512]{1,0:T(2,128)S(1)}, f32[2,512,128]{2,1,0:T(8,128)S(1)}) %tuple.108, (pred[1,2]{1,0:T(4,128)(4,1)S(1)}, ...), branch_computations={%region_3.2_spmd, %region_4.5_spmd} | conditional | flops 136841216 | bytes 4777246 | solution.py:51
  221.2 3.9 %conditional.3 = (f32[1,2,512]{2,1,0:T(2,128)}, f32[1,2,512]{2,1,0:T(2,128)S(1)}, f32[1,2,512,128]{3,2,1,0:T(8,128)S(1)}) conditional(s32[]{:T(128)} %convert_element_type.56, (f32[2,512]{1,0:T(2,128)}, f32[2,512]{1,0:T(2,128)S(1)}, f32[2,512,128]{2,1,0:T(8,128)S(1)}) %tuple.108, (pred[1,2]{1,0:T(4,128)(4,1)S(1)}, ...), branch_computations={%region_3.2_spmd, %region_4.5_spmd} | conditional | flops 136841216 | bytes 4777246 | solution.py:51
  229.9 14.6 %while.42 = (s32[]{:T(128)}, f32[2,2,512]{2,1,0:T(2,128)S(1)}, f32[2,2,512]{2,1,0:T(2,128)S(1)}, f32[2,2,512,128]{3,2,1,0:T(8,128)}, pred[2,2]{1,0:T(4,128)(4,1)...) while((s32[]{:T(128)}, f32[2,2,512]{2,1,0:T(2,128)S(1)}, ...), condition=%wide.region_7.7_spmd.clone, body=%wide.region_1.6_spmd.clone.sunk | while | flops 136841216 | bytes 6916081 | solution.py:60
  233.7 3.9 %conditional.3 = (f32[1,2,512]{2,1,0:T(2,128)}, f32[1,2,512]{2,1,0:T(2,128)S(1)}, f32[1,2,512,128]{3,2,1,0:T(8,128)S(1)}) conditional(s32[]{:T(128)} %convert_element_type.56, (f32[2,512]{1,0:T(2,128)}, f32[2,512]{1,0:T(2,128)S(1)}, f32[2,512,128]{2,1,0:T(8,128)S(1)}) %tuple.108, (pred[1,2]{1,0:T(4,128)(4,1)S(1)}, ...), branch_computations={%region_3.2_spmd, %region_4.5_spmd} | conditional | flops 136841216 | bytes 4777246 | solution.py:51
  247.8 14.6 %while.42 = (s32[]{:T(128)}, f32[2,2,512]{2,1,0:T(2,128)S(1)}, f32[2,2,512]{2,1,0:T(2,128)S(1)}, f32[2,2,512,128]{3,2,1,0:T(8,128)}, pred[2,2]{1,0:T(4,128)(4,1)...) while((s32[]{:T(128)}, f32[2,2,512]{2,1,0:T(2,128)S(1)}, ...), condition=%wide.region_7.7_spmd.clone, body=%wide.region_1.6_spmd.clone.sunk | while | flops 136841216 | bytes 6916081 | solution.py:60
  251.6 3.9 %conditional.3 = (f32[1,2,512]{2,1,0:T(2,128)}, f32[1,2,512]{2,1,0:T(2,128)S(1)}, f32[1,2,512,128]{3,2,1,0:T(8,128)S(1)}) conditional(s32[]{:T(128)} %convert_element_type.56, (f32[2,512]{1,0:T(2,128)}, f32[2,512]{1,0:T(2,128)S(1)}, f32[2,512,128]{2,1,0:T(8,128)S(1)}) %tuple.108, (pred[1,2]{1,0:T(4,128)(4,1)S(1)}, ...), branch_computations={%region_3.2_spmd, %region_4.5_spmd} | conditional | flops 136841216 | bytes 4777246 | solution.py:51
  264.7 7.1 %convolution_convert_fusion = bf16[256,4096]{1,0:T(8,128)(2,1)} fusion(bf16[256,1024]{1,0:T(8,128)(2,1)S(1)} %convert_element_type.47, bf16[1024,4096]{1,0:T(8,128)(2,1)} %param.17), kind=kOutput, calls=%fused_computation.28 | convolution fusion | flops 2148532224 | bytes 11010048 | tf_op jit(solution)/shard_map/dot_general | solution.py:130
  271.8 33.5 %reduce-scatter.2.cloned.1.call-done = bf16[64,4096]{1,0:T(8,128)(2,1)} async-done(((bf16[256,4096]{1,0:T(8,128)(2,1)}), bf16[64,4096]{1,0:T(8,128)(2,1)}) %reduce-scatter.2.cloned.1.call-update) | async-done | bytes 524304 | tf_op jit(solution)/shard_map/reduce_scatter | solution.py:131
  (258 shorter events, 154.4 us)
Async XLA Ops:
  6.5 40.7 %copy-start = (bf16[4096,256]{1,0:T(8,128)(2,1)S(1)}, bf16[4096,256]{1,0:T(8,128)(2,1)}, u32[]{:S(2)}) copy-start(bf16[4096,256]{1,0:T(8,128)(2,1)} %param.15) | copy-start | bytes 6291460
  6.5 40.7 %all-gather.4.cloned.1.call-start = ((), (), s32[]{:S(2)}) async-start(), calls=%async_computation.1 | async-start | bytes 2621440 | tf_op jit(solution)/shard_map/all_gather | solution.py:73
  7.3 67.4 %all-gather.6.cloned.1.call-start = ((), (), s32[]{:S(2)}) async-start(), calls=%async_computation.2 | async-start | bytes 1179648 | tf_op jit(solution)/shard_map/all_gather | solution.py:103
  50.5 3.9 %copy-start.1 = (s32[2,16]{1,0:T(2,128)S(1)}, s32[2,16]{1,0:T(2,128)}, u32[]{:S(2)}) copy-start(s32[2,16]{1,0:T(2,128)} %param.18) | copy-start | bytes 388
  50.5 46.5 %all-gather.8.cloned.1.call-start = ((), (), s32[]{:S(2)}) async-start(), calls=%async_computation.3 | async-start | bytes 1179648 | tf_op jit(solution)/shard_map/all_gather | solution.py:104
  54.2 251.1 %reduce-scatter.2.cloned.1.call-start = ((), (), s32[]{:S(2)}) async-start(), calls=%async_computation.4 | async-start | bytes 2621440 | tf_op jit(solution)/shard_map/reduce_scatter | solution.py:131
Sparse Core Ops, SparseCore 0:
  9.2 38.0 all-gather.3
  50.6 23.9 all-gather.5
  76.2 20.7 all-gather.7
  271.9 33.3 reduce-scatter.1
where the time goes:
time: 316 us; the launch traced here: 312 us
  waiting for transfers between devices  103 us (33%)
  local copies, waits for them, and re-layouts  94 us (30%)
  other arithmetic  44.2 us (14%)
  matrix products  40.1 us (13%)
  loops' own time  17.2 us (5%)
  between operations  13.2 us (4%)
    all_gather x1, waiting for transfers between devices, body(): piece = lax.all_gather(tokens, 'grp', axis=0, tiled=True)  38.9 us
    reduce_scatter x1, waiting for transfers between devices, body(): lax.psum_scatter(lax.optimization_barrier(term.astype(jnp.bfloat16)).asty...  33.5 us
    squeeze x32, local copies, waits for them, and re-layouts, fold_tiles(): lax.scan(over_query, 0, (query_tiles, fold_state[0], fold_state[1], fold_...  26.8 us
    dynamic_update_slice x48, local copies, waits for them, and re-layouts, fold_tiles(): lax.scan(over_query, 0, (query_tiles, fold_state[0], fold_state[1], fold_...  24.8 us
    all_gather x1, waiting for transfers between devices, body(): value_piece = lax.all_gather(value_rows, 'blk', axis=0, tiled=True)  17.2 us
    dot_general x13, matrix products, attend(): jnp.einsum('crg,gcd->crd', weights.astype(jnp.bfloat16), value_tile, pref...  16.4 us
    dynamic_slice x16, local copies, waits for them, and re-layouts, body(): lax.scan(over_group, initial, (key_groups, value_groups, jnp.arange(group...  12.6 us
    all_gather x1, waiting for transfers between devices, body(): key_piece = lax.all_gather(key_rows, 'blk', axis=0, tiled=True)  12.6 us
  transfers between devices with their start and end apart: 4, of which 4 were waited for; matrix products, arithmetic and copies ran while one was open for 6% of the time, Pallas kernels for 0%

commit v1 on v0

v1 whole, which is shorter than its diff:
```python
import functools
import math

import jax
import jax.numpy as jnp
from jax import lax
from jax.experimental import pallas as pl
from jax.experimental.pallas import tpu as pltpu
from jax.sharding import PartitionSpec as P

HEAD_WIDTH = 128
MASK_BLOCK_TOKENS = 128
ROPE_BASE = 500000.0
NEG_FILL = -1e30
WIDE = 8
QUERY_FACTOR = HEAD_WIDTH**-0.5 * math.log2(math.e)
VMEM = pl.BlockSpec(memory_space=pltpu.VMEM)
SMEM = pl.BlockSpec(memory_space=pltpu.SMEM)
MIB = 1 << 20


def params(mib):
    return pltpu.CompilerParams(vmem_limit_bytes=mib * MIB)


def turn(product, cosine, sine):
    return product * cosine + pltpu.roll(product, HEAD_WIDTH // 2, 1) * sine


def key_value_kernel(tokens_ref, key_ref, value_ref, cos_ref, sin_ref, out_ref):
    width = key_ref.shape[1]
    rows = tokens_ref[...]
    keys = jnp.dot(rows, key_ref[...], preferred_element_type=jnp.float32)
    values = jnp.dot(rows, value_ref[...], preferred_element_type=jnp.float32)
    cosine, sine = cos_ref[...], sin_ref[...]
    for at in range(0, width, HEAD_WIDTH):
        head = slice(at, at + HEAD_WIDTH)
        out_ref[:, head] = turn(keys[:, head], cosine, sine).astype(out_ref.dtype)
    out_ref[:, width:] = values.astype(out_ref.dtype)


def key_value_rows(rows, key_weight, value_weight, cosine, sine):
    width = key_weight.shape[1] + value_weight.shape[1]
    return pl.pallas_call(
        key_value_kernel,
        out_shape=jax.ShapeDtypeStruct((rows.shape[0], width), jnp.bfloat16),
        in_specs=[VMEM] * 5,
        out_specs=VMEM,
        compiler_params=params(24),
        cost_estimate=pl.CostEstimate(
            flops=2 * rows.shape[0] * rows.shape[1] * width,
            bytes_accessed=2 * (rows.size + key_weight.size + value_weight.size),
            transcendentals=0,
        ),
        name="key_value_rows",
    )(rows, key_weight, value_weight, cosine, sine)


def query_kernel(*refs):
    count = len(refs) - 4
    pieces, (weight_ref, cos_ref, sin_ref, out_ref) = refs[:count], refs[count:]
    step = 2 * HEAD_WIDTH
    rows = jnp.concatenate([piece[...] for piece in pieces], axis=0)

    @pl.loop(0, weight_ref.shape[1] // step)
    def _(tile):
        at = pl.multiple_of(tile * step, step)
        product = jnp.dot(rows, weight_ref[:, pl.ds(at, step)], preferred_element_type=jnp.float32)
        cosine, sine = cos_ref[...] * QUERY_FACTOR, sin_ref[...] * QUERY_FACTOR
        for half in range(2):
            head = turn(product[:, half * HEAD_WIDTH : (half + 1) * HEAD_WIDTH], cosine, sine)
            out_ref[:, pl.ds(at + half * HEAD_WIDTH, HEAD_WIDTH)] = head.astype(out_ref.dtype)


def query_rows(pieces, weight, cosine, sine):
    rows = sum(piece.shape[0] for piece in pieces)
    return pl.pallas_call(
        query_kernel,
        out_shape=jax.ShapeDtypeStruct((rows, weight.shape[1]), jnp.bfloat16),
        in_specs=[VMEM] * (len(pieces) + 3),
        out_specs=VMEM,
        compiler_params=params(32),
        cost_estimate=pl.CostEstimate(
            flops=2 * rows * weight.size, bytes_accessed=2 * weight.size, transcendentals=0
        ),
        name="query_rows",
    )(*pieces, weight, cosine, sine)


def attend_kernel(relatives, blk_count, groups, placed, place_ref, mask_ref, query_ref, kv_ref, weight_ref, *rest):
    out_refs, (live_ref, mixed_ref) = rest[: 2 * len(relatives)], rest[2 * len(relatives) :]
    grp, chip, core = place_ref[0], place_ref[1], place_ref[2]
    piece_rows = query_ref.shape[0] // groups
    own_blocks = mask_ref.shape[0]
    chips = blk_count // 2
    kv_heads = kv_ref.shape[1] // (2 * HEAD_WIDTH)
    repeat = query_ref.shape[1] // (kv_heads * HEAD_WIDTH)
    block = MASK_BLOCK_TOKENS
    turned = (grp * own_blocks) // groups

    for at, relative in enumerate(relatives):
        query_piece = lax.bitwise_xor(grp, relative) if placed else relative
        query_block = query_piece * piece_rows // block

        def note(index, count, query_block=query_block):
            key_block = index
            if placed:
                owner_at, inner = index // own_blocks, index % own_blocks
                shift, other = owner_at // 2, owner_at % 2
                owner = lax.rem(chip - shift + chips, chips) * 2 + lax.bitwise_xor(core, other)
                key_block = owner * own_blocks + lax.bitwise_xor(inner, turned)
            live = mask_ref[query_block, key_block]
            live_ref[count] = index
            return count + live

        count = lax.fori_loop(0, blk_count * own_blocks, note, jnp.int32(0))
        for spare in range(WIDE):
            live_ref[count + spare] = 0

        for head in range(kv_heads):
            query = jnp.concatenate(
                [
                    query_ref[
                        relative * piece_rows : (relative + 1) * piece_rows,
                        (head * repeat + q) * HEAD_WIDTH : (head * repeat + q + 1) * HEAD_WIDTH,
                    ]
                    for q in range(repeat)
                ],
                axis=0,
            )

            def step(index, state, head=head, query=query, count=count):
                top_old, total_old, mix_old = state
                first = index * WIDE
                starts = [
                    pl.multiple_of(live_ref[first + wide] * block, block) for wide in range(WIDE)
                ]
                key_cols = pl.ds(head * HEAD_WIDTH, HEAD_WIDTH)
                value_cols = pl.ds((kv_heads + head) * HEAD_WIDTH, HEAD_WIDTH)
                scores = []
                for wide, start in enumerate(starts):
                    tile = lax.dot_general(
                        query,
                        kv_ref[pl.ds(start, block), key_cols],
                        (((1,), (1,)), ((), ())),
                        preferred_element_type=jnp.float32,
                    )
                    if wide:
                        tile = tile + jnp.where(first + wide < count, 0.0, NEG_FILL)
                    scores.append(tile)
                scores = jnp.concatenate(scores, axis=1)
                top = jnp.maximum(top_old, jnp.max(scores, axis=1, keepdims=True))
                weights = jnp.exp2(scores - top)
                factor = jnp.exp2(top_old - top)
                total = total_old * factor + jnp.sum(weights, axis=1, keepdims=True)
                values = jnp.concatenate(
                    [kv_ref[pl.ds(start, block), value_cols] for start in starts], axis=0
                )
                product = jnp.dot(
                    weights.astype(jnp.bfloat16), values, preferred_element_type=jnp.float32
                )
                return top, total, mix_old * factor + product

            rows = repeat * piece_rows
            _, total, mix = lax.fori_loop(
                0,
                (count + WIDE - 1) // WIDE,
                step,
                (
                    jnp.full((rows, 1), NEG_FILL, jnp.float32),
                    jnp.zeros((rows, 1), jnp.float32),
                    jnp.zeros((rows, HEAD_WIDTH), jnp.float32),
                ),
            )
            mixed = (mix / total).astype(jnp.bfloat16)
            for q in range(repeat):
                mixed_ref[
                    at * piece_rows : (at + 1) * piece_rows,
                    (head * repeat + q) * HEAD_WIDTH : (head * repeat + q + 1) * HEAD_WIDTH,
                ] = mixed[q * piece_rows : (q + 1) * piece_rows]

    tile_cols = 512
    for side in range(2):
        side_cols = out_refs[side].shape[1]

        @pl.loop(0, side_cols // tile_cols)
        def _(tile, side=side, side_cols=side_cols):
            here = pl.multiple_of(tile * tile_cols, tile_cols)
            term = jnp.dot(
                mixed_ref[...],
                weight_ref[:, pl.ds(side * side_cols + here, tile_cols)],
                preferred_element_type=jnp.float32,
            ).astype(jnp.bfloat16)
            for at in range(len(relatives)):
                out_refs[2 * at + side][:, pl.ds(here, tile_cols)] = term[
                    at * piece_rows : (at + 1) * piece_rows
                ]


def attend(relatives, blk_count, groups, placed, place, mask, query, kv, weight):
    piece_rows = query.shape[0] // groups
    side = jax.ShapeDtypeStruct((piece_rows, weight.shape[1] // 2), jnp.bfloat16)
    return pl.pallas_call(
        functools.partial(attend_kernel, relatives, blk_count, groups, placed),
        out_shape=[side] * (2 * len(relatives)),
        in_specs=[SMEM, SMEM, VMEM, VMEM, VMEM],
        out_specs=[VMEM] * (2 * len(relatives)),
        scratch_shapes=[
            pltpu.SMEM((mask.shape[1] + 2 * WIDE,), jnp.int32),
            pltpu.VMEM((len(relatives) * piece_rows, weight.shape[0]), jnp.bfloat16),
        ],
        compiler_params=params(48),
        cost_estimate=pl.CostEstimate(
            flops=2 * len(relatives) * piece_rows * weight.size * 2,
            bytes_accessed=2 * weight.size,
            transcendentals=0,
        ),
        name="attend_project",
    )(place, mask, query, kv, weight)


def rotary_tables(rows):
    inverse = jnp.power(
        jnp.float32(ROPE_BASE),
        -(2.0 * jnp.arange(HEAD_WIDTH // 2, dtype=jnp.float32)) / HEAD_WIDTH,
    )
    angles = rows.astype(jnp.float32)[:, None] * inverse[None, :]
    cosine, sine = jnp.cos(angles), jnp.sin(angles)
    return jnp.concatenate([cosine, cosine], axis=1), jnp.concatenate([-sine, sine], axis=1)


def add(*values):
    total = values[0].astype(jnp.float32)
    for value in values[1:]:
        total = total + value.astype(jnp.float32)
    return total.astype(jnp.bfloat16)


def general_body(
    blk_count, groups, tokens, w_query, key_weight, value_weight, w_output, block_mask, positions
):
    rows = lax.all_gather(tokens, "grp", axis=0, tiled=True)
    cosine, sine = rotary_tables(positions)
    own = key_value_rows(rows, key_weight, value_weight, cosine, sine)
    kv = lax.all_gather(own, "blk", axis=0, tiled=True)
    query = query_rows((rows,), w_query, cosine, sine)
    place = jnp.zeros((3,), jnp.int32)
    order = tuple(range(groups))
    sides = attend(order, blk_count, groups, False, place, block_mask, query, kv, w_output)
    term = jnp.concatenate(
        [jnp.concatenate(sides[side::2], axis=0) for side in range(2)], axis=1
    )
    return lax.psum_scatter(term, "grp", scatter_dimension=0, tiled=True)


def square_body(
    blk_count, tokens, w_query, key_weight, value_weight, w_output, block_mask, positions
):
    grp, blk = lax.axis_index("grp"), lax.axis_index("blk")
    along_x = [(g, g ^ 1) for g in range(4)]
    along_y = [(g, g ^ 2) for g in range(4)]
    cores = [(b, b ^ 1) for b in range(blk_count)]
    chips = blk_count // 2
    piece_rows = tokens.shape[0]
    half = piece_rows // 2

    def send_x(value):
        return lax.ppermute(value, "grp", along_x)

    def send_y(value):
        return lax.ppermute(value, "grp", along_y)

    from_x, from_y = send_x(tokens), send_y(tokens)
    across = jnp.concatenate([send_y(from_x[:half]), send_x(from_y[half:])], axis=0)

    rows = positions.reshape(2, 2, piece_rows)
    rows = jnp.where(grp % 2 == 1, rows[:, ::-1], rows)
    rows = jnp.where(grp // 2 == 1, rows[::-1], rows).reshape(4 * piece_rows)
    cosine, sine = rotary_tables(rows)

    pieces = (tokens, from_x, from_y, across)
    received = []
    for relative, piece in enumerate(pieces):
        here = slice(relative * piece_rows, (relative + 1) * piece_rows)
        own = key_value_rows(piece, key_weight, value_weight, cosine[here], sine[here])
        shifted = [own] + [
            lax.ppermute(own, "blk", [(b, (b + 2 * s) % blk_count) for b in range(blk_count)])
            for s in range(1, chips)
        ]
        shifted = jnp.stack(shifted)
        received.append(jnp.stack([shifted, lax.ppermute(shifted, "blk", cores)], axis=1))
    width = received[0].shape[-1]
    kv = jnp.stack(received, axis=2).reshape(blk_count * 4 * piece_rows, width)
    query = query_rows(pieces, w_query, cosine, sine)
    place = jnp.stack([grp, blk // 2, blk % 2]).astype(jnp.int32)

    def terms(relatives):
        return attend(relatives, blk_count, 4, True, place, block_mask, query, kv, w_output)

    across_a, across_b = terms((3,))
    second_a, second_b = send_x(across_a), send_y(across_b)
    x_a, x_b, y_a, y_b = terms((1, 2))
    from_x_a, from_y_b = send_x(x_a), send_y(y_b)
    from_y_a = send_y(add(y_a, second_a))
    from_x_b = send_x(add(x_b, second_b))
    own_a, own_b = terms((0,))
    return jnp.concatenate(
        [add(own_a, from_x_a, from_y_a), add(own_b, from_y_b, from_x_b)], axis=1
    )


def solution(mesh):
    groups, blk_count = mesh.shape["grp"], mesh.shape["blk"]
    if groups == 4:
        body = functools.partial(square_body, blk_count)
    else:
        body = functools.partial(general_body, blk_count, groups)
    return jax.shard_map(
        body,
        mesh=mesh,
        in_specs=(
            P(("blk", "grp"), None),
            P(None, "grp"),
            P(None, "grp"),
            P(None, "grp"),
            P("grp", None),
            P("blk", None),
            P("blk"),
        ),
        out_specs=P(("blk", "grp"), None),
        check_vma=False,
    )
```

time: 316 us -> 101 us (0.32); the launches traced: 312 us -> 101 us
  local copies, waits for them, and re-layouts: 94 us -> 8 us
  waiting for transfers between devices: 103 us -> 23.2 us
  matrix products: 40.1 us -> 0 us
  other arithmetic: 44.2 us -> 5.79 us
  Pallas kernels: 0 us -> 36.1 us
  starting transfers between devices: 0.12 us -> 27.3 us
  loops' own time: 17.2 us -> 0 us
  between operations: 13.2 us -> 0.37 us
    all_gather x3 -> x0, waiting for transfers between devices: 68.7 us -> none  [the longest x1 38.9 us: body(): piece = lax.all_gather(tokens, 'grp', axis=0, tiled=True)]
    dot_general x30 -> x0, matrix products: 40.1 us -> none  [the longest x13 16.4 us: attend(): jnp.einsum('crg,gcd->crd', weights.astype(jnp.bfloat16), value_tile, pref...]
    pallas_call x0 -> x8, Pallas kernels: none -> 36.1 us  [the longest x3 28.9 us: attend(): pl.pallas_call(functools.partial(attend_kernel, relatives, blk_count, gro...]
    squeeze x40 -> x0, local copies, waits for them, and re-layouts: 34.3 us -> none  [the longest x32 26.8 us: fold_tiles(): lax.scan(over_query, 0, (query_tiles, fold_state[0], fold_state[1], fold_...]
    reduce_scatter x1 -> x0, waiting for transfers between devices: 33.5 us -> none  [body(): lax.psum_scatter(lax.optimization_barrier(term.astype(jnp.bfloat16)).asty...]
    ppermute x0 -> x26, starting transfers between devices: none -> 27.3 us  [the longest x12 16.1 us: square_body(): lax.ppermute(own, 'blk', [(b, (b + 2 * s) % blk_count) for b in range(blk...]
    dynamic_update_slice x48 -> x0, local copies, waits for them, and re-layouts: 24.8 us -> none  [fold_tiles(): lax.scan(over_query, 0, (query_tiles, fold_state[0], fold_state[1], fold_...]
    ppermute x0 -> x26, waiting for transfers between devices: none -> 23.2 us  [the longest x5 11.2 us: send_x(): return lax.ppermute(value, 'grp', along_x)]
  transfers between devices with their start and end apart: 4 -> 26, of which waited for: 4 -> 10; matrix products, arithmetic and copies ran while one was open for 6% -> 5% of each run, Pallas kernels for 0% -> 28%
where the time goes in v1:
time: 101 us
  Pallas kernels  36.1 us (36%)
  starting transfers between devices  27.3 us (27%)
  waiting for transfers between devices  23.2 us (23%)
  local copies, waits for them, and re-layouts  8 us (8%)
  other arithmetic  5.79 us (6%)
    pallas_call x3, Pallas kernels, attend(): pl.pallas_call(functools.partial(attend_kernel, relatives, blk_count, gro...  28.9 us
    ppermute x12, starting transfers between devices, square_body(): lax.ppermute(own, 'blk', [(b, (b + 2 * s) % blk_count) for b in range(blk...  16.1 us
    ppermute x5, waiting for transfers between devices, send_x(): return lax.ppermute(value, 'grp', along_x)  11.2 us
    ppermute x12, waiting for transfers between devices, square_body(): lax.ppermute(own, 'blk', [(b, (b + 2 * s) % blk_count) for b in range(blk...  10.4 us
    unnamed x25, local copies, waits for them, and re-layouts  6.94 us
    ppermute x5, starting transfers between devices, send_x(): return lax.ppermute(value, 'grp', along_x)  6.16 us
    ppermute x5, starting transfers between devices, send_y(): return lax.ppermute(value, 'grp', along_y)  4.89 us
    pallas_call x4, Pallas kernels, key_value_rows(): pl.pallas_call(key_value_kernel, out_shape=jax.ShapeDtypeStruct((rows.sha...  3.67 us
  transfers between devices with their start and end apart: 26, of which 10 were waited for; matrix products, arithmetic and copies ran while one was open for 5% of the time, Pallas kernels for 28%

profile of v1, /device:TPU:0, one launch (start us, length us, event | category | flops | bytes accessed | tf_op | source)
XLA Modules:
  0.0 100.7 jit_solution(3079987034504404034)
XLA Ops:
  0.0 2.9 %collective-permute-start = (bf16[64,4096]{1,0:T(8,128)(2,1)}, bf16[64,4096]{1,0:T(8,128)(2,1)S(1)}, u32[]{:S(2)}, u32[]{:S(2)}) collective-permute-start(bf16[64,4096]{1,0:T(8,128)(2,1)} %tokens_ref.1), channel_id=1, source_target_pairs={{0,8},{8,0},{16,24},{24,16},{1,9},{9,1},{17,25},{25,17},{2,10},{10... | collective-permute-start | bytes 1572872 | tf_op jit(solution)/shard_map/ppermute | solution.py:268
  2.9 1.5 %collective-permute-start.1 = (bf16[64,4096]{1,0:T(8,128)(2,1)}, bf16[64,4096]{1,0:T(8,128)(2,1)S(1)}, u32[]{:S(2)}, u32[]{:S(2)}) collective-permute-start(bf16[64,4096]{1,0:T(8,128)(2,1)} %tokens_ref.1), channel_id=1, source_target_pairs={{0,16},{8,24},{16,0},{24,8},{1,17},{9,25},{17,1},{25,9},{2,18},{10... | collective-permute-start | bytes 1572872 | tf_op jit(solution)/shard_map/ppermute | solution.py:271
  6.7 1.6 %copy-done = bf16[4096,256]{1,0:T(8,128)(2,1)S(1)} copy-done((bf16[4096,256]{1,0:T(8,128)(2,1)S(1)}, bf16[4096,256]{1,0:T(8,128)(2,1)}, u32[]{:S(2)}) %copy-start) | copy-done | bytes 2097176
  8.2 1.6 %copy-done.2 = bf16[4096,256]{1,0:T(8,128)(2,1)S(1)} copy-done((bf16[4096,256]{1,0:T(8,128)(2,1)S(1)}, bf16[4096,256]{1,0:T(8,128)(2,1)}, u32[]{:S(2)}) %copy-start.2) | copy-done | bytes 2097176
  9.8 1.0 %copy-done.4 = bf16[64,4096]{1,0:T(8,128)(2,1)S(1)} copy-done((bf16[64,4096]{1,0:T(8,128)(2,1)S(1)}, bf16[64,4096]{1,0:T(8,128)(2,1)}, u32[]{:S(2)}) %copy-start.4) | copy-done | bytes 524312
  11.8 3.7 %collective-permute-start.6 = (bf16[64,512]{1,0:T(8,128)(2,1)S(1)}, bf16[64,512]{1,0:T(8,128)(2,1)S(1)}, u32[]{:S(2)}, u32[]{:S(2)}) collective-permute-start(bf16[64,512]{1,0:T(8,128)(2,1)S(1)} %key_value_rows.4), channel_id=1, source_target_pairs={{0,6},{1,7},{2,0},{3,1},{4,2},{5,3},{6,4},{7,5},{8,14},{9,15},{10,... | collective-permute-start | bytes 196616 | tf_op jit(solution)/shard_map/ppermute | solution.py:287
  15.4 1.0 %collective-permute-start.4 = (bf16[64,512]{1,0:T(8,128)(2,1)S(1)}, bf16[64,512]{1,0:T(8,128)(2,1)S(1)}, u32[]{:S(2)}, u32[]{:S(2)}) collective-permute-start(bf16[64,512]{1,0:T(8,128)(2,1)S(1)} %key_value_rows.4), channel_id=1, source_target_pairs={{0,2},{1,3},{2,4},{3,5},{4,6},{5,7},{6,0},{7,1},{8,10},{9,11},{10,... | collective-permute-start | bytes 196616 | tf_op jit(solution)/shard_map/ppermute | solution.py:287
  16.5 1.2 %collective-permute-done.6 = bf16[64,512]{1,0:T(8,128)(2,1)S(1)} collective-permute-done((bf16[64,512]{1,0:T(8,128)(2,1)S(1)}, bf16[64,512]{1,0:T(8,128)(2,1)S(1)}, u32[]{:S(2)}, u32[]{:S(2)}) %collective-permute-start.6) | collective-permute-done | bytes 65568 | tf_op jit(solution)/shard_map/ppermute | solution.py:287
  17.6 3.1 %collective-permute-done.5 = bf16[64,512]{1,0:T(8,128)(2,1)S(1)} collective-permute-done((bf16[64,512]{1,0:T(8,128)(2,1)S(1)}, bf16[64,512]{1,0:T(8,128)(2,1)S(1)}, u32[]{:S(2)}, u32[]{:S(2)}) %collective-permute-start.5) | collective-permute-done | bytes 65568 | tf_op jit(solution)/shard_map/ppermute | solution.py:287
  22.4 1.2 %pad_maximum_fusion.6 = (f32[256,128]{1,0:T(8,128)S(1)}, f32[256,128]{1,0:T(8,128)S(1)}) fusion(f32[256,64]{1,0:T(8,128)} %copy-done.8, f32[256,64]{1,0:T(8,128)} %copy-done.7, f32[256,64]{1,0:T(8,128)S(1)} %get-tuple-element.37), kind=kLoop, calls=%fused_computation.20 | loop fusion | flops 65536 | bytes 458752 | tf_op jit(solution)/shard_map/concatenate | solution.py:229
  23.6 1.6 %copy-done.3 = bf16[4096,256]{1,0:T(8,128)(2,1)S(1)} copy-done((bf16[4096,256]{1,0:T(8,128)(2,1)S(1)}, bf16[4096,256]{1,0:T(8,128)(2,1)}, u32[]{:S(2)}) %copy-start.3) | copy-done | bytes 2097176
  25.2 0.9 key_value_rows.6
  26.1 1.8 %collective-permute-start.14 = (bf16[64,512]{1,0:T(8,128)(2,1)S(1)}, bf16[64,512]{1,0:T(8,128)(2,1)S(1)}, u32[]{:S(2)}, u32[]{:S(2)}) collective-permute-start(bf16[64,512]{1,0:T(8,128)(2,1)S(1)} %key_value_rows.6), channel_id=1, source_target_pairs={{0,6},{1,7},{2,0},{3,1},{4,2},{5,3},{6,4},{7,5},{8,14},{9,15},{10,... | collective-permute-start | bytes 196616 | tf_op jit(solution)/shard_map/ppermute | solution.py:287
  27.9 1.9 %collective-permute-start.12 = (bf16[64,512]{1,0:T(8,128)(2,1)S(1)}, bf16[64,512]{1,0:T(8,128)(2,1)S(1)}, u32[]{:S(2)}, u32[]{:S(2)}) collective-permute-start(bf16[64,512]{1,0:T(8,128)(2,1)S(1)} %key_value_rows.6), channel_id=1, source_target_pairs={{0,2},{1,3},{2,4},{3,5},{4,6},{5,7},{6,0},{7,1},{8,10},{9,11},{10,... | collective-permute-start | bytes 196616 | tf_op jit(solution)/shard_map/ppermute | solution.py:287
  30.4 1.3 %maximum_bitcast_fusion = bf16[4,2,1,64,512]{4,3,0,1,2:T(8,128)(2,1)S(1)} fusion(bf16[4,1,64,512]{3,2,0,1:T(8,128)(2,1)} %bitcast.8, bf16[4,1,64,512]{3,2,0,1:T(8,128)(2,1)S(1)} %copy-done.9), kind=kLoop, calls=%fused_computation.1 | loop fusion | flops 262144 | bytes 1048576 | tf_op jit(solution)/shard_map/stack | solution.py:293
  31.7 0.9 key_value_rows.5
  32.7 2.0 %collective-permute-start.10 = (bf16[64,512]{1,0:T(8,128)(2,1)S(1)}, bf16[64,512]{1,0:T(8,128)(2,1)S(1)}, u32[]{:S(2)}, u32[]{:S(2)}) collective-permute-start(bf16[64,512]{1,0:T(8,128)(2,1)S(1)} %key_value_rows.5), channel_id=1, source_target_pairs={{0,6},{1,7},{2,0},{3,1},{4,2},{5,3},{6,4},{7,5},{8,14},{9,15},{10,... | collective-permute-start | bytes 196616 | tf_op jit(solution)/shard_map/ppermute | solution.py:287
  34.7 1.2 %collective-permute-start.9 = (bf16[64,512]{1,0:T(8,128)(2,1)S(1)}, bf16[64,512]{1,0:T(8,128)(2,1)S(1)}, u32[]{:S(2)}, u32[]{:S(2)}) collective-permute-start(bf16[64,512]{1,0:T(8,128)(2,1)S(1)} %key_value_rows.5), channel_id=1, source_target_pairs={{0,4},{1,5},{2,6},{3,7},{4,0},{5,1},{6,2},{7,3},{8,12},{9,13},{10,... | collective-permute-start | bytes 196616 | tf_op jit(solution)/shard_map/ppermute | solution.py:287
  36.7 1.1 %collective-permute-done.2 = bf16[32,4096]{1,0:T(8,128)(2,1)S(1)} collective-permute-done((bf16[32,4096]{1,0:T(8,128)(2,1)S(1)}, bf16[32,4096]{1,0:T(8,128)(2,1)S(1)}, u32[]{:S(2)}, u32[]{:S(2)}) %collective-permute-start.2) | collective-permute-done | bytes 262176 | tf_op jit(solution)/shard_map/ppermute | solution.py:271
  37.8 5.9 %collective-permute-done.3 = bf16[32,4096]{1,0:T(8,128)(2,1)S(1)} collective-permute-done((bf16[32,4096]{1,0:T(8,128)(2,1)S(1)}, bf16[32,4096]{1,0:T(8,128)(2,1)S(1)}, u32[]{:S(2)}, u32[]{:S(2)}) %collective-permute-start.3) | collective-permute-done | bytes 262176 | tf_op jit(solution)/shard_map/ppermute | solution.py:268
  43.8 0.9 key_value_rows.7
  44.7 3.6 %collective-permute-start.18 = (bf16[64,512]{1,0:T(8,128)(2,1)S(1)}, bf16[64,512]{1,0:T(8,128)(2,1)S(1)}, u32[]{:S(2)}, u32[]{:S(2)}) collective-permute-start(bf16[64,512]{1,0:T(8,128)(2,1)S(1)} %key_value_rows.7), channel_id=1, source_target_pairs={{0,6},{1,7},{2,0},{3,1},{4,2},{5,3},{6,4},{7,5},{8,14},{9,15},{10,... | collective-permute-start | bytes 196616 | tf_op jit(solution)/shard_map/ppermute | solution.py:287
  49.1 1.1 %collective-permute-done.18 = bf16[64,512]{1,0:T(8,128)(2,1)S(1)} collective-permute-done((bf16[64,512]{1,0:T(8,128)(2,1)S(1)}, bf16[64,512]{1,0:T(8,128)(2,1)S(1)}, u32[]{:S(2)}, u32[]{:S(2)}) %collective-permute-start.18) | collective-permute-done | bytes 65568 | tf_op jit(solution)/shard_map/ppermute | solution.py:287
  50.2 3.3 %collective-permute-done.17 = bf16[64,512]{1,0:T(8,128)(2,1)S(1)} collective-permute-done((bf16[64,512]{1,0:T(8,128)(2,1)S(1)}, bf16[64,512]{1,0:T(8,128)(2,1)S(1)}, u32[]{:S(2)}, u32[]{:S(2)}) %collective-permute-start.17) | collective-permute-done | bytes 65568 | tf_op jit(solution)/shard_map/ppermute | solution.py:287
  53.5 1.0 collective-permute-done.16
  54.6 3.5 %query_rows.1.query_ref = bf16[256,1024]{1,0:T(8,128)(2,1)S(1)} custom-call(bf16[64,4096]{1,0:T(8,128)(2,1)S(1)} %copy-done.5, bf16[64,4096]{1,0:T(8,128)(2,1)S(1)} %collective-permute-done.refs_1_.tokens_ref, bf16[64,4096]{1,0:T(8,128)(2,1)S(1)} %collective-permute-done.1.refs_2_.tokens_ref, ...), custom_call_target="tpu_custom_call" | custom-call | flops 2147483648 | bytes 8388608 | tf_op jit(solution)/shard_map/query_rows/pallas_call | solution.py:77
  59.3 7.9 %attend_project.5 = (bf16[64,2048]{1,0:T(8,128)(2,1)S(1)}, bf16[64,2048]{1,0:T(8,128)(2,1)S(1)}) custom-call(s32[3]{0:T(128)S(1)} %pad_add_fusion.place_ref, s32[2,16]{1,0:T(2,128)S(1)} %copy-done.6, bf16[256,1024]{1,0:T(8,128)(2,1)S(1)} %query_rows.1.query_ref, bf16[2048,512]{1,0:T(8,128)(2,1)S(1)} %bitcast.40, bf16[1024,4096]{1,0:T(8,128)(2,1)} %weight_ref.5), custom_call_target="tpu_custom_call" | custom-call | flops 1073741824 | bytes 8388608 | tf_op jit(solution)/shard_map/attend_project/pallas_call | solution.py:203
  67.1 2.2 %collective-permute-start.24 = (bf16[64,2048]{1,0:T(8,128)(2,1)S(1)}, bf16[64,2048]{1,0:T(8,128)(2,1)S(1)}, u32[]{:S(2)}, u32[]{:S(2)}) collective-permute-start(bf16[64,2048]{1,0:T(8,128)(2,1)S(1)} %get-tuple-element.20), channel_id=1, source_target_pairs={{0,16},{8,24},{16,0},{24,8},{1,17},{9,25},{17,1},{25,9},{2,18},{10... | collective-permute-start | bytes 786440 | tf_op jit(solution)/shard_map/ppermute | solution.py:271
  69.3 11.7 %attend_project.4 = (bf16[64,2048]{1,0:T(8,128)(2,1)S(1)}, bf16[64,2048]{1,0:T(8,128)(2,1)S(1)}, bf16[64,2048]{1,0:T(8,128)(2,1)S(1)}, bf16[64,2048]{1,0:T(8,128)(2,1)S(1)}) custom-call(s32[3]{0:T(128)S(1)} %pad_add_fusion.place_ref, s32[2,16]{1,0:T(2,128)S(1)} %copy-done.6, bf16[256,1024]{1,0:T(8,128)(2,1)S(1)} %query_rows.1.query_ref, ...), custom_call_target="tpu_custom_call" | custom-call | flops 2147483648 | bytes 8388608 | tf_op jit(solution)/shard_map/attend_project/pallas_call | solution.py:203
  81.7 1.5 %collective-permute-start.20 = (bf16[64,2048]{1,0:T(8,128)(2,1)S(1)}, bf16[64,2048]{1,0:T(8,128)(2,1)S(1)}, u32[]{:S(2)}, u32[]{:S(2)}) collective-permute-start(bf16[64,2048]{1,0:T(8,128)(2,1)S(1)} %get-tuple-element.14), channel_id=1, source_target_pairs={{0,8},{8,0},{16,24},{24,16},{1,9},{9,1},{17,25},{25,17},{2,10},{10... | collective-permute-start | bytes 786440 | tf_op jit(solution)/shard_map/ppermute | solution.py:268
  83.2 9.4 %attend_project.3 = (bf16[64,2048]{1,0:T(8,128)(2,1)S(1)}, bf16[64,2048]{1,0:T(8,128)(2,1)S(1)}) custom-call(s32[3]{0:T(128)S(1)} %pad_add_fusion.place_ref, s32[2,16]{1,0:T(2,128)S(1)} %copy-done.6, bf16[256,1024]{1,0:T(8,128)(2,1)S(1)} %query_rows.1.query_ref, bf16[2048,512]{1,0:T(8,128)(2,1)S(1)} %bitcast.42, bf16[1024,4096]{1,0:T(8,128)(2,1)} %weight_ref.5), custom_call_target="tpu_custom_call" | custom-call | flops 1073741824 | bytes 8388608 | tf_op jit(solution)/shard_map/attend_project/pallas_call | solution.py:203
  93.8 5.2 %collective-permute-done.25 = bf16[64,2048]{1,0:T(8,128)(2,1)S(1)} collective-permute-done((bf16[64,2048]{1,0:T(8,128)(2,1)S(1)}, bf16[64,2048]{1,0:T(8,128)(2,1)S(1)}, u32[]{:S(2)}, u32[]{:S(2)}) %collective-permute-start.25) | collective-permute-done | bytes 262176 | tf_op jit(solution)/shard_map/ppermute | solution.py:268
  (82 shorter events, 11.8 us)
Async XLA Ops:
  0.0 29.8 %collective-permute-start = (bf16[64,4096]{1,0:T(8,128)(2,1)}, bf16[64,4096]{1,0:T(8,128)(2,1)S(1)}, u32[]{:S(2)}, u32[]{:S(2)}) collective-permute-start(bf16[64,4096]{1,0:T(8,128)(2,1)} %tokens_ref.1), channel_id=1, source_target_pairs={{0,8},{8,0},{16,24},{24,16},{1,9},{9,1},{17,25},{25,17},{2,10},{10... | collective-permute-start | bytes 1572872 | tf_op jit(solution)/shard_map/ppermute | solution.py:268
  2.9 20.7 %collective-permute-start.1 = (bf16[64,4096]{1,0:T(8,128)(2,1)}, bf16[64,4096]{1,0:T(8,128)(2,1)S(1)}, u32[]{:S(2)}, u32[]{:S(2)}) collective-permute-start(bf16[64,4096]{1,0:T(8,128)(2,1)} %tokens_ref.1), channel_id=1, source_target_pairs={{0,16},{8,24},{16,0},{24,8},{1,17},{9,25},{17,1},{25,9},{2,18},{10... | collective-permute-start | bytes 1572872 | tf_op jit(solution)/shard_map/ppermute | solution.py:271
  10.9 12.7 %copy-start.1 = (bf16[4096,256]{1,0:T(8,128)(2,1)S(1)}, bf16[4096,256]{1,0:T(8,128)(2,1)}, u32[]{:S(2)}) copy-start(bf16[4096,256]{1,0:T(8,128)(2,1)} %key_ref.7) | copy-start | bytes 6291460
  11.8 5.8 %collective-permute-start.6 = (bf16[64,512]{1,0:T(8,128)(2,1)S(1)}, bf16[64,512]{1,0:T(8,128)(2,1)S(1)}, u32[]{:S(2)}, u32[]{:S(2)}) collective-permute-start(bf16[64,512]{1,0:T(8,128)(2,1)S(1)} %key_value_rows.4), channel_id=1, source_target_pairs={{0,6},{1,7},{2,0},{3,1},{4,2},{5,3},{6,4},{7,5},{8,14},{9,15},{10,... | collective-permute-start | bytes 196616 | tf_op jit(solution)/shard_map/ppermute | solution.py:287
  15.4 5.3 %collective-permute-start.5 = (bf16[64,512]{1,0:T(8,128)(2,1)S(1)}, bf16[64,512]{1,0:T(8,128)(2,1)S(1)}, u32[]{:S(2)}, u32[]{:S(2)}) collective-permute-start(bf16[64,512]{1,0:T(8,128)(2,1)S(1)} %key_value_rows.4), channel_id=1, source_target_pairs={{0,4},{1,5},{2,6},{3,7},{4,0},{5,1},{6,2},{7,3},{8,12},{9,13},{10,... | collective-permute-start | bytes 196616 | tf_op jit(solution)/shard_map/ppermute | solution.py:287
  15.4 6.1 %collective-permute-start.4 = (bf16[64,512]{1,0:T(8,128)(2,1)S(1)}, bf16[64,512]{1,0:T(8,128)(2,1)S(1)}, u32[]{:S(2)}, u32[]{:S(2)}) collective-permute-start(bf16[64,512]{1,0:T(8,128)(2,1)S(1)} %key_value_rows.4), channel_id=1, source_target_pairs={{0,2},{1,3},{2,4},{3,5},{4,6},{5,7},{6,0},{7,1},{8,10},{9,11},{10,... | collective-permute-start | bytes 196616 | tf_op jit(solution)/shard_map/ppermute | solution.py:287
  22.3 8.1 %collective-permute-start.7 = (bf16[4,64,512]{2,1,0:T(8,128)(2,1)}, bf16[4,64,512]{2,1,0:T(8,128)(2,1)}, u32[]{:S(2)}, u32[]{:S(2)}) collective-permute-start(bf16[4,64,512]{2,1,0:T(8,128)(2,1)} %get-tuple-element.22), channel_id=1, source_target_pairs={{0,1},{1,0},{2,3},{3,2},{4,5},{5,4},{6,7},{7,6},{8,9},{9,8},{10,11... | collective-permute-start | bytes 786440 | tf_op jit(solution)/shard_map/ppermute | solution.py:291
  23.6 1.6 %copy-start.3 = (bf16[4096,256]{1,0:T(8,128)(2,1)S(1)}, bf16[4096,256]{1,0:T(8,128)(2,1)}, u32[]{:S(2)}) copy-start(bf16[4096,256]{1,0:T(8,128)(2,1)} %value_ref.7) | copy-start | bytes 6291460
  25.2 5.2 %copy-start.9 = (bf16[4,1,64,512]{3,2,0,1:T(8,128)(2,1)S(1)}, bf16[4,1,64,512]{3,2,0,1:T(8,128)(2,1)}, u32[]{:S(2)}) copy-start(bf16[4,1,64,512]{3,2,0,1:T(8,128)(2,1)} %get-tuple-element.21) | copy-start | bytes 786436
  26.1 8.5 %collective-permute-start.14 = (bf16[64,512]{1,0:T(8,128)(2,1)S(1)}, bf16[64,512]{1,0:T(8,128)(2,1)S(1)}, u32[]{:S(2)}, u32[]{:S(2)}) collective-permute-start(bf16[64,512]{1,0:T(8,128)(2,1)S(1)} %key_value_rows.6), channel_id=1, source_target_pairs={{0,6},{1,7},{2,0},{3,1},{4,2},{5,3},{6,4},{7,5},{8,14},{9,15},{10,... | collective-permute-start | bytes 196616 | tf_op jit(solution)/shard_map/ppermute | solution.py:287
  27.9 7.9 %collective-permute-start.13 = (bf16[64,512]{1,0:T(8,128)(2,1)S(1)}, bf16[64,512]{1,0:T(8,128)(2,1)S(1)}, u32[]{:S(2)}, u32[]{:S(2)}) collective-permute-start(bf16[64,512]{1,0:T(8,128)(2,1)S(1)} %key_value_rows.6), channel_id=1, source_target_pairs={{0,4},{1,5},{2,6},{3,7},{4,0},{5,1},{6,2},{7,3},{8,12},{9,13},{10,... | collective-permute-start | bytes 196616 | tf_op jit(solution)/shard_map/ppermute | solution.py:287
  27.9 8.2 %collective-permute-start.12 = (bf16[64,512]{1,0:T(8,128)(2,1)S(1)}, bf16[64,512]{1,0:T(8,128)(2,1)S(1)}, u32[]{:S(2)}, u32[]{:S(2)}) collective-permute-start(bf16[64,512]{1,0:T(8,128)(2,1)S(1)} %key_value_rows.6), channel_id=1, source_target_pairs={{0,2},{1,3},{2,4},{3,5},{4,6},{5,7},{6,0},{7,1},{8,10},{9,11},{10,... | collective-permute-start | bytes 196616 | tf_op jit(solution)/shard_map/ppermute | solution.py:287
  29.8 24.7 %slice-start = ((s8[8388608]{0:T(1024)(128)(4,1)}), s8[4194304]{0:T(1024)(128)(4,1)S(1)}, s32[]{:S(2)}) async-start(s8[8388608]{0:T(1024)(128)(4,1)} %bitcast.43), calls=%async_computation | async-start | bytes 8388608
  29.9 7.9 %collective-permute-start.2 = (bf16[32,4096]{1,0:T(8,128)(2,1)S(1)}, bf16[32,4096]{1,0:T(8,128)(2,1)S(1)}, u32[]{:S(2)}, u32[]{:S(2)}) collective-permute-start(bf16[32,4096]{1,0:T(8,128)(2,1)S(1)} %slice.40), channel_id=1, source_target_pairs={{0,16},{8,24},{16,0},{24,8},{1,17},{9,25},{17,1},{25,9},{2,18},{10... | collective-permute-start | bytes 786440 | tf_op jit(solution)/shard_map/ppermute | solution.py:271
  32.7 15.6 %collective-permute-start.10 = (bf16[64,512]{1,0:T(8,128)(2,1)S(1)}, bf16[64,512]{1,0:T(8,128)(2,1)S(1)}, u32[]{:S(2)}, u32[]{:S(2)}) collective-permute-start(bf16[64,512]{1,0:T(8,128)(2,1)S(1)} %key_value_rows.5), channel_id=1, source_target_pairs={{0,6},{1,7},{2,0},{3,1},{4,2},{5,3},{6,4},{7,5},{8,14},{9,15},{10,... | collective-permute-start | bytes 196616 | tf_op jit(solution)/shard_map/ppermute | solution.py:287
  34.7 13.6 %collective-permute-start.9 = (bf16[64,512]{1,0:T(8,128)(2,1)S(1)}, bf16[64,512]{1,0:T(8,128)(2,1)S(1)}, u32[]{:S(2)}, u32[]{:S(2)}) collective-permute-start(bf16[64,512]{1,0:T(8,128)(2,1)S(1)} %key_value_rows.5), channel_id=1, source_target_pairs={{0,4},{1,5},{2,6},{3,7},{4,0},{5,1},{6,2},{7,3},{8,12},{9,13},{10,... | collective-permute-start | bytes 196616 | tf_op jit(solution)/shard_map/ppermute | solution.py:287
  35.9 13.1 %collective-permute-start.8 = (bf16[64,512]{1,0:T(8,128)(2,1)S(1)}, bf16[64,512]{1,0:T(8,128)(2,1)S(1)}, u32[]{:S(2)}, u32[]{:S(2)}) collective-permute-start(bf16[64,512]{1,0:T(8,128)(2,1)S(1)} %key_value_rows.5), channel_id=1, source_target_pairs={{0,2},{1,3},{2,4},{3,5},{4,6},{5,7},{6,0},{7,1},{8,10},{9,11},{10,... | collective-permute-start | bytes 196616 | tf_op jit(solution)/shard_map/ppermute | solution.py:287
  36.2 7.6 %collective-permute-start.3 = (bf16[32,4096]{1,0:T(8,128)(2,1)S(1)}, bf16[32,4096]{1,0:T(8,128)(2,1)S(1)}, u32[]{:S(2)}, u32[]{:S(2)}) collective-permute-start(bf16[32,4096]{1,0:T(8,128)(2,1)S(1)} %slice.41), channel_id=1, source_target_pairs={{0,8},{8,0},{16,24},{24,16},{1,9},{9,1},{17,25},{25,17},{2,10},{10... | collective-permute-start | bytes 786440 | tf_op jit(solution)/shard_map/ppermute | solution.py:268
  36.7 17.9 %slice-start.1 = ((s8[8388608]{0:T(1024)(128)(4,1)}), s8[4194304]{0:T(1024)(128)(4,1)S(1)}, s32[]{:S(2)}) async-start(s8[8388608]{0:T(1024)(128)(4,1)} %bitcast.43), calls=%async_computation.1 | async-start | bytes 8388608
  37.8 20.3 %collective-permute-start.15 = (bf16[4,64,512]{2,1,0:T(8,128)(2,1)S(1)}, bf16[4,64,512]{2,1,0:T(8,128)(2,1)S(1)}, u32[]{:S(2)}, u32[]{:S(2)}) collective-permute-start(bf16[4,64,512]{2,1,0:T(8,128)(2,1)S(1)} %get-tuple-element.30), channel_id=1, source_target_pairs={{0,1},{1,0},{2,3},{3,2},{4,5},{5,4},{6,7},{7,6},{8,9},{9,8},{10,11... | collective-permute-start | bytes 786440 | tf_op jit(solution)/shard_map/ppermute | solution.py:291
  43.8 10.8 %copy-start.5 = (bf16[64,4096]{1,0:T(8,128)(2,1)S(1)}, bf16[64,4096]{1,0:T(8,128)(2,1)}, u32[]{:S(2)}) copy-start(bf16[64,4096]{1,0:T(8,128)(2,1)} %tokens_ref.1) | copy-start | bytes 1572868
  44.7 5.5 %collective-permute-start.18 = (bf16[64,512]{1,0:T(8,128)(2,1)S(1)}, bf16[64,512]{1,0:T(8,128)(2,1)S(1)}, u32[]{:S(2)}, u32[]{:S(2)}) collective-permute-start(bf16[64,512]{1,0:T(8,128)(2,1)S(1)} %key_value_rows.7), channel_id=1, source_target_pairs={{0,6},{1,7},{2,0},{3,1},{4,2},{5,3},{6,4},{7,5},{8,14},{9,15},{10,... | collective-permute-start | bytes 196616 | tf_op jit(solution)/shard_map/ppermute | solution.py:287
  48.3 5.2 %collective-permute-start.17 = (bf16[64,512]{1,0:T(8,128)(2,1)S(1)}, bf16[64,512]{1,0:T(8,128)(2,1)S(1)}, u32[]{:S(2)}, u32[]{:S(2)}) collective-permute-start(bf16[64,512]{1,0:T(8,128)(2,1)S(1)} %key_value_rows.7), channel_id=1, source_target_pairs={{0,4},{1,5},{2,6},{3,7},{4,0},{5,1},{6,2},{7,3},{8,12},{9,13},{10,... | collective-permute-start | bytes 196616 | tf_op jit(solution)/shard_map/ppermute | solution.py:287
  48.3 6.1 %collective-permute-start.16 = (bf16[64,512]{1,0:T(8,128)(2,1)S(1)}, bf16[64,512]{1,0:T(8,128)(2,1)S(1)}, u32[]{:S(2)}, u32[]{:S(2)}) collective-permute-start(bf16[64,512]{1,0:T(8,128)(2,1)S(1)} %key_value_rows.7), channel_id=1, source_target_pairs={{0,2},{1,3},{2,4},{3,5},{4,6},{5,7},{6,0},{7,1},{8,10},{9,11},{10,... | collective-permute-start | bytes 196616 | tf_op jit(solution)/shard_map/ppermute | solution.py:287
  49.0 9.2 %collective-permute-start.11 = (bf16[4,64,512]{2,1,0:T(8,128)(2,1)S(1)}, bf16[4,64,512]{2,1,0:T(8,128)(2,1)S(1)}, u32[]{:S(2)}, u32[]{:S(2)}) collective-permute-start(bf16[4,64,512]{2,1,0:T(8,128)(2,1)S(1)} %get-tuple-element.28), channel_id=1, source_target_pairs={{0,1},{1,0},{2,3},{3,2},{4,5},{5,4},{6,7},{7,6},{8,9},{9,8},{10,11... | collective-permute-start | bytes 786440 | tf_op jit(solution)/shard_map/ppermute | solution.py:291
  54.5 3.8 %collective-permute-start.19 = (bf16[4,64,512]{2,1,0:T(8,128)(2,1)S(1)}, bf16[4,64,512]{2,1,0:T(8,128)(2,1)S(1)}, u32[]{:S(2)}, u32[]{:S(2)}) collective-permute-start(bf16[4,64,512]{2,1,0:T(8,128)(2,1)S(1)} %get-tuple-element.32), channel_id=1, source_target_pairs={{0,1},{1,0},{2,3},{3,2},{4,5},{5,4},{6,7},{7,6},{8,9},{9,8},{10,11... | collective-permute-start | bytes 786440 | tf_op jit(solution)/shard_map/ppermute | solution.py:291
  67.1 25.4 %collective-permute-start.24 = (bf16[64,2048]{1,0:T(8,128)(2,1)S(1)}, bf16[64,2048]{1,0:T(8,128)(2,1)S(1)}, u32[]{:S(2)}, u32[]{:S(2)}) collective-permute-start(bf16[64,2048]{1,0:T(8,128)(2,1)S(1)} %get-tuple-element.20), channel_id=1, source_target_pairs={{0,16},{8,24},{16,0},{24,8},{1,17},{9,25},{17,1},{25,9},{2,18},{10... | collective-permute-start | bytes 786440 | tf_op jit(solution)/shard_map/ppermute | solution.py:271
  81.0 12.8 %collective-permute-start.23 = (bf16[64,2048]{1,0:T(8,128)(2,1)S(1)}, bf16[64,2048]{1,0:T(8,128)(2,1)S(1)}, u32[]{:S(2)}, u32[]{:S(2)}) collective-permute-start(bf16[64,2048]{1,0:T(8,128)(2,1)S(1)} %get-tuple-element.18), channel_id=1, source_target_pairs={{0,16},{8,24},{16,0},{24,8},{1,17},{9,25},{17,1},{25,9},{2,18},{10... | collective-permute-start | bytes 786440 | tf_op jit(solution)/shard_map/ppermute | solution.py:271
  81.1 12.1 %collective-permute-start.21 = (bf16[64,2048]{1,0:T(8,128)(2,1)S(1)}, bf16[64,2048]{1,0:T(8,128)(2,1)S(1)}, u32[]{:S(2)}, u32[]{:S(2)}) collective-permute-start(bf16[64,2048]{1,0:T(8,128)(2,1)S(1)} %get-tuple-element.16), channel_id=1, source_target_pairs={{0,8},{8,0},{16,24},{24,16},{1,9},{9,1},{17,25},{25,17},{2,10},{10... | collective-permute-start | bytes 786440 | tf_op jit(solution)/shard_map/ppermute | solution.py:268
  81.7 17.5 %collective-permute-start.20 = (bf16[64,2048]{1,0:T(8,128)(2,1)S(1)}, bf16[64,2048]{1,0:T(8,128)(2,1)S(1)}, u32[]{:S(2)}, u32[]{:S(2)}) collective-permute-start(bf16[64,2048]{1,0:T(8,128)(2,1)S(1)} %get-tuple-element.14), channel_id=1, source_target_pairs={{0,8},{8,0},{16,24},{24,16},{1,9},{9,1},{17,25},{25,17},{2,10},{10... | collective-permute-start | bytes 786440 | tf_op jit(solution)/shard_map/ppermute | solution.py:268
  92.6 6.4 %collective-permute-start.25 = (bf16[64,2048]{1,0:T(8,128)(2,1)S(1)}, bf16[64,2048]{1,0:T(8,128)(2,1)S(1)}, u32[]{:S(2)}, u32[]{:S(2)}) collective-permute-start(bf16[64,2048]{1,0:T(8,128)(2,1)S(1)} %add_convert_fusion.1), channel_id=1, source_target_pairs={{0,8},{8,0},{16,24},{24,16},{1,9},{9,1},{17,25},{25,17},{2,10},{10... | collective-permute-start | bytes 786440 | tf_op jit(solution)/shard_map/ppermute | solution.py:268
  93.3 6.4 %collective-permute-start.22 = (bf16[64,2048]{1,0:T(8,128)(2,1)S(1)}, bf16[64,2048]{1,0:T(8,128)(2,1)S(1)}, u32[]{:S(2)}, u32[]{:S(2)}) collective-permute-start(bf16[64,2048]{1,0:T(8,128)(2,1)S(1)} %add_convert_fusion.3), channel_id=1, source_target_pairs={{0,16},{8,24},{16,0},{24,8},{1,17},{9,25},{17,1},{25,9},{2,18},{10... | collective-permute-start | bytes 786440 | tf_op jit(solution)/shard_map/ppermute | solution.py:271
  (6 other events, 6.3 us)

commit v2 on v1

--- a/solution.py
+++ b/solution.py
@@ -14,6 +14,7 @@
 NEG_FILL = -1e30
 WIDE = 8
 QUERY_FACTOR = HEAD_WIDTH**-0.5 * math.log2(math.e)
+ANY = pl.BlockSpec(memory_space=pl.ANY)
 VMEM = pl.BlockSpec(memory_space=pltpu.VMEM)
 SMEM = pl.BlockSpec(memory_space=pltpu.SMEM)
 MIB = 1 << 20
@@ -27,36 +28,82 @@
     return product * cosine + pltpu.roll(product, HEAD_WIDTH // 2, 1) * sine
 
 
-def key_value_kernel(tokens_ref, key_ref, value_ref, cos_ref, sin_ref, out_ref):
+def preload_kernel(count, *refs):
+    sources, targets, sems = refs[:count], refs[-1 - count : -1], refs[-1]
+    copies = [
+        pltpu.make_async_copy(source, target, sems.at[at])
+        for at, (source, target) in enumerate(zip(sources, targets))
+    ]
+    for copy in copies:
+        copy.start()
+    for copy in copies:
+        copy.wait()
+
+
+def preload(weights, after):
+    return pl.pallas_call(
+        functools.partial(preload_kernel, len(weights)),
+        out_shape=[pltpu.VMEM(weight.shape, weight.dtype) for weight in weights],
+        in_specs=[ANY] * (len(weights) + len(after)),
+        out_specs=[VMEM] * len(weights),
+        scratch_shapes=[pltpu.SemaphoreType.DMA((len(weights),))],
+        compiler_params=params(1),
+        name="preload",
+    )(*[pltpu.with_memory_space_constraint(weight, pltpu.HBM) for weight in weights], *after)
+
+
+def kept(weight):
+    return pltpu.with_memory_space_constraint(weight, pltpu.VMEM)
+
+
+def table_rows(ref, relatives, piece_rows):
+    if relatives is None:
+        return ref[...]
+    grp = lax.axis_index("grp")
+    return jnp.concatenate(
+        [
+            ref[pl.ds(pl.multiple_of((grp ^ r) * piece_rows, piece_rows), piece_rows)]
+            for r in relatives
+        ],
+        axis=0,
+    )
+
+
+def key_value_kernel(count, relatives, *refs):
+    pieces, (key_ref, value_ref, cos_ref, sin_ref, *_, out_ref) = refs[:count], refs[count:]
     width = key_ref.shape[1]
-    rows = tokens_ref[...]
+    rows = jnp.concatenate([piece[...] for piece in pieces], axis=0)
     keys = jnp.dot(rows, key_ref[...], preferred_element_type=jnp.float32)
     values = jnp.dot(rows, value_ref[...], preferred_element_type=jnp.float32)
-    cosine, sine = cos_ref[...], sin_ref[...]
+    cosine = table_rows(cos_ref, relatives, pieces[0].shape[0])
+    sine = table_rows(sin_ref, relatives, pieces[0].shape[0])
     for at in range(0, width, HEAD_WIDTH):
         head = slice(at, at + HEAD_WIDTH)
         out_ref[:, head] = turn(keys[:, head], cosine, sine).astype(out_ref.dtype)
     out_ref[:, width:] = values.astype(out_ref.dtype)
 
 
-def key_value_rows(rows, key_weight, value_weight, cosine, sine):
+def key_value_rows(
+    pieces, key_weight, value_weight, cosine, sine, relatives=None, after=(), weigh=1
+):
+    rows = sum(piece.shape[0] for piece in pieces)
     width = key_weight.shape[1] + value_weight.shape[1]
     return pl.pallas_call(
-        key_value_kernel,
-        out_shape=jax.ShapeDtypeStruct((rows.shape[0], width), jnp.bfloat16),
-        in_specs=[VMEM] * 5,
+        functools.partial(key_value_kernel, len(pieces), relatives),
+        out_shape=jax.ShapeDtypeStruct((rows, width), jnp.bfloat16),
+        in_specs=[VMEM] * (len(pieces) + 4) + [ANY] * len(after),
         out_specs=VMEM,
-        compiler_params=params(24),
+        compiler_params=params(16),
         cost_estimate=pl.CostEstimate(
-            flops=2 * rows.shape[0] * rows.shape[1] * width,
-            bytes_accessed=2 * (rows.size + key_weight.size + value_weight.size),
+            flops=2 * rows * (key_weight.size + value_weight.size) * weigh,
+            bytes_accessed=2 * (key_weight.size + value_weight.size),
             transcendentals=0,
         ),
         name="key_value_rows",
-    )(rows, key_weight, value_weight, cosine, sine)
-
-
-def query_kernel(*refs):
+    )(*pieces, kept(key_weight), kept(value_weight), cosine, sine, *after)
+
+
+def query_kernel(relatives, *refs):
     count = len(refs) - 4
     pieces, (weight_ref, cos_ref, sin_ref, out_ref) = refs[:count], refs[count:]
     step = 2 * HEAD_WIDTH
@@ -66,33 +113,34 @@
     def _(tile):
         at = pl.multiple_of(tile * step, step)
         product = jnp.dot(rows, weight_ref[:, pl.ds(at, step)], preferred_element_type=jnp.float32)
-        cosine, sine = cos_ref[...] * QUERY_FACTOR, sin_ref[...] * QUERY_FACTOR
+        cosine = table_rows(cos_ref, relatives, pieces[0].shape[0]) * QUERY_FACTOR
+        sine = table_rows(sin_ref, relatives, pieces[0].shape[0]) * QUERY_FACTOR
         for half in range(2):
             head = turn(product[:, half * HEAD_WIDTH : (half + 1) * HEAD_WIDTH], cosine, sine)
             out_ref[:, pl.ds(at + half * HEAD_WIDTH, HEAD_WIDTH)] = head.astype(out_ref.dtype)
 
 
-def query_rows(pieces, weight, cosine, sine):
+def query_rows(pieces, weight, cosine, sine, relatives=None):
     rows = sum(piece.shape[0] for piece in pieces)
     return pl.pallas_call(
-        query_kernel,
+        functools.partial(query_kernel, relatives),
         out_shape=jax.ShapeDtypeStruct((rows, weight.shape[1]), jnp.bfloat16),
         in_specs=[VMEM] * (len(pieces) + 3),
         out_specs=VMEM,
-        compiler_params=params(32),
+        compiler_params=params(18),
         cost_estimate=pl.CostEstimate(
             flops=2 * rows * weight.size, bytes_accessed=2 * weight.size, transcendentals=0
         ),
         name="query_rows",
-    )(*pieces, weight, cosine, sine)
-
-
-def attend_kernel(relatives, blk_count, groups, placed, place_ref, mask_ref, query_ref, kv_ref, weight_ref, *rest):
+    )(*pieces, kept(weight), cosine, sine)
+
+
+def attend_kernel(relatives, blk_count, groups, placed, mask_ref, query_ref, kv_ref, weight_ref, *rest):
     out_refs, (live_ref, mixed_ref) = rest[: 2 * len(relatives)], rest[2 * len(relatives) :]
-    grp, chip, core = place_ref[0], place_ref[1], place_ref[2]
+    grp, blk = lax.axis_index("grp"), lax.axis_index("blk")
+    chip, core = blk // 2, blk % 2
     piece_rows = query_ref.shape[0] // groups
     own_blocks = mask_ref.shape[0]
-    chips = blk_count // 2
     kv_heads = kv_ref.shape[1] // (2 * HEAD_WIDTH)
     repeat = query_ref.shape[1] // (kv_heads * HEAD_WIDTH)
     block = MASK_BLOCK_TOKENS
@@ -107,7 +155,7 @@
             if placed:
                 owner_at, inner = index // own_blocks, index % own_blocks
                 shift, other = owner_at // 2, owner_at % 2
-                owner = lax.rem(chip - shift + chips, chips) * 2 + lax.bitwise_xor(core, other)
+                owner = lax.bitwise_xor(chip, shift) * 2 + lax.bitwise_xor(core, other)
                 key_block = owner * own_blocks + lax.bitwise_xor(inner, turned)
             live = mask_ref[query_block, key_block]
             live_ref[count] = index
@@ -197,36 +245,64 @@
                 ]
 
 
-def attend(relatives, blk_count, groups, placed, place, mask, query, kv, weight):
+def gather_kernel(piece_counts, *refs):
+    parts, out_ref = refs[:-1], refs[-1]
+    shifts = parts[0].shape[0]
+    piece_rows = parts[0].shape[1] // piece_counts[0]
+    total = sum(piece_counts)
+    for shift in range(shifts):
+        for core in range(2):
+            piece = 0
+            for chunk, pieces in enumerate(piece_counts):
+                at = ((shift * 2 + core) * total + piece) * piece_rows
+                out_ref[at : at + pieces * piece_rows] = parts[2 * chunk + core][shift]
+                piece += pieces
+
+
+def gather_rows(piece_counts, parts):
+    shifts, _, width = parts[0].shape
+    rows = sum(2 * shifts * part.shape[1] for part in parts[::2])
+    return pl.pallas_call(
+        functools.partial(gather_kernel, piece_counts),
+        out_shape=jax.ShapeDtypeStruct((rows, width), jnp.bfloat16),
+        in_specs=[VMEM] * len(parts),
+        out_specs=VMEM,
+        compiler_params=params(12),
+        name="key_value_gather",
+    )(*parts)
+
+
+def attend(relatives, blk_count, groups, placed, mask, query, kv, weight):
     piece_rows = query.shape[0] // groups
     side = jax.ShapeDtypeStruct((piece_rows, weight.shape[1] // 2), jnp.bfloat16)
     return pl.pallas_call(
         functools.partial(attend_kernel, relatives, blk_count, groups, placed),
         out_shape=[side] * (2 * len(relatives)),
-        in_specs=[SMEM, SMEM, VMEM, VMEM, VMEM],
+        in_specs=[SMEM, VMEM, VMEM, VMEM],
         out_specs=[VMEM] * (2 * len(relatives)),
         scratch_shapes=[
             pltpu.SMEM((mask.shape[1] + 2 * WIDE,), jnp.int32),
             pltpu.VMEM((len(relatives) * piece_rows, weight.shape[0]), jnp.bfloat16),
         ],
-        compiler_params=params(48),
+        compiler_params=params(20 if placed else 48),
         cost_estimate=pl.CostEstimate(
             flops=2 * len(relatives) * piece_rows * weight.size * 2,
             bytes_accessed=2 * weight.size,
             transcendentals=0,
         ),
         name="attend_project",
-    )(place, mask, query, kv, weight)
-
-
-def rotary_tables(rows):
+    )(mask, query, kv, kept(weight))
+
+
+def rotary_tables(positions):
+    half = HEAD_WIDTH // 2
     inverse = jnp.power(
         jnp.float32(ROPE_BASE),
-        -(2.0 * jnp.arange(HEAD_WIDTH // 2, dtype=jnp.float32)) / HEAD_WIDTH,
-    )
-    angles = rows.astype(jnp.float32)[:, None] * inverse[None, :]
-    cosine, sine = jnp.cos(angles), jnp.sin(angles)
-    return jnp.concatenate([cosine, cosine], axis=1), jnp.concatenate([-sine, sine], axis=1)
+        -(2.0 * (jnp.arange(HEAD_WIDTH) % half).astype(jnp.float32)) / HEAD_WIDTH,
+    )
+    sign = jnp.where(jnp.arange(HEAD_WIDTH) < half, -1.0, 1.0)
+    angles = positions.astype(jnp.float32)[:, None] * inverse[None, :]
+    return jnp.cos(angles), jnp.sin(angles) * sign[None, :]
 
 
 def add(*values):
@@ -241,12 +317,11 @@
 ):
     rows = lax.all_gather(tokens, "grp", axis=0, tiled=True)
     cosine, sine = rotary_tables(positions)
-    own = key_value_rows(rows, key_weight, value_weight, cosine, sine)
+    own = key_value_rows((rows,), key_weight, value_weight, cosine, sine)
     kv = lax.all_gather(own, "blk", axis=0, tiled=True)
     query = query_rows((rows,), w_query, cosine, sine)
-    place = jnp.zeros((3,), jnp.int32)
     order = tuple(range(groups))
-    sides = attend(order, blk_count, groups, False, place, block_mask, query, kv, w_output)
+    sides = attend(order, blk_count, groups, False, block_mask, query, kv, w_output)
     term = jnp.concatenate(
         [jnp.concatenate(sides[side::2], axis=0) for side in range(2)], axis=1
     )
@@ -256,7 +331,6 @@
 def square_body(
     blk_count, tokens, w_query, key_weight, value_weight, w_output, block_mask, positions
 ):
-    grp, blk = lax.axis_index("grp"), lax.axis_index("blk")
     along_x = [(g, g ^ 1) for g in range(4)]
     along_y = [(g, g ^ 2) for g in range(4)]
     cores = [(b, b ^ 1) for b in range(blk_count)]
@@ -273,29 +347,34 @@
     from_x, from_y = send_x(tokens), send_y(tokens)
     across = jnp.concatenate([send_y(from_x[:half]), send_x(from_y[half:])], axis=0)
 
-    rows = positions.reshape(2, 2, piece_rows)
-    rows = jnp.where(grp % 2 == 1, rows[:, ::-1], rows)
-    rows = jnp.where(grp // 2 == 1, rows[::-1], rows).reshape(4 * piece_rows)
-    cosine, sine = rotary_tables(rows)
-
-    pieces = (tokens, from_x, from_y, across)
-    received = []
-    for relative, piece in enumerate(pieces):
-        here = slice(relative * piece_rows, (relative + 1) * piece_rows)
-        own = key_value_rows(piece, key_weight, value_weight, cosine[here], sine[here])
+    cosine, sine = rotary_tables(positions)
+    key_weight, value_weight, w_query, w_output = preload(
+        (key_weight, value_weight, w_query, w_output), (cosine, sine)
+    )
+
+    def exchange(pieces, first, after, weigh):
+        relatives = tuple(range(first, first + len(pieces)))
+        own = key_value_rows(
+            pieces, key_weight, value_weight, cosine, sine, relatives, after, weigh
+        )
         shifted = [own] + [
-            lax.ppermute(own, "blk", [(b, (b + 2 * s) % blk_count) for b in range(blk_count)])
+            lax.ppermute(own, "blk", [(b, b ^ (2 * s)) for b in range(blk_count)])
             for s in range(1, chips)
         ]
         shifted = jnp.stack(shifted)
-        received.append(jnp.stack([shifted, lax.ppermute(shifted, "blk", cores)], axis=1))
-    width = received[0].shape[-1]
-    kv = jnp.stack(received, axis=2).reshape(blk_count * 4 * piece_rows, width)
-    query = query_rows(pieces, w_query, cosine, sine)
-    place = jnp.stack([grp, blk // 2, blk % 2]).astype(jnp.int32)
+        return [shifted, lax.ppermute(shifted, "blk", cores)]
+
+    pieces = (tokens, from_x, from_y, across)
+    chunks = ((tokens,), (from_x, from_y), (across,))
+    parts, first = [], 0
+    for chunk in chunks:
+        parts += exchange(chunk, first, parts[:2], 40 if len(chunk) > 1 else 1)
+        first += len(chunk)
+    kv = gather_rows(tuple(len(chunk) for chunk in chunks), parts)
+    query = query_rows(pieces, w_query, cosine, sine, tuple(range(4)))
 
     def terms(relatives):
-        return attend(relatives, blk_count, 4, True, place, block_mask, query, kv, w_output)
+        return attend(relatives, blk_count, 4, True, block_mask, query, kv, w_output)
 
     across_a, across_b = terms((3,))
     second_a, second_b = send_x(across_a), send_y(across_b)
@@ -311,7 +390,7 @@
 
 def solution(mesh):
     groups, blk_count = mesh.shape["grp"], mesh.shape["blk"]
-    if groups == 4:
+    if groups == 4 and blk_count & (blk_count - 1) == 0:
         body = functools.partial(square_body, blk_count)
     else:
         body = functools.partial(general_body, blk_count, groups)

time: 101 us -> 86.7 us (0.86)
  local copies, waits for them, and re-layouts: 8 us -> 0.59 us
  other arithmetic: 5.79 us -> 2.53 us
  Pallas kernels: 36.1 us -> 33.3 us
  starting transfers between devices: 27.3 us -> 24.8 us
  waiting for transfers between devices: 23.2 us -> 25.1 us
    ppermute x5, waiting for transfers between devices: 11.2 us -> 0.59 us  [send_x(): return lax.ppermute(value, 'grp', along_x)]
    pallas_call x3, Pallas kernels: 28.9 us -> 19.9 us  [attend(): pl.pallas_call(functools.partial(attend_kernel, relatives, blk_count, gro...]
    ppermute x16 -> x12, waiting for transfers between devices: 10.4 us -> 19.3 us  [the longest x9 18.4 us: exchange(): lax.ppermute(own, 'blk', [(b, b ^ 2 * s) for b in range(blk_count)])]
    unnamed x25 -> x5, local copies, waits for them, and re-layouts: 6.94 us -> 0.53 us
    pallas_call x5 -> x6, Pallas kernels: 7.17 us -> 13.4 us  [the longest x1 7.13 us: preload(): pl.pallas_call(functools.partial(preload_kernel, len(weights)), out_shape...]
    ppermute x5, waiting for transfers between devices: 1.63 us -> 5.15 us  [send_y(): return lax.ppermute(value, 'grp', along_y)]
    another operation x10 -> x3, other arithmetic: 2.76 us -> 0.14 us  [exchange(): shifted = jnp.stack(shifted)]
    ppermute x16 -> x12, starting transfers between devices: 16.2 us -> 13.6 us  [the longest x9 13.4 us: exchange(): lax.ppermute(own, 'blk', [(b, b ^ 2 * s) for b in range(blk_count)])]
  transfers between devices with their start and end apart: 26 -> 22, of which waited for: 10 -> 9; matrix products, arithmetic and copies ran while one was open for 5% -> 2% of each run, Pallas kernels for 28% -> 33%
where the time goes in v2:
time: 86.7 us; the launch traced here: 86.5 us
  Pallas kernels  33.3 us (38%)
  waiting for transfers between devices  25.1 us (29%)
  starting transfers between devices  24.8 us (29%)
  other arithmetic  2.53 us (3%)
    pallas_call x3, Pallas kernels, attend(): pl.pallas_call(functools.partial(attend_kernel, relatives, blk_count, gro...  19.9 us
    ppermute x9, waiting for transfers between devices, exchange(): lax.ppermute(own, 'blk', [(b, b ^ 2 * s) for b in range(blk_count)])  18.4 us
    ppermute x9, starting transfers between devices, exchange(): lax.ppermute(own, 'blk', [(b, b ^ 2 * s) for b in range(blk_count)])  13.4 us
    pallas_call x1, Pallas kernels, preload(): pl.pallas_call(functools.partial(preload_kernel, len(weights)), out_shape...  7.13 us
    ppermute x5, starting transfers between devices, send_y(): return lax.ppermute(value, 'grp', along_y)  6.31 us
    ppermute x5, waiting for transfers between devices, send_y(): return lax.ppermute(value, 'grp', along_y)  5.15 us
    ppermute x5, starting transfers between devices, send_x(): return lax.ppermute(value, 'grp', along_x)  4.85 us
    pallas_call x1, Pallas kernels, query_rows(): pl.pallas_call(functools.partial(query_kernel, relatives), out_shape=jax....  3.49 us
  transfers between devices with their start and end apart: 22, of which 9 were waited for; matrix products, arithmetic and copies ran while one was open for 2% of the time, Pallas kernels for 33%

profile of v2, /device:TPU:0, one launch (start us, length us, event | category | flops | bytes accessed | tf_op | source)
XLA Modules:
  0.0 86.5 jit_solution(12494609556655118926)
XLA Ops:
  0.0 3.0 %collective-permute-start.1 = (bf16[64,4096]{1,0:T(8,128)(2,1)}, bf16[64,4096]{1,0:T(8,128)(2,1)S(1)}, u32[]{:S(2)}, u32[]{:S(2)}) collective-permute-start(bf16[64,4096]{1,0:T(8,128)(2,1)} %refs_0_.5), channel_id=1, source_target_pairs={{0,16},{8,24},{16,0},{24,8},{1,17},{9,25},{17,1},{25,9},{2,18},{10... | collective-permute-start | bytes 1572872 | tf_op jit(solution)/shard_map/ppermute | solution.py:345
  3.0 1.5 %collective-permute-start = (bf16[64,4096]{1,0:T(8,128)(2,1)}, bf16[64,4096]{1,0:T(8,128)(2,1)S(1)}, u32[]{:S(2)}, u32[]{:S(2)}) collective-permute-start(bf16[64,4096]{1,0:T(8,128)(2,1)} %refs_0_.5), channel_id=1, source_target_pairs={{0,8},{8,0},{16,24},{24,16},{1,9},{9,1},{17,25},{25,17},{2,10},{10... | collective-permute-start | bytes 1572872 | tf_op jit(solution)/shard_map/ppermute | solution.py:342
  4.5 0.7 convert_element_type.52
  5.7 7.1 %preload.1 = (bf16[4096,256]{1,0:T(8,128)(2,1)S(1)}, bf16[4096,256]{1,0:T(8,128)(2,1)S(1)}, bf16[4096,1024]{1,0:T(8,128)(2,1)S(1)}, bf16[1024,4096]{1,0:T(8,128)(2,1)S(1)}) custom-call(bf16[4096,256]{1,0:T(8,128)(2,1)} %refs_0_.3, bf16[4096,256]{1,0:T(8,128)(2,1)} %refs_1_.1, bf16[4096,1024]{1,0:T(8,128)(2,1)} %refs_2_.1, bf16[1024,4096]{1,0:T(8,128)(2,1)} %refs_3_.1, ...), custom_call_target="tpu_custom_call" | custom-call | tf_op jit(solution)/shard_map/preload/pallas_call | solution.py:44
  12.9 0.9 %key_value_rows.3 = bf16[64,512]{1,0:T(8,128)(2,1)S(1)} custom-call(bf16[64,4096]{1,0:T(8,128)(2,1)S(1)} %copy-done, bf16[4096,256]{1,0:T(8,128)(2,1)S(1)} %get-tuple-element.18.refs_1_.refs_2_, bf16[4096,256]{1,0:T(8,128)(2,1)S(1)} %get-tuple-element.19.refs_2_.refs_3_, f32[256,128]{1,0:T(8,128)S(1)} %get-tuple-element.30.refs_4_.refs_5_.refs_3_, ...), custom_call_target="tpu_custom_call" | custom-call | flops 268435456 | bytes 4194304 | tf_op jit(solution)/shard_map/key_value_rows/pallas_call | solution.py:91
  13.8 3.7 %collective-permute-start.6 = (bf16[64,512]{1,0:T(8,128)(2,1)S(1)}, bf16[64,512]{1,0:T(8,128)(2,1)S(1)}, u32[]{:S(2)}, u32[]{:S(2)}) collective-permute-start(bf16[64,512]{1,0:T(8,128)(2,1)S(1)} %key_value_rows.3), channel_id=1, source_target_pairs={{0,6},{1,7},{2,4},{3,5},{4,2},{5,3},{6,0},{7,1},{8,14},{9,15},{10,... | collective-permute-start | bytes 196616 | tf_op jit(solution)/shard_map/ppermute | solution.py:361
  17.4 0.8 collective-permute-start.4
  18.2 2.2 %collective-permute-done.6 = bf16[64,512]{1,0:T(8,128)(2,1)S(1)} collective-permute-done((bf16[64,512]{1,0:T(8,128)(2,1)S(1)}, bf16[64,512]{1,0:T(8,128)(2,1)S(1)}, u32[]{:S(2)}, u32[]{:S(2)}) %collective-permute-start.6) | collective-permute-done | bytes 65568 | tf_op jit(solution)/shard_map/ppermute | solution.py:361
  20.4 2.3 %collective-permute-done.5 = bf16[64,512]{1,0:T(8,128)(2,1)S(1)} collective-permute-done((bf16[64,512]{1,0:T(8,128)(2,1)S(1)}, bf16[64,512]{1,0:T(8,128)(2,1)S(1)}, u32[]{:S(2)}, u32[]{:S(2)}) %collective-permute-start.5) | collective-permute-done | bytes 65568 | tf_op jit(solution)/shard_map/ppermute | solution.py:361
  23.4 0.9 %collective-permute-done.7.refs_7_.refs_6_.refs_1_ = bf16[4,64,512]{2,1,0:T(8,128)(2,1)S(1)} collective-permute-done((bf16[4,64,512]{2,1,0:T(8,128)(2,1)S(1)}, bf16[4,64,512]{2,1,0:T(8,128)(2,1)S(1)}, u32[]{:S(2)}, u32[]{:S(2)}) %collective-permute-start.7) | collective-permute-done | bytes 262176 | tf_op jit(solution)/shard_map/ppermute | solution.py:365
  24.3 0.8 key_value_rows.4
  25.1 2.6 %collective-permute-start.10 = (bf16[128,512]{1,0:T(8,128)(2,1)S(1)}, bf16[128,512]{1,0:T(8,128)(2,1)S(1)}, u32[]{:S(2)}, u32[]{:S(2)}) collective-permute-start(bf16[128,512]{1,0:T(8,128)(2,1)S(1)} %key_value_rows.4), channel_id=1, source_target_pairs={{0,6},{1,7},{2,4},{3,5},{4,2},{5,3},{6,0},{7,1},{8,14},{9,15},{10,... | collective-permute-start | bytes 393224 | tf_op jit(solution)/shard_map/ppermute | solution.py:361
  27.7 1.9 %collective-permute-start.8 = (bf16[128,512]{1,0:T(8,128)(2,1)S(1)}, bf16[128,512]{1,0:T(8,128)(2,1)S(1)}, u32[]{:S(2)}, u32[]{:S(2)}) collective-permute-start(bf16[128,512]{1,0:T(8,128)(2,1)S(1)} %key_value_rows.4), channel_id=1, source_target_pairs={{0,2},{1,3},{2,0},{3,1},{4,6},{5,7},{6,4},{7,5},{8,10},{9,11},{10,... | collective-permute-start | bytes 393224 | tf_op jit(solution)/shard_map/ppermute | solution.py:361
  29.6 0.6 collective-permute-start.3
  30.2 3.2 %collective-permute-done.10 = bf16[128,512]{1,0:T(8,128)(2,1)S(1)} collective-permute-done((bf16[128,512]{1,0:T(8,128)(2,1)S(1)}, bf16[128,512]{1,0:T(8,128)(2,1)S(1)}, u32[]{:S(2)}, u32[]{:S(2)}) %collective-permute-start.10) | collective-permute-done | bytes 131104 | tf_op jit(solution)/shard_map/ppermute | solution.py:361
  33.4 6.0 %collective-permute-done.9 = bf16[128,512]{1,0:T(8,128)(2,1)S(1)} collective-permute-done((bf16[128,512]{1,0:T(8,128)(2,1)S(1)}, bf16[128,512]{1,0:T(8,128)(2,1)S(1)}, u32[]{:S(2)}, u32[]{:S(2)}) %collective-permute-start.9) | collective-permute-done | bytes 131104 | tf_op jit(solution)/shard_map/ppermute | solution.py:361
  39.7 0.9 %key_value_rows.5 = bf16[64,512]{1,0:T(8,128)(2,1)S(1)} custom-call(bf16[64,4096]{1,0:T(8,128)(2,1)S(1)} %constant_dynamic-update-slice_fusion.refs_3_.refs_0_, bf16[4096,256]{1,0:T(8,128)(2,1)S(1)} %get-tuple-element.18.refs_1_.refs_2_, bf16[4096,256]{1,0:T(8,128)(2,1)S(1)} %get-tuple-element.19.refs_2_.refs_3_, ...), custom_call_target="tpu_custom_call" | custom-call | flops 268435456 | bytes 4194304 | tf_op jit(solution)/shard_map/key_value_rows/pallas_call | solution.py:91
  40.6 2.6 %collective-permute-start.14 = (bf16[64,512]{1,0:T(8,128)(2,1)S(1)}, bf16[64,512]{1,0:T(8,128)(2,1)S(1)}, u32[]{:S(2)}, u32[]{:S(2)}) collective-permute-start(bf16[64,512]{1,0:T(8,128)(2,1)S(1)} %key_value_rows.5), channel_id=1, source_target_pairs={{0,6},{1,7},{2,4},{3,5},{4,2},{5,3},{6,0},{7,1},{8,14},{9,15},{10,... | collective-permute-start | bytes 196616 | tf_op jit(solution)/shard_map/ppermute | solution.py:361
  43.2 1.9 %collective-permute-start.12 = (bf16[64,512]{1,0:T(8,128)(2,1)S(1)}, bf16[64,512]{1,0:T(8,128)(2,1)S(1)}, u32[]{:S(2)}, u32[]{:S(2)}) collective-permute-start(bf16[64,512]{1,0:T(8,128)(2,1)S(1)} %key_value_rows.5), channel_id=1, source_target_pairs={{0,2},{1,3},{2,0},{3,1},{4,6},{5,7},{6,4},{7,5},{8,10},{9,11},{10,... | collective-permute-start | bytes 196616 | tf_op jit(solution)/shard_map/ppermute | solution.py:361
  45.1 2.3 %collective-permute-done.14 = bf16[64,512]{1,0:T(8,128)(2,1)S(1)} collective-permute-done((bf16[64,512]{1,0:T(8,128)(2,1)S(1)}, bf16[64,512]{1,0:T(8,128)(2,1)S(1)}, u32[]{:S(2)}, u32[]{:S(2)}) %collective-permute-start.14) | collective-permute-done | bytes 65568 | tf_op jit(solution)/shard_map/ppermute | solution.py:361
  47.4 2.4 %collective-permute-done.13 = bf16[64,512]{1,0:T(8,128)(2,1)S(1)} collective-permute-done((bf16[64,512]{1,0:T(8,128)(2,1)S(1)}, bf16[64,512]{1,0:T(8,128)(2,1)S(1)}, u32[]{:S(2)}, u32[]{:S(2)}) %collective-permute-start.13) | collective-permute-done | bytes 65568 | tf_op jit(solution)/shard_map/ppermute | solution.py:361
  49.9 3.5 %query_rows.1.query_ref = bf16[256,1024]{1,0:T(8,128)(2,1)S(1)} custom-call(bf16[64,4096]{1,0:T(8,128)(2,1)S(1)} %copy-done, bf16[64,4096]{1,0:T(8,128)(2,1)S(1)} %collective-permute-done.refs_1_.refs_0_, bf16[64,4096]{1,0:T(8,128)(2,1)S(1)} %collective-permute-done.1.refs_2_.refs_1_, bf16[64,4096]{1,0:T(8,128)(2,1)S(1)} %constant_dynamic-update-slice_fusion.refs_3_.refs_0_, ...), custom_call_target="tpu_custom_call" | custom-call | flops 2147483648 | bytes 8388608 | tf_op jit(solution)/shard_map/query_rows/pallas_call | solution.py:125
  54.1 5.0 %attend_project.5 = (bf16[64,2048]{1,0:T(8,128)(2,1)S(1)}, bf16[64,2048]{1,0:T(8,128)(2,1)S(1)}) custom-call(s32[2,16]{1,0:T(2,128)S(1)} %copy-done.1, bf16[256,1024]{1,0:T(8,128)(2,1)S(1)} %query_rows.1.query_ref, bf16[2048,512]{1,0:T(8,128)(2,1)S(1)} %key_value_gather.1.kv_ref, bf16[1024,4096]{1,0:T(8,128)(2,1)S(1)} %get-tuple-element.20.weight_ref), custom_call_target="tpu_custom_call" | custom-call | flops 1073741824 | bytes 8388608 | tf_op jit(solution)/shard_map/attend_project/pallas_call | solution.py:278
  59.1 0.6 collective-permute-start.17
  59.7 2.2 %collective-permute-start.20 = (bf16[64,2048]{1,0:T(8,128)(2,1)S(1)}, bf16[64,2048]{1,0:T(8,128)(2,1)S(1)}, u32[]{:S(2)}, u32[]{:S(2)}) collective-permute-start(bf16[64,2048]{1,0:T(8,128)(2,1)S(1)} %get-tuple-element.28), channel_id=1, source_target_pairs={{0,16},{8,24},{16,0},{24,8},{1,17},{9,25},{17,1},{25,9},{2,18},{10... | collective-permute-start | bytes 786440 | tf_op jit(solution)/shard_map/ppermute | solution.py:345
  61.8 8.5 %attend_project.4 = (bf16[64,2048]{1,0:T(8,128)(2,1)S(1)}, bf16[64,2048]{1,0:T(8,128)(2,1)S(1)}, bf16[64,2048]{1,0:T(8,128)(2,1)S(1)}, bf16[64,2048]{1,0:T(8,128)(2,1)S(1)}) custom-call(s32[2,16]{1,0:T(2,128)S(1)} %copy-done.1, bf16[256,1024]{1,0:T(8,128)(2,1)S(1)} %query_rows.1.query_ref, bf16[2048,512]{1,0:T(8,128)(2,1)S(1)} %key_value_gather.1.kv_ref, ...), custom_call_target="tpu_custom_call" | custom-call | flops 2147483648 | bytes 8388608 | tf_op jit(solution)/shard_map/attend_project/pallas_call | solution.py:278
  70.4 1.6 %collective-permute-start.16 = (bf16[64,2048]{1,0:T(8,128)(2,1)S(1)}, bf16[64,2048]{1,0:T(8,128)(2,1)S(1)}, u32[]{:S(2)}, u32[]{:S(2)}) collective-permute-start(bf16[64,2048]{1,0:T(8,128)(2,1)S(1)} %get-tuple-element.22), channel_id=1, source_target_pairs={{0,8},{8,0},{16,24},{24,16},{1,9},{9,1},{17,25},{25,17},{2,10},{10... | collective-permute-start | bytes 786440 | tf_op jit(solution)/shard_map/ppermute | solution.py:342
  71.9 6.4 %attend_project.3 = (bf16[64,2048]{1,0:T(8,128)(2,1)S(1)}, bf16[64,2048]{1,0:T(8,128)(2,1)S(1)}) custom-call(s32[2,16]{1,0:T(2,128)S(1)} %copy-done.1, bf16[256,1024]{1,0:T(8,128)(2,1)S(1)} %query_rows.1.query_ref, bf16[2048,512]{1,0:T(8,128)(2,1)S(1)} %key_value_gather.1.kv_ref, bf16[1024,4096]{1,0:T(8,128)(2,1)S(1)} %get-tuple-element.20.weight_ref), custom_call_target="tpu_custom_call" | custom-call | flops 1073741824 | bytes 8388608 | tf_op jit(solution)/shard_map/attend_project/pallas_call | solution.py:278
  78.5 0.6 collective-permute-start.18
  79.1 0.6 collective-permute-start.21
  79.8 5.1 %collective-permute-done.18 = bf16[64,2048]{1,0:T(8,128)(2,1)S(1)} collective-permute-done((bf16[64,2048]{1,0:T(8,128)(2,1)S(1)}, bf16[64,2048]{1,0:T(8,128)(2,1)S(1)}, u32[]{:S(2)}, u32[]{:S(2)}) %collective-permute-start.18) | collective-permute-done | bytes 262176 | tf_op jit(solution)/shard_map/ppermute | solution.py:345
  85.7 0.8 pad_maximum_fusion.1
  (40 shorter events, 3.2 us)
Async XLA Ops:
  0.0 24.3 %collective-permute-start.1 = (bf16[64,4096]{1,0:T(8,128)(2,1)}, bf16[64,4096]{1,0:T(8,128)(2,1)S(1)}, u32[]{:S(2)}, u32[]{:S(2)}) collective-permute-start(bf16[64,4096]{1,0:T(8,128)(2,1)} %refs_0_.5), channel_id=1, source_target_pairs={{0,16},{8,24},{16,0},{24,8},{1,17},{9,25},{17,1},{25,9},{2,18},{10... | collective-permute-start | bytes 1572872 | tf_op jit(solution)/shard_map/ppermute | solution.py:345
  3.0 19.8 %collective-permute-start = (bf16[64,4096]{1,0:T(8,128)(2,1)}, bf16[64,4096]{1,0:T(8,128)(2,1)S(1)}, u32[]{:S(2)}, u32[]{:S(2)}) collective-permute-start(bf16[64,4096]{1,0:T(8,128)(2,1)} %refs_0_.5), channel_id=1, source_target_pairs={{0,8},{8,0},{16,24},{24,16},{1,9},{9,1},{17,25},{25,17},{2,10},{10... | collective-permute-start | bytes 1572872 | tf_op jit(solution)/shard_map/ppermute | solution.py:342
  5.7 7.1 %copy-start = (bf16[64,4096]{1,0:T(8,128)(2,1)S(1)}, bf16[64,4096]{1,0:T(8,128)(2,1)}, u32[]{:S(2)}) copy-start(bf16[64,4096]{1,0:T(8,128)(2,1)} %refs_0_.5) | copy-start | bytes 1572868
  13.8 6.7 %collective-permute-start.6 = (bf16[64,512]{1,0:T(8,128)(2,1)S(1)}, bf16[64,512]{1,0:T(8,128)(2,1)S(1)}, u32[]{:S(2)}, u32[]{:S(2)}) collective-permute-start(bf16[64,512]{1,0:T(8,128)(2,1)S(1)} %key_value_rows.3), channel_id=1, source_target_pairs={{0,6},{1,7},{2,4},{3,5},{4,2},{5,3},{6,0},{7,1},{8,14},{9,15},{10,... | collective-permute-start | bytes 196616 | tf_op jit(solution)/shard_map/ppermute | solution.py:361
  17.4 5.2 %collective-permute-start.5 = (bf16[64,512]{1,0:T(8,128)(2,1)S(1)}, bf16[64,512]{1,0:T(8,128)(2,1)S(1)}, u32[]{:S(2)}, u32[]{:S(2)}) collective-permute-start(bf16[64,512]{1,0:T(8,128)(2,1)S(1)} %key_value_rows.3), channel_id=1, source_target_pairs={{0,4},{1,5},{2,6},{3,7},{4,0},{5,1},{6,2},{7,3},{8,12},{9,13},{10,... | collective-permute-start | bytes 196616 | tf_op jit(solution)/shard_map/ppermute | solution.py:361
  17.4 5.2 %collective-permute-start.4 = (bf16[64,512]{1,0:T(8,128)(2,1)S(1)}, bf16[64,512]{1,0:T(8,128)(2,1)S(1)}, u32[]{:S(2)}, u32[]{:S(2)}) collective-permute-start(bf16[64,512]{1,0:T(8,128)(2,1)S(1)} %key_value_rows.3), channel_id=1, source_target_pairs={{0,2},{1,3},{2,0},{3,1},{4,6},{5,7},{6,4},{7,5},{8,10},{9,11},{10,... | collective-permute-start | bytes 196616 | tf_op jit(solution)/shard_map/ppermute | solution.py:361
  22.7 1.6 %collective-permute-start.7 = (bf16[4,64,512]{2,1,0:T(8,128)(2,1)S(1)}, bf16[4,64,512]{2,1,0:T(8,128)(2,1)S(1)}, u32[]{:S(2)}, u32[]{:S(2)}) collective-permute-start(bf16[4,64,512]{2,1,0:T(8,128)(2,1)S(1)} %pad_maximum_fusion.2.refs_6_.refs_5_.refs_0_), channel_id=1, source_target_pairs={{0,1},{1,0},{2,3},{3,2},{4,5},{5,4},{6,7},{7,6},{8,9},{9,8},{10,11... | collective-permute-start | bytes 786440 | tf_op jit(solution)/shard_map/ppermute | solution.py:365
  22.8 16.8 %collective-permute-start.2 = (bf16[32,4096]{1,0:T(8,128)(2,1)S(1)}, bf16[32,4096]{1,0:T(8,128)(2,1)S(1)}, u32[]{:S(2)}, u32[]{:S(2)}) collective-permute-start(bf16[32,4096]{1,0:T(8,128)(2,1)S(1)} %slice.8), channel_id=1, source_target_pairs={{0,16},{8,24},{16,0},{24,8},{1,17},{9,25},{17,1},{25,9},{2,18},{10... | collective-permute-start | bytes 786440 | tf_op jit(solution)/shard_map/ppermute | solution.py:345
  25.1 8.3 %collective-permute-start.10 = (bf16[128,512]{1,0:T(8,128)(2,1)S(1)}, bf16[128,512]{1,0:T(8,128)(2,1)S(1)}, u32[]{:S(2)}, u32[]{:S(2)}) collective-permute-start(bf16[128,512]{1,0:T(8,128)(2,1)S(1)} %key_value_rows.4), channel_id=1, source_target_pairs={{0,6},{1,7},{2,4},{3,5},{4,2},{5,3},{6,0},{7,1},{8,14},{9,15},{10,... | collective-permute-start | bytes 393224 | tf_op jit(solution)/shard_map/ppermute | solution.py:361
  27.7 11.8 %collective-permute-start.9 = (bf16[128,512]{1,0:T(8,128)(2,1)S(1)}, bf16[128,512]{1,0:T(8,128)(2,1)S(1)}, u32[]{:S(2)}, u32[]{:S(2)}) collective-permute-start(bf16[128,512]{1,0:T(8,128)(2,1)S(1)} %key_value_rows.4), channel_id=1, source_target_pairs={{0,4},{1,5},{2,6},{3,7},{4,0},{5,1},{6,2},{7,3},{8,12},{9,13},{10,... | collective-permute-start | bytes 393224 | tf_op jit(solution)/shard_map/ppermute | solution.py:361
  27.7 11.8 %collective-permute-start.8 = (bf16[128,512]{1,0:T(8,128)(2,1)S(1)}, bf16[128,512]{1,0:T(8,128)(2,1)S(1)}, u32[]{:S(2)}, u32[]{:S(2)}) collective-permute-start(bf16[128,512]{1,0:T(8,128)(2,1)S(1)} %key_value_rows.4), channel_id=1, source_target_pairs={{0,2},{1,3},{2,0},{3,1},{4,6},{5,7},{6,4},{7,5},{8,10},{9,11},{10,... | collective-permute-start | bytes 393224 | tf_op jit(solution)/shard_map/ppermute | solution.py:361
  29.6 10.1 %collective-permute-start.3 = (bf16[32,4096]{1,0:T(8,128)(2,1)S(1)}, bf16[32,4096]{1,0:T(8,128)(2,1)S(1)}, u32[]{:S(2)}, u32[]{:S(2)}) collective-permute-start(bf16[32,4096]{1,0:T(8,128)(2,1)S(1)} %slice.9), channel_id=1, source_target_pairs={{0,8},{8,0},{16,24},{24,16},{1,9},{9,1},{17,25},{25,17},{2,10},{10... | collective-permute-start | bytes 786440 | tf_op jit(solution)/shard_map/ppermute | solution.py:342
  39.5 13.9 %collective-permute-start.11 = (bf16[4,128,512]{2,1,0:T(8,128)(2,1)S(1)}, bf16[4,128,512]{2,1,0:T(8,128)(2,1)S(1)}, u32[]{:S(2)}, u32[]{:S(2)}) collective-permute-start(bf16[4,128,512]{2,1,0:T(8,128)(2,1)S(1)} %pad_maximum_fusion.refs_2_), channel_id=1, source_target_pairs={{0,1},{1,0},{2,3},{3,2},{4,5},{5,4},{6,7},{7,6},{8,9},{9,8},{10,11... | collective-permute-start | bytes 1572872 | tf_op jit(solution)/shard_map/ppermute | solution.py:365
  40.6 6.8 %collective-permute-start.14 = (bf16[64,512]{1,0:T(8,128)(2,1)S(1)}, bf16[64,512]{1,0:T(8,128)(2,1)S(1)}, u32[]{:S(2)}, u32[]{:S(2)}) collective-permute-start(bf16[64,512]{1,0:T(8,128)(2,1)S(1)} %key_value_rows.5), channel_id=1, source_target_pairs={{0,6},{1,7},{2,4},{3,5},{4,2},{5,3},{6,0},{7,1},{8,14},{9,15},{10,... | collective-permute-start | bytes 196616 | tf_op jit(solution)/shard_map/ppermute | solution.py:361
  43.2 6.6 %collective-permute-start.13 = (bf16[64,512]{1,0:T(8,128)(2,1)S(1)}, bf16[64,512]{1,0:T(8,128)(2,1)S(1)}, u32[]{:S(2)}, u32[]{:S(2)}) collective-permute-start(bf16[64,512]{1,0:T(8,128)(2,1)S(1)} %key_value_rows.5), channel_id=1, source_target_pairs={{0,4},{1,5},{2,6},{3,7},{4,0},{5,1},{6,2},{7,3},{8,12},{9,13},{10,... | collective-permute-start | bytes 196616 | tf_op jit(solution)/shard_map/ppermute | solution.py:361
  43.2 6.6 %collective-permute-start.12 = (bf16[64,512]{1,0:T(8,128)(2,1)S(1)}, bf16[64,512]{1,0:T(8,128)(2,1)S(1)}, u32[]{:S(2)}, u32[]{:S(2)}) collective-permute-start(bf16[64,512]{1,0:T(8,128)(2,1)S(1)} %key_value_rows.5), channel_id=1, source_target_pairs={{0,2},{1,3},{2,0},{3,1},{4,6},{5,7},{6,4},{7,5},{8,10},{9,11},{10,... | collective-permute-start | bytes 196616 | tf_op jit(solution)/shard_map/ppermute | solution.py:361
  49.8 3.6 %collective-permute-start.15 = (bf16[4,64,512]{2,1,0:T(8,128)(2,1)S(1)}, bf16[4,64,512]{2,1,0:T(8,128)(2,1)S(1)}, u32[]{:S(2)}, u32[]{:S(2)}) collective-permute-start(bf16[4,64,512]{2,1,0:T(8,128)(2,1)S(1)} %pad_maximum_fusion.3.refs_4_), channel_id=1, source_target_pairs={{0,1},{1,0},{2,3},{3,2},{4,5},{5,4},{6,7},{7,6},{8,9},{9,8},{10,11... | collective-permute-start | bytes 786440 | tf_op jit(solution)/shard_map/ppermute | solution.py:365
  53.4 0.7 copy-start.1
  59.1 19.3 %collective-permute-start.17 = (bf16[64,2048]{1,0:T(8,128)(2,1)S(1)}, bf16[64,2048]{1,0:T(8,128)(2,1)S(1)}, u32[]{:S(2)}, u32[]{:S(2)}) collective-permute-start(bf16[64,2048]{1,0:T(8,128)(2,1)S(1)} %get-tuple-element.24), channel_id=1, source_target_pairs={{0,8},{8,0},{16,24},{24,16},{1,9},{9,1},{17,25},{25,17},{2,10},{10... | collective-permute-start | bytes 786440 | tf_op jit(solution)/shard_map/ppermute | solution.py:342
  59.7 19.4 %collective-permute-start.20 = (bf16[64,2048]{1,0:T(8,128)(2,1)S(1)}, bf16[64,2048]{1,0:T(8,128)(2,1)S(1)}, u32[]{:S(2)}, u32[]{:S(2)}) collective-permute-start(bf16[64,2048]{1,0:T(8,128)(2,1)S(1)} %get-tuple-element.28), channel_id=1, source_target_pairs={{0,16},{8,24},{16,0},{24,8},{1,17},{9,25},{17,1},{25,9},{2,18},{10... | collective-permute-start | bytes 786440 | tf_op jit(solution)/shard_map/ppermute | solution.py:345
  70.4 9.4 %collective-permute-start.16 = (bf16[64,2048]{1,0:T(8,128)(2,1)S(1)}, bf16[64,2048]{1,0:T(8,128)(2,1)S(1)}, u32[]{:S(2)}, u32[]{:S(2)}) collective-permute-start(bf16[64,2048]{1,0:T(8,128)(2,1)S(1)} %get-tuple-element.22), channel_id=1, source_target_pairs={{0,8},{8,0},{16,24},{24,16},{1,9},{9,1},{17,25},{25,17},{2,10},{10... | collective-permute-start | bytes 786440 | tf_op jit(solution)/shard_map/ppermute | solution.py:342
  71.9 13.1 %collective-permute-start.19 = (bf16[64,2048]{1,0:T(8,128)(2,1)S(1)}, bf16[64,2048]{1,0:T(8,128)(2,1)S(1)}, u32[]{:S(2)}, u32[]{:S(2)}) collective-permute-start(bf16[64,2048]{1,0:T(8,128)(2,1)S(1)} %get-tuple-element.26), channel_id=1, source_target_pairs={{0,16},{8,24},{16,0},{24,8},{1,17},{9,25},{17,1},{25,9},{2,18},{10... | collective-permute-start | bytes 786440 | tf_op jit(solution)/shard_map/ppermute | solution.py:345
  78.5 6.4 %collective-permute-start.18 = (bf16[64,2048]{1,0:T(8,128)(2,1)S(1)}, bf16[64,2048]{1,0:T(8,128)(2,1)S(1)}, u32[]{:S(2)}, u32[]{:S(2)}) collective-permute-start(bf16[64,2048]{1,0:T(8,128)(2,1)S(1)} %add_convert_fusion.3), channel_id=1, source_target_pairs={{0,16},{8,24},{16,0},{24,8},{1,17},{9,25},{17,1},{25,9},{2,18},{10... | collective-permute-start | bytes 786440 | tf_op jit(solution)/shard_map/ppermute | solution.py:345
  79.1 6.4 %collective-permute-start.21 = (bf16[64,2048]{1,0:T(8,128)(2,1)S(1)}, bf16[64,2048]{1,0:T(8,128)(2,1)S(1)}, u32[]{:S(2)}, u32[]{:S(2)}) collective-permute-start(bf16[64,2048]{1,0:T(8,128)(2,1)S(1)} %add_convert_fusion.1), channel_id=1, source_target_pairs={{0,8},{8,0},{16,24},{24,16},{1,9},{9,1},{17,25},{25,17},{2,10},{10... | collective-permute-start | bytes 786440 | tf_op jit(solution)/shard_map/ppermute | solution.py:342

commit v3 on v2

v3 whole, which is shorter than its diff:
```python
import functools
import math

import jax
import jax.numpy as jnp
from jax import lax
from jax.experimental import pallas as pl
from jax.experimental.pallas import tpu as pltpu
from jax.sharding import PartitionSpec as P

HEAD_WIDTH = 128
MASK_BLOCK_TOKENS = 128
ROPE_BASE = 500000.0
NEG_FILL = -1e30
WIDE = 8
QUERY_FACTOR = HEAD_WIDTH**-0.5 * math.log2(math.e)
ANY = pl.BlockSpec(memory_space=pl.ANY)
VMEM = pl.BlockSpec(memory_space=pltpu.VMEM)
SMEM = pl.BlockSpec(memory_space=pltpu.SMEM)
MIB = 1 << 20


def params(mib):
    return pltpu.CompilerParams(vmem_limit_bytes=mib * MIB)


def turn(product, cosine, sine):
    return product * cosine + pltpu.roll(product, HEAD_WIDTH // 2, 1) * sine


def preload_kernel(count, *refs):
    sources, targets, sems = refs[:count], refs[-1 - count : -1], refs[-1]
    copies = [
        pltpu.make_async_copy(source, target, sems.at[at])
        for at, (source, target) in enumerate(zip(sources, targets))
    ]
    for copy in copies:
        copy.start()
    for copy in copies:
        copy.wait()


def preload(weights, after):
    return pl.pallas_call(
        functools.partial(preload_kernel, len(weights)),
        out_shape=[pltpu.VMEM(weight.shape, weight.dtype) for weight in weights],
        in_specs=[ANY] * (len(weights) + len(after)),
        out_specs=[VMEM] * len(weights),
        scratch_shapes=[pltpu.SemaphoreType.DMA((len(weights),))],
        compiler_params=params(1),
        name="preload",
    )(*[pltpu.with_memory_space_constraint(weight, pltpu.HBM) for weight in weights], *after)


def kept(weight):
    return pltpu.with_memory_space_constraint(weight, pltpu.VMEM)


def group_of(slot, core):
    return {0: 0, 1: 1 + core, 2: 2 - core, 3: 3}[slot]


def chip_of(at, chips):
    shift, step, place = 0, chips // 2, 1
    while step:
        shift = shift ^ ((at // place % 2) * (2 * step - 1))
        step, place = step // 2, place * 2
    return shift


def table_rows(ref, slots, piece_rows):
    if slots is None:
        return ref[...]
    grp, core = lax.axis_index("grp"), lax.axis_index("blk") % 2
    rows = []
    for slot in slots:
        at = lax.bitwise_xor(grp, group_of(slot, core)) * piece_rows
        rows.append(ref[pl.ds(pl.multiple_of(at, piece_rows), piece_rows)])
    return jnp.concatenate(rows, axis=0)


def key_value_kernel(count, slots, *refs):
    pieces, (key_ref, value_ref, cos_ref, sin_ref, *_, out_ref) = refs[:count], refs[count:]
    width = key_ref.shape[1]
    rows = jnp.concatenate([piece[...] for piece in pieces], axis=0)
    keys = jnp.dot(rows, key_ref[...], preferred_element_type=jnp.float32)
    values = jnp.dot(rows, value_ref[...], preferred_element_type=jnp.float32)
    cosine = table_rows(cos_ref, slots, pieces[0].shape[0])
    sine = table_rows(sin_ref, slots, pieces[0].shape[0])
    for at in range(0, width, HEAD_WIDTH):
        head = slice(at, at + HEAD_WIDTH)
        out_ref[:, head] = turn(keys[:, head], cosine, sine).astype(out_ref.dtype)
    out_ref[:, width:] = values.astype(out_ref.dtype)


def key_value_rows(
    pieces, key_weight, value_weight, cosine, sine, slots=None, after=(), weigh=1
):
    rows = sum(piece.shape[0] for piece in pieces)
    width = key_weight.shape[1] + value_weight.shape[1]
    return pl.pallas_call(
        functools.partial(key_value_kernel, len(pieces), slots),
        out_shape=jax.ShapeDtypeStruct((rows, width), jnp.bfloat16),
        in_specs=[VMEM] * (len(pieces) + 4) + [ANY] * len(after),
        out_specs=VMEM,
        compiler_params=params(16),
        cost_estimate=pl.CostEstimate(
            flops=2 * rows * (key_weight.size + value_weight.size) * weigh,
            bytes_accessed=2 * (key_weight.size + value_weight.size),
            transcendentals=0,
        ),
        name="key_value_rows",
    )(*pieces, key_weight, value_weight, cosine, sine, *after)


def query_kernel(slots, *refs):
    count = len(refs) - 4
    pieces, (weight_ref, cos_ref, sin_ref, out_ref) = refs[:count], refs[count:]
    step = 2 * HEAD_WIDTH
    rows = jnp.concatenate([piece[...] for piece in pieces], axis=0)

    @pl.loop(0, weight_ref.shape[1] // step)
    def _(tile):
        at = pl.multiple_of(tile * step, step)
        product = jnp.dot(rows, weight_ref[:, pl.ds(at, step)], preferred_element_type=jnp.float32)
        cosine = table_rows(cos_ref, slots, pieces[0].shape[0]) * QUERY_FACTOR
        sine = table_rows(sin_ref, slots, pieces[0].shape[0]) * QUERY_FACTOR
        for half in range(2):
            head = turn(product[:, half * HEAD_WIDTH : (half + 1) * HEAD_WIDTH], cosine, sine)
            out_ref[:, pl.ds(at + half * HEAD_WIDTH, HEAD_WIDTH)] = head.astype(out_ref.dtype)


def query_rows(pieces, weight, cosine, sine, slots=None):
    rows = sum(piece.shape[0] for piece in pieces)
    return pl.pallas_call(
        functools.partial(query_kernel, slots),
        out_shape=jax.ShapeDtypeStruct((rows, weight.shape[1]), jnp.bfloat16),
        in_specs=[VMEM] * (len(pieces) + 3),
        out_specs=VMEM,
        compiler_params=params(18),
        cost_estimate=pl.CostEstimate(
            flops=2 * rows * weight.size, bytes_accessed=2 * weight.size, transcendentals=0
        ),
        name="query_rows",
    )(*pieces, weight, cosine, sine)


def attend_kernel(slots, groups, placed, mask_ref, query_ref, kv_ref, weight_ref, *rest):
    out_refs, (live_ref, mixed_ref) = rest[: len(slots)], rest[len(slots) :]
    grp, core = lax.axis_index("grp"), lax.axis_index("blk") % 2
    piece_rows = query_ref.shape[0] // groups
    kv_heads = kv_ref.shape[1] // (2 * HEAD_WIDTH)
    repeat = query_ref.shape[1] // (kv_heads * HEAD_WIDTH)
    block = MASK_BLOCK_TOKENS

    for at, slot in enumerate(slots):
        query_piece = lax.bitwise_xor(grp, group_of(slot, core)) if placed else slot
        query_block = query_piece * piece_rows // block

        def note(index, count, query_block=query_block):
            live_ref[count] = index
            return count + mask_ref[query_block, index]

        count = lax.fori_loop(0, mask_ref.shape[1], note, jnp.int32(0))
        for spare in range(WIDE):
            live_ref[count + spare] = 0

        for head in range(kv_heads):
            query = jnp.concatenate(
                [
                    query_ref[
                        slot * piece_rows : (slot + 1) * piece_rows,
                        (head * repeat + q) * HEAD_WIDTH : (head * repeat + q + 1) * HEAD_WIDTH,
                    ]
                    for q in range(repeat)
                ],
                axis=0,
            )

            def step(index, state, head=head, query=query, count=count):
                top_old, total_old, mix_old = state
                first = index * WIDE
                starts = [
                    pl.multiple_of(live_ref[first + wide] * block, block) for wide in range(WIDE)
                ]
                key_cols = pl.ds(head * HEAD_WIDTH, HEAD_WIDTH)
                value_cols = pl.ds((kv_heads + head) * HEAD_WIDTH, HEAD_WIDTH)
                scores = []
                for wide, start in enumerate(starts):
                    tile = lax.dot_general(
                        query,
                        kv_ref[pl.ds(start, block), key_cols],
                        (((1,), (1,)), ((), ())),
                        preferred_element_type=jnp.float32,
                    )
                    if wide:
                        tile = tile + jnp.where(first + wide < count, 0.0, NEG_FILL)
                    scores.append(tile)
                scores = jnp.concatenate(scores, axis=1)
                top = jnp.maximum(top_old, jnp.max(scores, axis=1, keepdims=True))
                weights = jnp.exp2(scores - top)
                factor = jnp.exp2(top_old - top)
                total = total_old * factor + jnp.sum(weights, axis=1, keepdims=True)
                values = jnp.concatenate(
                    [kv_ref[pl.ds(start, block), value_cols] for start in starts], axis=0
                )
                product = jnp.dot(
                    weights.astype(jnp.bfloat16), values, preferred_element_type=jnp.float32
                )
                return top, total, mix_old * factor + product

            rows = repeat * piece_rows
            _, total, mix = lax.fori_loop(
                0,
                (count + WIDE - 1) // WIDE,
                step,
                (
                    jnp.full((rows, 1), NEG_FILL, jnp.float32),
                    jnp.zeros((rows, 1), jnp.float32),
                    jnp.zeros((rows, HEAD_WIDTH), jnp.float32),
                ),
            )
            mixed = (mix / total).astype(jnp.bfloat16)
            for q in range(repeat):
                mixed_ref[
                    at * piece_rows : (at + 1) * piece_rows,
                    (head * repeat + q) * HEAD_WIDTH : (head * repeat + q + 1) * HEAD_WIDTH,
                ] = mixed[q * piece_rows : (q + 1) * piece_rows]

    tile_cols = 512

    @pl.loop(0, weight_ref.shape[1] // tile_cols)
    def _(tile):
        here = pl.ds(pl.multiple_of(tile * tile_cols, tile_cols), tile_cols)
        term = jnp.dot(
            mixed_ref[...], weight_ref[:, here], preferred_element_type=jnp.float32
        ).astype(jnp.bfloat16)
        for at in range(len(slots)):
            out_refs[at][:, here] = term[at * piece_rows : (at + 1) * piece_rows]


def gather_kernel(chunks, *refs):
    parts, out_ref = refs[:-1], refs[-1]
    grp, blk = lax.axis_index("grp"), lax.axis_index("blk")

    def place(owner, group, rows):
        at = (owner * 4 + group) * rows.shape[0]
        out_ref[pl.ds(pl.multiple_of(at, rows.shape[0]), rows.shape[0])] = rows

    at = 0
    for slots in chunks:
        shifts = parts[at].shape[0]
        piece_rows = parts[at].shape[1] // len(slots)
        for other in range(2):
            core = lax.bitwise_xor(blk % 2, other)
            for shift in range(shifts):
                owner = lax.bitwise_xor(blk // 2, chip_of(shift, shifts)) * 2 + core
                for index, slot in enumerate(slots):
                    group = lax.bitwise_xor(grp, group_of(slot, core))
                    rows = slice(index * piece_rows, (index + 1) * piece_rows)
                    place(owner, group, parts[at + other][shift, rows])
        at += 2


def gather_rows(chunks, parts, rows):
    return pl.pallas_call(
        functools.partial(gather_kernel, chunks),
        out_shape=jax.ShapeDtypeStruct((rows, parts[0].shape[-1]), jnp.bfloat16),
        in_specs=[VMEM] * len(parts),
        out_specs=VMEM,
        compiler_params=params(12),
        name="key_value_gather",
    )(*parts)


def attend(slots, groups, placed, mask, query, kv, weight):
    piece_rows = query.shape[0] // groups
    term = jax.ShapeDtypeStruct((piece_rows, weight.shape[1]), jnp.bfloat16)
    return pl.pallas_call(
        functools.partial(attend_kernel, slots, groups, placed),
        out_shape=[term] * len(slots),
        in_specs=[SMEM, VMEM, VMEM, VMEM],
        out_specs=[VMEM] * len(slots),
        scratch_shapes=[
            pltpu.SMEM((mask.shape[1] + 2 * WIDE,), jnp.int32),
            pltpu.VMEM((len(slots) * piece_rows, weight.shape[0]), jnp.bfloat16),
        ],
        compiler_params=params(20 if placed else 48),
        cost_estimate=pl.CostEstimate(
            flops=2 * len(slots) * piece_rows * weight.size * 2,
            bytes_accessed=2 * weight.size,
            transcendentals=0,
        ),
        name="attend_project",
    )(mask, query, kv, weight)


def rotary_tables(positions):
    half = HEAD_WIDTH // 2
    inverse = jnp.power(
        jnp.float32(ROPE_BASE),
        -(2.0 * (jnp.arange(HEAD_WIDTH) % half).astype(jnp.float32)) / HEAD_WIDTH,
    )
    sign = jnp.where(jnp.arange(HEAD_WIDTH) < half, -1.0, 1.0)
    angles = positions.astype(jnp.float32)[:, None] * inverse[None, :]
    return jnp.cos(angles), jnp.sin(angles) * sign[None, :]


def add(*values):
    total = values[0].astype(jnp.float32)
    for value in values[1:]:
        total = total + value.astype(jnp.float32)
    return total.astype(jnp.bfloat16)


def general_body(
    blk_count, groups, tokens, w_query, key_weight, value_weight, w_output, block_mask, positions
):
    rows = lax.all_gather(tokens, "grp", axis=0, tiled=True)
    cosine, sine = rotary_tables(positions)
    own = key_value_rows((rows,), key_weight, value_weight, cosine, sine)
    kv = lax.all_gather(own, "blk", axis=0, tiled=True)
    query = query_rows((rows,), w_query, cosine, sine)
    order = tuple(range(groups))
    terms = attend(order, groups, False, block_mask, query, kv, w_output)
    term = jnp.concatenate(terms, axis=0)
    return lax.psum_scatter(term, "grp", scatter_dimension=0, tiled=True)


def square_body(
    blk_count, tokens, w_query, key_weight, value_weight, w_output, block_mask, positions
):
    chips = blk_count // 2

    def send(value, slot):
        pairs = []
        for g in range(4):
            for b in range(blk_count):
                pairs.append((g * blk_count + b, (g ^ group_of(slot, b % 2)) * blk_count + b))
        return lax.ppermute(value, ("grp", "blk"), pairs)

    first, second = send(tokens, 1), send(tokens, 2)
    across = send(first, 2)

    cosine, sine = rotary_tables(positions)
    key_weight, value_weight = preload((key_weight, value_weight), (cosine, sine))

    def exchange(slots, after=(), weigh=1, beside=None, direct=False):
        own = key_value_rows(
            [pieces[slot] for slot in slots],
            kept(key_weight),
            kept(value_weight),
            cosine,
            sine,
            slots,
            after,
            weigh,
        )
        held = own[None]
        if direct:
            sent = [
                lax.ppermute(own, "blk", [(b, b ^ (2 * chip_of(at, chips))) for b in range(blk_count)])
                for at in range(1, chips)
            ]
            held = jnp.stack([own, *sent])
        step = 0 if direct else chips // 2
        while step:
            mask = 4 * step - 2
            pairs = [(b, b ^ mask) for b in range(blk_count)]
            held = jnp.concatenate([held, lax.ppermute(held, "blk", pairs)], axis=0)
            step //= 2
        if beside is not None:
            held, beside = lax.optimization_barrier((held, beside))
        both = [held, lax.ppermute(held, "blk", [(b, b ^ 1) for b in range(blk_count)])]
        return own, both, beside

    pieces = (tokens, first, second, across)
    rows_0, parts_0, _ = exchange((0,), direct=True)
    rows_1, parts_1, _ = exchange((1,), (rows_0,), direct=True)
    query = query_rows(pieces, w_query, cosine, sine, tuple(range(4)))
    _, parts_2, query = exchange((2, 3), (*parts_0, *parts_1), beside=query, direct=True)
    chunks = ((0,), (1,), (2, 3))
    parts = parts_0 + parts_1 + parts_2
    kv = gather_rows(chunks, parts, blk_count * positions.shape[0])

    def terms(slots):
        return attend(slots, 4, True, block_mask, query, kv, w_output)

    (term_across,) = terms((3,))
    sent_across = send(term_across, 2)
    term_first, term_second = terms((1, 2))
    sent_second = send(term_second, 2)
    sent_first = send(add(term_first, sent_across), 1)
    (term_own,) = terms((0,))
    return add(term_own, sent_second, sent_first)


def solution(mesh):
    groups, blk_count = mesh.shape["grp"], mesh.shape["blk"]
    if groups == 4 and blk_count & (blk_count - 1) == 0:
        body = functools.partial(square_body, blk_count)
    else:
        body = functools.partial(general_body, blk_count, groups)
    return jax.shard_map(
        body,
        mesh=mesh,
        in_specs=(
            P(("blk", "grp"), None),
            P(None, "grp"),
            P(None, "grp"),
            P(None, "grp"),
            P("grp", None),
            P("blk", None),
            P("blk"),
        ),
        out_specs=P(("blk", "grp"), None),
        check_vma=False,
    )
```

time: 86.7 us -> 70.6 us (0.81)
  waiting for transfers between devices: 25.1 us -> 17.5 us
  Pallas kernels: 33.3 us -> 27.7 us
  starting transfers between devices: 24.8 us -> 22.4 us
    ppermute x22 -> x18, waiting for transfers between devices: 25.1 us -> 17.5 us  [the longest x9 9.83 us: exchange(): lax.ppermute(own, 'blk', [(b, b ^ 2 * chip_of(at, chips)) for b in range(...]
    pallas_call x1, Pallas kernels: 7.13 us -> 2.3 us  [preload(): pl.pallas_call(functools.partial(preload_kernel, len(weights)), out_shape...]
    ppermute x22 -> x18, starting transfers between devices: 24.8 us -> 22.4 us  [the longest x9 13.6 us: exchange(): lax.ppermute(own, 'blk', [(b, b ^ 2 * chip_of(at, chips)) for b in range(...]
  transfers between devices with their start and end apart: 22 -> 18, of which waited for: 9 -> 8; matrix products, arithmetic and copies ran while one was open for 2% -> 2% of each run, Pallas kernels for 33% -> 31%
where the time goes in v3:
time: 70.6 us; the launch traced here: 70.4 us
  Pallas kernels  27.7 us (39%)
  starting transfers between devices  22.4 us (32%)
  waiting for transfers between devices  17.5 us (25%)
  other arithmetic  2.49 us (4%)
    pallas_call x3, Pallas kernels, attend(): pl.pallas_call(functools.partial(attend_kernel, slots, groups, placed), o...  19.1 us
    ppermute x9, starting transfers between devices, exchange(): lax.ppermute(own, 'blk', [(b, b ^ 2 * chip_of(at, chips)) for b in range(...  13.6 us
    ppermute x9, waiting for transfers between devices, exchange(): lax.ppermute(own, 'blk', [(b, b ^ 2 * chip_of(at, chips)) for b in range(...  9.83 us
    ppermute x6, starting transfers between devices, send(): return lax.ppermute(value, ('grp', 'blk'), pairs)  8.69 us
    ppermute x6, waiting for transfers between devices, send(): return lax.ppermute(value, ('grp', 'blk'), pairs)  4.29 us
    pallas_call x1, Pallas kernels, query_rows(): pl.pallas_call(functools.partial(query_kernel, slots), out_shape=jax.Shap...  3.5 us
    ppermute x3, waiting for transfers between devices, exchange(): lax.ppermute(held, 'blk', [(b, b ^ 1) for b in range(blk_count)])  3.4 us
    pallas_call x3, Pallas kernels, key_value_rows(): pl.pallas_call(functools.partial(key_value_kernel, len(pieces), slots), o...  2.6 us
  transfers between devices with their start and end apart: 18, of which 8 were waited for; matrix products, arithmetic and copies ran while one was open for 2% of the time, Pallas kernels for 31%

profile of v3, /device:TPU:0, one launch (start us, length us, event | category | flops | bytes accessed | tf_op | source)
XLA Modules:
  0.0 70.4 jit_solution(845650246149788252)
XLA Ops:
  0.0 2.9 %collective-permute-start.1 = (bf16[64,4096]{1,0:T(8,128)(2,1)}, bf16[64,4096]{1,0:T(8,128)(2,1)S(1)}, u32[]{:S(2)}, u32[]{:S(2)}) collective-permute-start(bf16[64,4096]{1,0:T(8,128)(2,1)} %refs_0_.5), channel_id=1, source_target_pairs={{0,8},{1,17},{2,10},{3,19},{4,12},{5,21},{6,14},{7,23},{8,0},{9,25... | collective-permute-start | bytes 1572872 | tf_op jit(solution)/shard_map/ppermute | solution.py:340
  2.9 0.7 convert_element_type.31
  3.6 0.5 fusion
  4.2 2.3 %preload.1 = (bf16[4096,256]{1,0:T(8,128)(2,1)S(1)}, bf16[4096,256]{1,0:T(8,128)(2,1)S(1)}) custom-call(bf16[4096,256]{1,0:T(8,128)(2,1)} %refs_0_.3, bf16[4096,256]{1,0:T(8,128)(2,1)} %refs_1_.1, f32[256,128]{1,0:T(8,128)S(1)} %get-tuple-element.18.refs_2_.refs_3_.refs_4_.refs_5_, f32[256,128]{1,0:T(8,128)S(1)} %get-tuple-element.17.refs_3_.refs_4_.refs_5_.refs_6_), custom_call_target="tpu_custom_call" | custom-call | tf_op jit(solution)/shard_map/preload/pallas_call | solution.py:44
  6.5 0.9 %key_value_rows.3.refs_5_ = bf16[64,512]{1,0:T(8,128)(2,1)S(1)} custom-call(bf16[64,4096]{1,0:T(8,128)(2,1)S(1)} %copy-done, bf16[4096,256]{1,0:T(8,128)(2,1)S(1)} %get-tuple-element.11.refs_1_.refs_2_, bf16[4096,256]{1,0:T(8,128)(2,1)S(1)} %get-tuple-element.12.refs_2_.refs_3_, f32[256,128]{1,0:T(8,128)S(1)} %get-tuple-element.18.refs_2_.refs_3_.refs_4_.refs_5_, ...), custom_call_target="tpu_custom_call" | custom-call | flops 268435456 | bytes 4194304 | tf_op jit(solution)/shard_map/key_value_rows/pallas_call | solution.py:101
  7.4 2.7 %collective-permute-start.5 = (bf16[64,512]{1,0:T(8,128)(2,1)S(1)}, bf16[64,512]{1,0:T(8,128)(2,1)S(1)}, u32[]{:S(2)}, u32[]{:S(2)}) collective-permute-start(bf16[64,512]{1,0:T(8,128)(2,1)S(1)} %key_value_rows.3.refs_5_), channel_id=1, source_target_pairs={{0,4},{1,5},{2,6},{3,7},{4,0},{5,1},{6,2},{7,3},{8,12},{9,13},{10,... | collective-permute-start | bytes 196616 | tf_op jit(solution)/shard_map/ppermute | solution.py:362
  10.1 1.6 %collective-permute-start.4 = (bf16[64,512]{1,0:T(8,128)(2,1)S(1)}, bf16[64,512]{1,0:T(8,128)(2,1)S(1)}, u32[]{:S(2)}, u32[]{:S(2)}) collective-permute-start(bf16[64,512]{1,0:T(8,128)(2,1)S(1)} %key_value_rows.3.refs_5_), channel_id=1, source_target_pairs={{0,2},{1,3},{2,0},{3,1},{4,6},{5,7},{6,4},{7,5},{8,10},{9,11},{10,... | collective-permute-start | bytes 196616 | tf_op jit(solution)/shard_map/ppermute | solution.py:362
  11.7 0.2 collective-permute-start.3
  11.9 1.5 %collective-permute-start = (bf16[64,4096]{1,0:T(8,128)(2,1)S(1)}, bf16[64,4096]{1,0:T(8,128)(2,1)S(1)}, u32[]{:S(2)}, u32[]{:S(2)}) collective-permute-start(bf16[64,4096]{1,0:T(8,128)(2,1)S(1)} %copy-done), channel_id=1, source_target_pairs={{0,16},{1,9},{2,18},{3,11},{4,20},{5,13},{6,22},{7,15},{8,24},{9,1... | collective-permute-start | bytes 1572872 | tf_op jit(solution)/shard_map/ppermute | solution.py:340
  13.4 0.5 collective-permute-start.2
  13.9 0.9 %key_value_rows.4 = bf16[64,512]{1,0:T(8,128)(2,1)S(1)} custom-call(bf16[64,4096]{1,0:T(8,128)(2,1)S(1)} %collective-permute-done.1.refs_0_.refs_1_, bf16[4096,256]{1,0:T(8,128)(2,1)S(1)} %get-tuple-element.11.refs_1_.refs_2_, bf16[4096,256]{1,0:T(8,128)(2,1)S(1)} %get-tuple-element.12.refs_2_.refs_3_, ...), custom_call_target="tpu_custom_call" | custom-call | flops 268435456 | bytes 4194304 | tf_op jit(solution)/shard_map/key_value_rows/pallas_call | solution.py:101
  14.9 1.8 %collective-permute-start.9 = (bf16[64,512]{1,0:T(8,128)(2,1)S(1)}, bf16[64,512]{1,0:T(8,128)(2,1)S(1)}, u32[]{:S(2)}, u32[]{:S(2)}) collective-permute-start(bf16[64,512]{1,0:T(8,128)(2,1)S(1)} %key_value_rows.4), channel_id=1, source_target_pairs={{0,4},{1,5},{2,6},{3,7},{4,0},{5,1},{6,2},{7,3},{8,12},{9,13},{10,... | collective-permute-start | bytes 196616 | tf_op jit(solution)/shard_map/ppermute | solution.py:362
  16.6 2.9 %collective-permute-start.8 = (bf16[64,512]{1,0:T(8,128)(2,1)S(1)}, bf16[64,512]{1,0:T(8,128)(2,1)S(1)}, u32[]{:S(2)}, u32[]{:S(2)}) collective-permute-start(bf16[64,512]{1,0:T(8,128)(2,1)S(1)} %key_value_rows.4), channel_id=1, source_target_pairs={{0,2},{1,3},{2,0},{3,1},{4,6},{5,7},{6,4},{7,5},{8,10},{9,11},{10,... | collective-permute-start | bytes 196616 | tf_op jit(solution)/shard_map/ppermute | solution.py:362
  19.6 0.9 %collective-permute-done.9 = bf16[64,512]{1,0:T(8,128)(2,1)S(1)} collective-permute-done((bf16[64,512]{1,0:T(8,128)(2,1)S(1)}, bf16[64,512]{1,0:T(8,128)(2,1)S(1)}, u32[]{:S(2)}, u32[]{:S(2)}) %collective-permute-start.9) | collective-permute-done | bytes 65568 | tf_op jit(solution)/shard_map/ppermute | solution.py:362
  20.5 2.0 %collective-permute-done.8 = bf16[64,512]{1,0:T(8,128)(2,1)S(1)} collective-permute-done((bf16[64,512]{1,0:T(8,128)(2,1)S(1)}, bf16[64,512]{1,0:T(8,128)(2,1)S(1)}, u32[]{:S(2)}, u32[]{:S(2)}) %collective-permute-start.8) | collective-permute-done | bytes 65568 | tf_op jit(solution)/shard_map/ppermute | solution.py:362
  22.5 3.1 %collective-permute-done.7 = bf16[64,512]{1,0:T(8,128)(2,1)S(1)} collective-permute-done((bf16[64,512]{1,0:T(8,128)(2,1)S(1)}, bf16[64,512]{1,0:T(8,128)(2,1)S(1)}, u32[]{:S(2)}, u32[]{:S(2)}) %collective-permute-start.7) | collective-permute-done | bytes 65568 | tf_op jit(solution)/shard_map/ppermute | solution.py:362
  25.8 1.5 %collective-permute-done.10.refs_9_.refs_3_ = bf16[4,64,512]{2,1,0:T(8,128)(2,1)S(1)} collective-permute-done((bf16[4,64,512]{2,1,0:T(8,128)(2,1)S(1)}, bf16[4,64,512]{2,1,0:T(8,128)(2,1)S(1)}, u32[]{:S(2)}, u32[]{:S(2)}) %collective-permute-start.10) | collective-permute-done | bytes 262176 | tf_op jit(solution)/shard_map/ppermute | solution.py:374
  27.3 0.8 %key_value_rows.5 = bf16[128,512]{1,0:T(8,128)(2,1)S(1)} custom-call(bf16[64,4096]{1,0:T(8,128)(2,1)S(1)} %collective-permute-done.refs_0_.refs_2_, bf16[64,4096]{1,0:T(8,128)(2,1)S(1)} %collective-permute-done.2.refs_1_.refs_3_, bf16[4096,256]{1,0:T(8,128)(2,1)S(1)} %get-tuple-element.11.refs_1_.refs_2_, ...), custom_call_target="tpu_custom_call" | custom-call | flops 536870912 | bytes 4194304 | tf_op jit(solution)/shard_map/key_value_rows/pallas_call | solution.py:101
  28.1 1.2 %collective-permute-start.13 = (bf16[128,512]{1,0:T(8,128)(2,1)S(1)}, bf16[128,512]{1,0:T(8,128)(2,1)S(1)}, u32[]{:S(2)}, u32[]{:S(2)}) collective-permute-start(bf16[128,512]{1,0:T(8,128)(2,1)S(1)} %key_value_rows.5), channel_id=1, source_target_pairs={{0,4},{1,5},{2,6},{3,7},{4,0},{5,1},{6,2},{7,3},{8,12},{9,13},{10,... | collective-permute-start | bytes 393224 | tf_op jit(solution)/shard_map/ppermute | solution.py:362
  29.3 2.5 %collective-permute-start.12 = (bf16[128,512]{1,0:T(8,128)(2,1)S(1)}, bf16[128,512]{1,0:T(8,128)(2,1)S(1)}, u32[]{:S(2)}, u32[]{:S(2)}) collective-permute-start(bf16[128,512]{1,0:T(8,128)(2,1)S(1)} %key_value_rows.5), channel_id=1, source_target_pairs={{0,2},{1,3},{2,0},{3,1},{4,6},{5,7},{6,4},{7,5},{8,10},{9,11},{10,... | collective-permute-start | bytes 393224 | tf_op jit(solution)/shard_map/ppermute | solution.py:362
  31.7 0.8 %collective-permute-start.11 = (bf16[128,512]{1,0:T(8,128)(2,1)S(1)}, bf16[128,512]{1,0:T(8,128)(2,1)S(1)}, u32[]{:S(2)}, u32[]{:S(2)}) collective-permute-start(bf16[128,512]{1,0:T(8,128)(2,1)S(1)} %key_value_rows.5), channel_id=1, source_target_pairs={{0,6},{1,7},{2,4},{3,5},{4,2},{5,3},{6,0},{7,1},{8,14},{9,15},{10,... | collective-permute-start | bytes 393224 | tf_op jit(solution)/shard_map/ppermute | solution.py:362
  32.5 3.5 %query_rows.1.query_ref = bf16[256,1024]{1,0:T(8,128)(2,1)S(1)} custom-call(bf16[64,4096]{1,0:T(8,128)(2,1)S(1)} %copy-done, bf16[64,4096]{1,0:T(8,128)(2,1)S(1)} %collective-permute-done.1.refs_0_.refs_1_, bf16[64,4096]{1,0:T(8,128)(2,1)S(1)} %collective-permute-done.refs_0_.refs_2_, bf16[64,4096]{1,0:T(8,128)(2,1)S(1)} %collective-permute-done.2.refs_1_.refs_3_, ...), custom_call_target="tpu_custom_call" | custom-call | flops 2147483648 | bytes 8388608 | tf_op jit(solution)/shard_map/query_rows/pallas_call | solution.py:135
  36.0 1.8 %collective-permute-done.13 = bf16[128,512]{1,0:T(8,128)(2,1)S(1)} collective-permute-done((bf16[128,512]{1,0:T(8,128)(2,1)S(1)}, bf16[128,512]{1,0:T(8,128)(2,1)S(1)}, u32[]{:S(2)}, u32[]{:S(2)}) %collective-permute-start.13) | collective-permute-done | bytes 131104 | tf_op jit(solution)/shard_map/ppermute | solution.py:362
  37.8 2.0 %collective-permute-done.11 = bf16[128,512]{1,0:T(8,128)(2,1)S(1)} collective-permute-done((bf16[128,512]{1,0:T(8,128)(2,1)S(1)}, bf16[128,512]{1,0:T(8,128)(2,1)S(1)}, u32[]{:S(2)}, u32[]{:S(2)}) %collective-permute-start.11) | collective-permute-done | bytes 131104 | tf_op jit(solution)/shard_map/ppermute | solution.py:362
  40.0 1.9 %collective-permute-done.14.refs_5_ = bf16[4,128,512]{2,1,0:T(8,128)(2,1)S(1)} collective-permute-done((bf16[4,128,512]{2,1,0:T(8,128)(2,1)S(1)}, bf16[4,128,512]{2,1,0:T(8,128)(2,1)S(1)}, u32[]{:S(2)}, u32[]{:S(2)}) %collective-permute-start.14) | collective-permute-done | bytes 524320 | tf_op jit(solution)/shard_map/ppermute | solution.py:374
  42.2 4.7 %attend_project.5 = bf16[64,4096]{1,0:T(8,128)(2,1)S(1)} custom-call(s32[2,16]{1,0:T(2,128)S(1)} %copy-done.1, bf16[256,1024]{1,0:T(8,128)(2,1)S(1)} %query_rows.1.query_ref, bf16[2048,512]{1,0:T(8,128)(2,1)S(1)} %key_value_gather.1.kv_ref, bf16[1024,4096]{1,0:T(8,128)(2,1)S(1)} %bitcast.13), custom_call_target="tpu_custom_call" | custom-call | flops 1073741824 | bytes 8388608 | tf_op jit(solution)/shard_map/attend_project/pallas_call | solution.py:279
  46.9 2.8 %collective-permute-start.16 = (bf16[64,4096]{1,0:T(8,128)(2,1)S(1)}, bf16[64,4096]{1,0:T(8,128)(2,1)S(1)}, u32[]{:S(2)}, u32[]{:S(2)}) collective-permute-start(bf16[64,4096]{1,0:T(8,128)(2,1)S(1)} %attend_project.5), channel_id=1, source_target_pairs={{0,16},{1,9},{2,18},{3,11},{4,20},{5,13},{6,22},{7,15},{8,24},{9,1... | collective-permute-start | bytes 1572872 | tf_op jit(solution)/shard_map/ppermute | solution.py:340
  49.7 8.1 %attend_project.4 = (bf16[64,4096]{1,0:T(8,128)(2,1)S(1)}, bf16[64,4096]{1,0:T(8,128)(2,1)S(1)}) custom-call(s32[2,16]{1,0:T(2,128)S(1)} %copy-done.1, bf16[256,1024]{1,0:T(8,128)(2,1)S(1)} %query_rows.1.query_ref, bf16[2048,512]{1,0:T(8,128)(2,1)S(1)} %key_value_gather.1.kv_ref, bf16[1024,4096]{1,0:T(8,128)(2,1)S(1)} %bitcast.13), custom_call_target="tpu_custom_call" | custom-call | flops 2147483648 | bytes 8388608 | tf_op jit(solution)/shard_map/attend_project/pallas_call | solution.py:279
  58.1 0.8 %collective-permute-start.17 = (bf16[64,4096]{1,0:T(8,128)(2,1)S(1)}, bf16[64,4096]{1,0:T(8,128)(2,1)S(1)}, u32[]{:S(2)}, u32[]{:S(2)}) collective-permute-start(bf16[64,4096]{1,0:T(8,128)(2,1)S(1)} %add_convert_fusion.1), channel_id=1, source_target_pairs={{0,8},{1,17},{2,10},{3,19},{4,12},{5,21},{6,14},{7,23},{8,0},{9,25... | collective-permute-start | bytes 1572872 | tf_op jit(solution)/shard_map/ppermute | solution.py:340
  58.9 6.2 %attend_project.3 = bf16[64,4096]{1,0:T(8,128)(2,1)S(1)} custom-call(s32[2,16]{1,0:T(2,128)S(1)} %copy-done.1, bf16[256,1024]{1,0:T(8,128)(2,1)S(1)} %query_rows.1.query_ref, bf16[2048,512]{1,0:T(8,128)(2,1)S(1)} %key_value_gather.1.kv_ref, bf16[1024,4096]{1,0:T(8,128)(2,1)S(1)} %bitcast.13), custom_call_target="tpu_custom_call" | custom-call | flops 1073741824 | bytes 8388608 | tf_op jit(solution)/shard_map/attend_project/pallas_call | solution.py:279
  65.1 4.3 %collective-permute-done.15 = bf16[64,4096]{1,0:T(8,128)(2,1)S(1)} collective-permute-done((bf16[64,4096]{1,0:T(8,128)(2,1)S(1)}, bf16[64,4096]{1,0:T(8,128)(2,1)S(1)}, u32[]{:S(2)}, u32[]{:S(2)}) %collective-permute-start.15) | collective-permute-done | bytes 524320 | tf_op jit(solution)/shard_map/ppermute | solution.py:340
  69.4 1.0 %add_convert_fusion = bf16[64,4096]{1,0:T(8,128)(2,1)} fusion(bf16[64,4096]{1,0:T(8,128)(2,1)S(1)} %collective-permute-done.17, bf16[64,4096]{1,0:T(8,128)(2,1)S(1)} %collective-permute-done.15, bf16[64,4096]{1,0:T(8,128)(2,1)S(1)} %attend_project.3), kind=kLoop, calls=%fused_computation | loop fusion | flops 1572864 | bytes 2097152 | tf_op jit(solution)/shard_map/convert_element_type | solution.py:313
  (35 shorter events, 0.8 us)
Async XLA Ops:
  0.0 13.4 %collective-permute-start.1 = (bf16[64,4096]{1,0:T(8,128)(2,1)}, bf16[64,4096]{1,0:T(8,128)(2,1)S(1)}, u32[]{:S(2)}, u32[]{:S(2)}) collective-permute-start(bf16[64,4096]{1,0:T(8,128)(2,1)} %refs_0_.5), channel_id=1, source_target_pairs={{0,8},{1,17},{2,10},{3,19},{4,12},{5,21},{6,14},{7,23},{8,0},{9,25... | collective-permute-start | bytes 1572872 | tf_op jit(solution)/shard_map/ppermute | solution.py:340
  4.2 2.3 %copy-start = (bf16[64,4096]{1,0:T(8,128)(2,1)S(1)}, bf16[64,4096]{1,0:T(8,128)(2,1)}, u32[]{:S(2)}) copy-start(bf16[64,4096]{1,0:T(8,128)(2,1)} %refs_0_.5) | copy-start | bytes 1572868
  6.5 26.0 %slice-start.2 = ((s8[8388608]{0:T(1024)(128)(4,1)}), s8[4194304]{0:T(1024)(128)(4,1)S(1)}, s32[]{:S(2)}) async-start(s8[8388608]{0:T(1024)(128)(4,1)} %bitcast.14), calls=%async_computation.2 | async-start | bytes 8388608
  7.4 25.1 %slice-start.3 = ((s8[8388608]{0:T(1024)(128)(4,1)}), s8[4194304]{0:T(1024)(128)(4,1)S(1)}, s32[]{:S(2)}) async-start(s8[8388608]{0:T(1024)(128)(4,1)} %bitcast.14), calls=%async_computation.3 | async-start | bytes 8388608
  7.4 7.4 %collective-permute-start.5 = (bf16[64,512]{1,0:T(8,128)(2,1)S(1)}, bf16[64,512]{1,0:T(8,128)(2,1)S(1)}, u32[]{:S(2)}, u32[]{:S(2)}) collective-permute-start(bf16[64,512]{1,0:T(8,128)(2,1)S(1)} %key_value_rows.3.refs_5_), channel_id=1, source_target_pairs={{0,4},{1,5},{2,6},{3,7},{4,0},{5,1},{6,2},{7,3},{8,12},{9,13},{10,... | collective-permute-start | bytes 196616 | tf_op jit(solution)/shard_map/ppermute | solution.py:362
  10.1 6.5 %collective-permute-start.4 = (bf16[64,512]{1,0:T(8,128)(2,1)S(1)}, bf16[64,512]{1,0:T(8,128)(2,1)S(1)}, u32[]{:S(2)}, u32[]{:S(2)}) collective-permute-start(bf16[64,512]{1,0:T(8,128)(2,1)S(1)} %key_value_rows.3.refs_5_), channel_id=1, source_target_pairs={{0,2},{1,3},{2,0},{3,1},{4,6},{5,7},{6,4},{7,5},{8,10},{9,11},{10,... | collective-permute-start | bytes 196616 | tf_op jit(solution)/shard_map/ppermute | solution.py:362
  11.7 7.9 %collective-permute-start.3 = (bf16[64,512]{1,0:T(8,128)(2,1)S(1)}, bf16[64,512]{1,0:T(8,128)(2,1)S(1)}, u32[]{:S(2)}, u32[]{:S(2)}) collective-permute-start(bf16[64,512]{1,0:T(8,128)(2,1)S(1)} %key_value_rows.3.refs_5_), channel_id=1, source_target_pairs={{0,6},{1,7},{2,4},{3,5},{4,2},{5,3},{6,0},{7,1},{8,14},{9,15},{10,... | collective-permute-start | bytes 196616 | tf_op jit(solution)/shard_map/ppermute | solution.py:362
  11.9 13.9 %collective-permute-start = (bf16[64,4096]{1,0:T(8,128)(2,1)S(1)}, bf16[64,4096]{1,0:T(8,128)(2,1)S(1)}, u32[]{:S(2)}, u32[]{:S(2)}) collective-permute-start(bf16[64,4096]{1,0:T(8,128)(2,1)S(1)} %copy-done), channel_id=1, source_target_pairs={{0,16},{1,9},{2,18},{3,11},{4,20},{5,13},{6,22},{7,15},{8,24},{9,1... | collective-permute-start | bytes 1572872 | tf_op jit(solution)/shard_map/ppermute | solution.py:340
  13.4 13.8 %collective-permute-start.2 = (bf16[64,4096]{1,0:T(8,128)(2,1)S(1)}, bf16[64,4096]{1,0:T(8,128)(2,1)S(1)}, u32[]{:S(2)}, u32[]{:S(2)}) collective-permute-start(bf16[64,4096]{1,0:T(8,128)(2,1)S(1)} %collective-permute-done.1.refs_0_.refs_1_), channel_id=1, source_target_pairs={{0,16},{1,9},{2,18},{3,11},{4,20},{5,13},{6,22},{7,15},{8,24},{9,1... | collective-permute-start | bytes 1572872 | tf_op jit(solution)/shard_map/ppermute | solution.py:340
  14.9 5.6 %collective-permute-start.9 = (bf16[64,512]{1,0:T(8,128)(2,1)S(1)}, bf16[64,512]{1,0:T(8,128)(2,1)S(1)}, u32[]{:S(2)}, u32[]{:S(2)}) collective-permute-start(bf16[64,512]{1,0:T(8,128)(2,1)S(1)} %key_value_rows.4), channel_id=1, source_target_pairs={{0,4},{1,5},{2,6},{3,7},{4,0},{5,1},{6,2},{7,3},{8,12},{9,13},{10,... | collective-permute-start | bytes 196616 | tf_op jit(solution)/shard_map/ppermute | solution.py:362
  16.6 5.9 %collective-permute-start.8 = (bf16[64,512]{1,0:T(8,128)(2,1)S(1)}, bf16[64,512]{1,0:T(8,128)(2,1)S(1)}, u32[]{:S(2)}, u32[]{:S(2)}) collective-permute-start(bf16[64,512]{1,0:T(8,128)(2,1)S(1)} %key_value_rows.4), channel_id=1, source_target_pairs={{0,2},{1,3},{2,0},{3,1},{4,6},{5,7},{6,4},{7,5},{8,10},{9,11},{10,... | collective-permute-start | bytes 196616 | tf_op jit(solution)/shard_map/ppermute | solution.py:362
  19.6 6.1 %collective-permute-start.7 = (bf16[64,512]{1,0:T(8,128)(2,1)S(1)}, bf16[64,512]{1,0:T(8,128)(2,1)S(1)}, u32[]{:S(2)}, u32[]{:S(2)}) collective-permute-start(bf16[64,512]{1,0:T(8,128)(2,1)S(1)} %key_value_rows.4), channel_id=1, source_target_pairs={{0,6},{1,7},{2,4},{3,5},{4,2},{5,3},{6,0},{7,1},{8,14},{9,15},{10,... | collective-permute-start | bytes 196616 | tf_op jit(solution)/shard_map/ppermute | solution.py:362
  20.5 5.2 %collective-permute-start.6 = (bf16[4,64,512]{2,1,0:T(8,128)(2,1)S(1)}, bf16[4,64,512]{2,1,0:T(8,128)(2,1)S(1)}, u32[]{:S(2)}, u32[]{:S(2)}) collective-permute-start(bf16[4,64,512]{2,1,0:T(8,128)(2,1)S(1)} %pad_maximum_fusion.1.refs_6_.refs_0_), channel_id=1, source_target_pairs={{0,1},{1,0},{2,3},{3,2},{4,5},{5,4},{6,7},{7,6},{8,9},{9,8},{10,11... | collective-permute-start | bytes 786440 | tf_op jit(solution)/shard_map/ppermute | solution.py:374
  25.7 1.6 %collective-permute-start.10 = (bf16[4,64,512]{2,1,0:T(8,128)(2,1)S(1)}, bf16[4,64,512]{2,1,0:T(8,128)(2,1)S(1)}, u32[]{:S(2)}, u32[]{:S(2)}) collective-permute-start(bf16[4,64,512]{2,1,0:T(8,128)(2,1)S(1)} %pad_maximum_fusion.2.refs_8_.refs_2_), channel_id=1, source_target_pairs={{0,1},{1,0},{2,3},{3,2},{4,5},{5,4},{6,7},{7,6},{8,9},{9,8},{10,11... | collective-permute-start | bytes 786440 | tf_op jit(solution)/shard_map/ppermute | solution.py:374
  27.3 14.8 %slice-start = ((s8[8388608]{0:T(1024)(128)(4,1)}), s8[4194304]{0:T(1024)(128)(4,1)S(1)}, s32[]{:S(2)}) async-start(s8[8388608]{0:T(1024)(128)(4,1)} %bitcast.12), calls=%async_computation | async-start | bytes 8388608
  28.1 14.1 %slice-start.1 = ((s8[8388608]{0:T(1024)(128)(4,1)}), s8[4194304]{0:T(1024)(128)(4,1)S(1)}, s32[]{:S(2)}) async-start(s8[8388608]{0:T(1024)(128)(4,1)} %bitcast.12), calls=%async_computation.1 | async-start | bytes 8388608
  28.1 9.7 %collective-permute-start.13 = (bf16[128,512]{1,0:T(8,128)(2,1)S(1)}, bf16[128,512]{1,0:T(8,128)(2,1)S(1)}, u32[]{:S(2)}, u32[]{:S(2)}) collective-permute-start(bf16[128,512]{1,0:T(8,128)(2,1)S(1)} %key_value_rows.5), channel_id=1, source_target_pairs={{0,4},{1,5},{2,6},{3,7},{4,0},{5,1},{6,2},{7,3},{8,12},{9,13},{10,... | collective-permute-start | bytes 393224 | tf_op jit(solution)/shard_map/ppermute | solution.py:362
  29.3 8.6 %collective-permute-start.12 = (bf16[128,512]{1,0:T(8,128)(2,1)S(1)}, bf16[128,512]{1,0:T(8,128)(2,1)S(1)}, u32[]{:S(2)}, u32[]{:S(2)}) collective-permute-start(bf16[128,512]{1,0:T(8,128)(2,1)S(1)} %key_value_rows.5), channel_id=1, source_target_pairs={{0,2},{1,3},{2,0},{3,1},{4,6},{5,7},{6,4},{7,5},{8,10},{9,11},{10,... | collective-permute-start | bytes 393224 | tf_op jit(solution)/shard_map/ppermute | solution.py:362
  31.7 8.1 %collective-permute-start.11 = (bf16[128,512]{1,0:T(8,128)(2,1)S(1)}, bf16[128,512]{1,0:T(8,128)(2,1)S(1)}, u32[]{:S(2)}, u32[]{:S(2)}) collective-permute-start(bf16[128,512]{1,0:T(8,128)(2,1)S(1)} %key_value_rows.5), channel_id=1, source_target_pairs={{0,6},{1,7},{2,4},{3,5},{4,2},{5,3},{6,0},{7,1},{8,14},{9,15},{10,... | collective-permute-start | bytes 393224 | tf_op jit(solution)/shard_map/ppermute | solution.py:362
  39.9 2.2 %copy-start.1 = (s32[2,16]{1,0:T(2,128)S(1)}, s32[2,16]{1,0:T(2,128)}, u32[]{:S(2)}) copy-start(s32[2,16]{1,0:T(2,128)} %mask_ref.5) | copy-start | bytes 388
  39.9 2.0 %collective-permute-start.14 = (bf16[4,128,512]{2,1,0:T(8,128)(2,1)S(1)}, bf16[4,128,512]{2,1,0:T(8,128)(2,1)S(1)}, u32[]{:S(2)}, u32[]{:S(2)}) collective-permute-start(bf16[4,128,512]{2,1,0:T(8,128)(2,1)S(1)} %pad_maximum_fusion.refs_4_), channel_id=1, source_target_pairs={{0,1},{1,0},{2,3},{3,2},{4,5},{5,4},{6,7},{7,6},{8,9},{9,8},{10,11... | collective-permute-start | bytes 1572872 | tf_op jit(solution)/shard_map/ppermute | solution.py:374
  46.9 11.0 %collective-permute-start.16 = (bf16[64,4096]{1,0:T(8,128)(2,1)S(1)}, bf16[64,4096]{1,0:T(8,128)(2,1)S(1)}, u32[]{:S(2)}, u32[]{:S(2)}) collective-permute-start(bf16[64,4096]{1,0:T(8,128)(2,1)S(1)} %attend_project.5), channel_id=1, source_target_pairs={{0,16},{1,9},{2,18},{3,11},{4,20},{5,13},{6,22},{7,15},{8,24},{9,1... | collective-permute-start | bytes 1572872 | tf_op jit(solution)/shard_map/ppermute | solution.py:340
  57.8 11.6 %collective-permute-start.15 = (bf16[64,4096]{1,0:T(8,128)(2,1)S(1)}, bf16[64,4096]{1,0:T(8,128)(2,1)S(1)}, u32[]{:S(2)}, u32[]{:S(2)}) collective-permute-start(bf16[64,4096]{1,0:T(8,128)(2,1)S(1)} %get-tuple-element.15), channel_id=1, source_target_pairs={{0,16},{1,9},{2,18},{3,11},{4,20},{5,13},{6,22},{7,15},{8,24},{9,1... | collective-permute-start | bytes 1572872 | tf_op jit(solution)/shard_map/ppermute | solution.py:340
  58.1 11.4 %collective-permute-start.17 = (bf16[64,4096]{1,0:T(8,128)(2,1)S(1)}, bf16[64,4096]{1,0:T(8,128)(2,1)S(1)}, u32[]{:S(2)}, u32[]{:S(2)}) collective-permute-start(bf16[64,4096]{1,0:T(8,128)(2,1)S(1)} %add_convert_fusion.1), channel_id=1, source_target_pairs={{0,8},{1,17},{2,10},{3,19},{4,12},{5,21},{6,14},{7,23},{8,0},{9,25... | collective-permute-start | bytes 1572872 | tf_op jit(solution)/shard_map/ppermute | solution.py:340

commit v4 on v3

--- a/solution.py
+++ b/solution.py
@@ -12,7 +12,9 @@
 MASK_BLOCK_TOKENS = 128
 ROPE_BASE = 500000.0
 NEG_FILL = -1e30
+QUERY_COLS = 1024
 WIDE = 8
+SURE = 6
 QUERY_FACTOR = HEAD_WIDTH**-0.5 * math.log2(math.e)
 ANY = pl.BlockSpec(memory_space=pl.ANY)
 VMEM = pl.BlockSpec(memory_space=pltpu.VMEM)
@@ -116,18 +118,18 @@
 def query_kernel(slots, *refs):
     count = len(refs) - 4
     pieces, (weight_ref, cos_ref, sin_ref, out_ref) = refs[:count], refs[count:]
-    step = 2 * HEAD_WIDTH
     rows = jnp.concatenate([piece[...] for piece in pieces], axis=0)
+    cosine = table_rows(cos_ref, slots, pieces[0].shape[0]) * QUERY_FACTOR
+    sine = table_rows(sin_ref, slots, pieces[0].shape[0]) * QUERY_FACTOR
+    step = min(weight_ref.shape[1], QUERY_COLS)
 
     @pl.loop(0, weight_ref.shape[1] // step)
     def _(tile):
         at = pl.multiple_of(tile * step, step)
         product = jnp.dot(rows, weight_ref[:, pl.ds(at, step)], preferred_element_type=jnp.float32)
-        cosine = table_rows(cos_ref, slots, pieces[0].shape[0]) * QUERY_FACTOR
-        sine = table_rows(sin_ref, slots, pieces[0].shape[0]) * QUERY_FACTOR
-        for half in range(2):
-            head = turn(product[:, half * HEAD_WIDTH : (half + 1) * HEAD_WIDTH], cosine, sine)
-            out_ref[:, pl.ds(at + half * HEAD_WIDTH, HEAD_WIDTH)] = head.astype(out_ref.dtype)
+        for head in range(0, step, HEAD_WIDTH):
+            turned = turn(product[:, head : head + HEAD_WIDTH], cosine, sine)
+            out_ref[:, pl.ds(at + head, HEAD_WIDTH)] = turned.astype(out_ref.dtype)
 
 
 def query_rows(pieces, weight, cosine, sine, slots=None):
@@ -145,10 +147,10 @@
     )(*pieces, weight, cosine, sine)
 
 
-def attend_kernel(slots, groups, placed, mask_ref, query_ref, kv_ref, weight_ref, *rest):
+def attend_kernel(slots, held, placed, mask_ref, query_ref, kv_ref, weight_ref, *rest):
     out_refs, (live_ref, mixed_ref) = rest[: len(slots)], rest[len(slots) :]
     grp, core = lax.axis_index("grp"), lax.axis_index("blk") % 2
-    piece_rows = query_ref.shape[0] // groups
+    piece_rows = query_ref.shape[0] // len(held)
     kv_heads = kv_ref.shape[1] // (2 * HEAD_WIDTH)
     repeat = query_ref.shape[1] // (kv_heads * HEAD_WIDTH)
     block = MASK_BLOCK_TOKENS
@@ -161,73 +163,79 @@
             live_ref[count] = index
             return count + mask_ref[query_block, index]
 
-        count = lax.fori_loop(0, mask_ref.shape[1], note, jnp.int32(0))
+        count = lax.fori_loop(0, mask_ref.shape[1], note, jnp.int32(0), unroll=16)
         for spare in range(WIDE):
             live_ref[count + spare] = 0
 
-        for head in range(kv_heads):
-            query = jnp.concatenate(
+        queries = [
+            jnp.concatenate(
                 [
                     query_ref[
-                        slot * piece_rows : (slot + 1) * piece_rows,
+                        held.index(slot) * piece_rows : (held.index(slot) + 1) * piece_rows,
                         (head * repeat + q) * HEAD_WIDTH : (head * repeat + q + 1) * HEAD_WIDTH,
                     ]
                     for q in range(repeat)
                 ],
                 axis=0,
             )
-
-            def step(index, state, head=head, query=query, count=count):
-                top_old, total_old, mix_old = state
-                first = index * WIDE
-                starts = [
-                    pl.multiple_of(live_ref[first + wide] * block, block) for wide in range(WIDE)
-                ]
-                key_cols = pl.ds(head * HEAD_WIDTH, HEAD_WIDTH)
-                value_cols = pl.ds((kv_heads + head) * HEAD_WIDTH, HEAD_WIDTH)
-                scores = []
-                for wide, start in enumerate(starts):
-                    tile = lax.dot_general(
-                        query,
-                        kv_ref[pl.ds(start, block), key_cols],
-                        (((1,), (1,)), ((), ())),
-                        preferred_element_type=jnp.float32,
-                    )
-                    if wide:
-                        tile = tile + jnp.where(first + wide < count, 0.0, NEG_FILL)
-                    scores.append(tile)
-                scores = jnp.concatenate(scores, axis=1)
-                top = jnp.maximum(top_old, jnp.max(scores, axis=1, keepdims=True))
-                weights = jnp.exp2(scores - top)
-                factor = jnp.exp2(top_old - top)
-                total = total_old * factor + jnp.sum(weights, axis=1, keepdims=True)
+            for head in range(kv_heads)
+        ]
+        ones = jnp.ones((WIDE * block, HEAD_WIDTH), jnp.bfloat16)
+
+        def step(index, state, queries=queries, count=count):
+            first = index * WIDE
+            starts = [
+                pl.multiple_of(live_ref[first + wide] * block, block) for wide in range(WIDE)
+            ]
+            new_state = []
+            for head, query in enumerate(queries):
+                key_cols = slice(head * HEAD_WIDTH, (head + 1) * HEAD_WIDTH)
+                value_cols = slice(
+                    (kv_heads + head) * HEAD_WIDTH, (kv_heads + head + 1) * HEAD_WIDTH
+                )
+                keys = jnp.concatenate(
+                    [kv_ref[pl.ds(start, block), key_cols] for start in starts], axis=0
+                )
                 values = jnp.concatenate(
                     [kv_ref[pl.ds(start, block), value_cols] for start in starts], axis=0
                 )
-                product = jnp.dot(
-                    weights.astype(jnp.bfloat16), values, preferred_element_type=jnp.float32
-                )
-                return top, total, mix_old * factor + product
-
-            rows = repeat * piece_rows
-            _, total, mix = lax.fori_loop(
-                0,
-                (count + WIDE - 1) // WIDE,
-                step,
-                (
-                    jnp.full((rows, 1), NEG_FILL, jnp.float32),
-                    jnp.zeros((rows, 1), jnp.float32),
-                    jnp.zeros((rows, HEAD_WIDTH), jnp.float32),
-                ),
-            )
-            mixed = (mix / total).astype(jnp.bfloat16)
+                scores = lax.dot_general(
+                    query, keys, (((1,), (1,)), ((), ())), preferred_element_type=jnp.float32
+                )
+                scores = jnp.concatenate(
+                    [scores[:, : SURE * block]]
+                    + [
+                        scores[:, wide * block : (wide + 1) * block]
+                        + jnp.where(first + wide < count, 0.0, NEG_FILL)
+                        for wide in range(SURE, WIDE)
+                    ],
+                    axis=1,
+                )
+                top = jnp.max(scores, axis=1, keepdims=True)
+                if state is not None:
+                    top = jnp.maximum(state[2 * head], top)
+                weights = jnp.exp2(scores - top).astype(jnp.bfloat16)
+                sums = jnp.dot(
+                    weights,
+                    jnp.concatenate([values, ones], axis=1),
+                    preferred_element_type=jnp.float32,
+                )
+                if state is not None:
+                    sums = sums + state[2 * head + 1] * jnp.exp2(state[2 * head] - top)
+                new_state += [top, sums]
+            return tuple(new_state)
+
+        state = lax.fori_loop(1, (count + WIDE - 1) // WIDE, step, step(0, None))
+        for head in range(kv_heads):
+            sums = state[2 * head + 1]
+            mixed = (sums[:, :HEAD_WIDTH] / sums[:, HEAD_WIDTH:]).astype(jnp.bfloat16)
             for q in range(repeat):
                 mixed_ref[
                     at * piece_rows : (at + 1) * piece_rows,
                     (head * repeat + q) * HEAD_WIDTH : (head * repeat + q + 1) * HEAD_WIDTH,
                 ] = mixed[q * piece_rows : (q + 1) * piece_rows]
 
-    tile_cols = 512
+    tile_cols = weight_ref.shape[1] if mixed_ref.shape[0] <= 128 else 512
 
     @pl.loop(0, weight_ref.shape[1] // tile_cols)
     def _(tile):
@@ -273,11 +281,11 @@
     )(*parts)
 
 
-def attend(slots, groups, placed, mask, query, kv, weight):
-    piece_rows = query.shape[0] // groups
+def attend(slots, held, placed, mask, query, kv, weight):
+    piece_rows = query.shape[0] // len(held)
     term = jax.ShapeDtypeStruct((piece_rows, weight.shape[1]), jnp.bfloat16)
     return pl.pallas_call(
-        functools.partial(attend_kernel, slots, groups, placed),
+        functools.partial(attend_kernel, slots, held, placed),
         out_shape=[term] * len(slots),
         in_specs=[SMEM, VMEM, VMEM, VMEM],
         out_specs=[VMEM] * len(slots),
@@ -322,7 +330,7 @@
     kv = lax.all_gather(own, "blk", axis=0, tiled=True)
     query = query_rows((rows,), w_query, cosine, sine)
     order = tuple(range(groups))
-    terms = attend(order, groups, False, block_mask, query, kv, w_output)
+    terms = attend(order, order, False, block_mask, query, kv, w_output)
     term = jnp.concatenate(terms, axis=0)
     return lax.psum_scatter(term, "grp", scatter_dimension=0, tiled=True)
 
@@ -345,7 +353,7 @@
     cosine, sine = rotary_tables(positions)
     key_weight, value_weight = preload((key_weight, value_weight), (cosine, sine))
 
-    def exchange(slots, after=(), weigh=1, beside=None, direct=False):
+    def exchange(slots, after=(), direct=True):
         own = key_value_rows(
             [pieces[slot] for slot in slots],
             kept(key_weight),
@@ -354,37 +362,39 @@
             sine,
             slots,
             after,
-            weigh,
         )
-        held = own[None]
+        def across_chips(value, by):
+            return lax.ppermute(value, "blk", [(b, b ^ (2 * by)) for b in range(blk_count)])
+
+        near, far = across_chips(own, 1), across_chips(own, 3)
         if direct:
-            sent = [
-                lax.ppermute(own, "blk", [(b, b ^ (2 * chip_of(at, chips))) for b in range(blk_count)])
-                for at in range(1, chips)
-            ]
-            held = jnp.stack([own, *sent])
-        step = 0 if direct else chips // 2
-        while step:
-            mask = 4 * step - 2
-            pairs = [(b, b ^ mask) for b in range(blk_count)]
-            held = jnp.concatenate([held, lax.ppermute(held, "blk", pairs)], axis=0)
-            step //= 2
-        if beside is not None:
-            held, beside = lax.optimization_barrier((held, beside))
-        both = [held, lax.ppermute(held, "blk", [(b, b ^ 1) for b in range(blk_count)])]
-        return own, both, beside
+            last = across_chips(own, 2)
+        else:
+            near, far = lax.optimization_barrier((near, far))
+            last = across_chips(far, 1)
+        held = jnp.stack([own, far, near, last])
+        return own, held
+
+    def with_other_core(*held):
+        held = jnp.concatenate(held, axis=1)
+        return [held, lax.ppermute(held, "blk", [(b, b ^ 1) for b in range(blk_count)])]
 
     pieces = (tokens, first, second, across)
-    rows_0, parts_0, _ = exchange((0,), direct=True)
-    rows_1, parts_1, _ = exchange((1,), (rows_0,), direct=True)
-    query = query_rows(pieces, w_query, cosine, sine, tuple(range(4)))
-    _, parts_2, query = exchange((2, 3), (*parts_0, *parts_1), beside=query, direct=True)
-    chunks = ((0,), (1,), (2, 3))
-    parts = parts_0 + parts_1 + parts_2
+    rows_0, held_0 = exchange((0,), (), True)
+    parts_0 = with_other_core(held_0)
+    rows_1, held_1 = exchange((1, 2), parts_0, False)
+    query_1 = query_rows(pieces[:3], w_query, cosine, sine, (0, 1, 2))
+    rows_2, held_2 = exchange((3,), (rows_1, query_1), True)
+    query_2 = query_rows(pieces[3:], w_query, cosine, sine, (3,))
+    held_2, query_2 = lax.optimization_barrier((held_2, query_2))
+    query = {(0, 1, 2): query_1, (3,): query_2}
+    parts = parts_0 + with_other_core(held_1, held_2)
+    chunks = ((0,), (1, 2, 3))
     kv = gather_rows(chunks, parts, blk_count * positions.shape[0])
 
     def terms(slots):
-        return attend(slots, 4, True, block_mask, query, kv, w_output)
+        held = next(held for held in query if slots[0] in held)
+        return attend(slots, held, True, block_mask, query[held], kv, w_output)
 
     (term_across,) = terms((3,))
     sent_across = send(term_across, 2)
@@ -397,7 +407,7 @@
 
 def solution(mesh):
     groups, blk_count = mesh.shape["grp"], mesh.shape["blk"]
-    if groups == 4 and blk_count & (blk_count - 1) == 0:
+    if groups == 4 and blk_count == 8:
         body = functools.partial(square_body, blk_count)
     else:
         body = functools.partial(general_body, blk_count, groups)

time: 70.6 us -> 67.3 us (0.953)
  Pallas kernels: 27.7 us -> 22.5 us
  waiting for transfers between devices: 17.5 us -> 19.3 us
    ppermute x6, waiting for transfers between devices: 4.29 us -> 10.2 us  [send(): return lax.ppermute(value, ('grp', 'blk'), pairs)]
    pallas_call x3, Pallas kernels: 19.1 us -> 13.6 us  [attend(): pl.pallas_call(functools.partial(attend_kernel, slots, held, placed), out...]
    ppermute x12 -> x11, waiting for transfers between devices: 13.2 us -> 9.1 us  [the longest x9 5.31 us: across_chips(): lax.ppermute(value, 'blk', [(b, b ^ 2 * by) for b in range(blk_count)])]
    ppermute x6, starting transfers between devices: 8.69 us -> 9.64 us  [send(): return lax.ppermute(value, ('grp', 'blk'), pairs)]
    ppermute x12 -> x11, starting transfers between devices: 13.8 us -> 12.9 us  [the longest x9 12.7 us: across_chips(): lax.ppermute(value, 'blk', [(b, b ^ 2 * by) for b in range(blk_count)])]
    pallas_call x1 -> x2, Pallas kernels: 3.5 us -> 3.67 us  [query_rows(): pl.pallas_call(functools.partial(query_kernel, slots), out_shape=jax.Shap...]
  transfers between devices with their start and end apart: 18 -> 17, of which waited for: 8 -> 10; matrix products, arithmetic and copies ran while one was open for 2% -> 2% of each run, Pallas kernels for 31% -> 28%
where the time goes in v4:
time: 67.3 us; the launch traced here: 67.1 us
  starting transfers between devices  22.5 us (33%)
  Pallas kernels  22.5 us (33%)
  waiting for transfers between devices  19.3 us (29%)
  other arithmetic  2.47 us (4%)
    pallas_call x3, Pallas kernels, attend(): pl.pallas_call(functools.partial(attend_kernel, slots, held, placed), out...  13.6 us
    ppermute x9, starting transfers between devices, across_chips(): lax.ppermute(value, 'blk', [(b, b ^ 2 * by) for b in range(blk_count)])  12.7 us
    ppermute x6, waiting for transfers between devices, send(): return lax.ppermute(value, ('grp', 'blk'), pairs)  10.2 us
    ppermute x6, starting transfers between devices, send(): return lax.ppermute(value, ('grp', 'blk'), pairs)  9.64 us
    ppermute x9, waiting for transfers between devices, across_chips(): lax.ppermute(value, 'blk', [(b, b ^ 2 * by) for b in range(blk_count)])  5.31 us
    ppermute x2, waiting for transfers between devices, with_other_core(): lax.ppermute(held, 'blk', [(b, b ^ 1) for b in range(blk_count)])  3.79 us
    pallas_call x2, Pallas kernels, query_rows(): pl.pallas_call(functools.partial(query_kernel, slots), out_shape=jax.Shap...  3.67 us
    pallas_call x3, Pallas kernels, key_value_rows(): pl.pallas_call(functools.partial(key_value_kernel, len(pieces), slots), o...  2.65 us
  transfers between devices with their start and end apart: 17, of which 10 were waited for; matrix products, arithmetic and copies ran while one was open for 2% of the time, Pallas kernels for 28%

profile of v4, /device:TPU:0, one launch (start us, length us, event | category | flops | bytes accessed | tf_op | source)
XLA Modules:
  0.0 67.1 jit_solution(11829586866329893991)
XLA Ops:
  0.0 2.9 %collective-permute-start = (bf16[64,4096]{1,0:T(8,128)(2,1)}, bf16[64,4096]{1,0:T(8,128)(2,1)S(1)}, u32[]{:S(2)}, u32[]{:S(2)}) collective-permute-start(bf16[64,4096]{1,0:T(8,128)(2,1)} %refs_0_.5), channel_id=1, source_target_pairs={{0,8},{1,17},{2,10},{3,19},{4,12},{5,21},{6,14},{7,23},{8,0},{9,25... | collective-permute-start | bytes 1572872 | tf_op jit(solution)/shard_map/ppermute | solution.py:348
  2.9 1.5 %collective-permute-start.1 = (bf16[64,4096]{1,0:T(8,128)(2,1)}, bf16[64,4096]{1,0:T(8,128)(2,1)S(1)}, u32[]{:S(2)}, u32[]{:S(2)}) collective-permute-start(bf16[64,4096]{1,0:T(8,128)(2,1)} %refs_0_.5), channel_id=1, source_target_pairs={{0,16},{1,9},{2,18},{3,11},{4,20},{5,13},{6,22},{7,15},{8,24},{9,1... | collective-permute-start | bytes 1572872 | tf_op jit(solution)/shard_map/ppermute | solution.py:348
  4.5 0.7 %convert_element_type.31 = f32[256]{0:T(256)S(1)} convert(s32[256]{0:T(256)} %param.13) | non-fusion elementwise | flops 256 | bytes 2048 | tf_op jit(solution)/shard_map/convert_element_type | solution.py:313
  5.7 2.4 %preload.1 = (bf16[4096,256]{1,0:T(8,128)(2,1)S(1)}, bf16[4096,256]{1,0:T(8,128)(2,1)S(1)}) custom-call(bf16[4096,256]{1,0:T(8,128)(2,1)} %refs_0_.4, bf16[4096,256]{1,0:T(8,128)(2,1)} %refs_1_.2, f32[256,128]{1,0:T(8,128)S(1)} %get-tuple-element.22.refs_4_.refs_2_.refs_3_, f32[256,128]{1,0:T(8,128)S(1)} %get-tuple-element.21.refs_5_.refs_3_.refs_4_), custom_call_target="tpu_custom_call" | custom-call | tf_op jit(solution)/shard_map/preload/pallas_call | solution.py:46
  8.1 0.9 %key_value_rows.3 = bf16[64,512]{1,0:T(8,128)(2,1)S(1)} custom-call(bf16[64,4096]{1,0:T(8,128)(2,1)S(1)} %copy-done, bf16[4096,256]{1,0:T(8,128)(2,1)S(1)} %get-tuple-element.13.refs_1_.refs_2_, bf16[4096,256]{1,0:T(8,128)(2,1)S(1)} %get-tuple-element.14.refs_2_.refs_3_, f32[256,128]{1,0:T(8,128)S(1)} %get-tuple-element.22.refs_4_.refs_2_.refs_3_, ...), custom_call_target="tpu_custom_call" | custom-call | flops 268435456 | bytes 4194304 | tf_op jit(solution)/shard_map/key_value_rows/pallas_call | solution.py:103
  9.1 3.7 %collective-permute-start.2 = (bf16[64,512]{1,0:T(8,128)(2,1)S(1)}, bf16[64,512]{1,0:T(8,128)(2,1)S(1)}, u32[]{:S(2)}, u32[]{:S(2)}) collective-permute-start(bf16[64,512]{1,0:T(8,128)(2,1)S(1)} %key_value_rows.3), channel_id=1, source_target_pairs={{0,6},{1,7},{2,4},{3,5},{4,2},{5,3},{6,0},{7,1},{8,14},{9,15},{10,... | collective-permute-start | bytes 196616 | tf_op jit(solution)/shard_map/ppermute | solution.py:367
  12.7 0.8 %collective-permute-start.4 = (bf16[64,512]{1,0:T(8,128)(2,1)S(1)}, bf16[64,512]{1,0:T(8,128)(2,1)S(1)}, u32[]{:S(2)}, u32[]{:S(2)}) collective-permute-start(bf16[64,512]{1,0:T(8,128)(2,1)S(1)} %key_value_rows.3), channel_id=1, source_target_pairs={{0,4},{1,5},{2,6},{3,7},{4,0},{5,1},{6,2},{7,3},{8,12},{9,13},{10,... | collective-permute-start | bytes 196616 | tf_op jit(solution)/shard_map/ppermute | solution.py:367
  13.5 1.9 %collective-permute-done.refs_1_.refs_0_ = bf16[64,4096]{1,0:T(8,128)(2,1)S(1)} collective-permute-done((bf16[64,4096]{1,0:T(8,128)(2,1)}, bf16[64,4096]{1,0:T(8,128)(2,1)S(1)}, u32[]{:S(2)}, u32[]{:S(2)}) %collective-permute-start) | collective-permute-done | bytes 524320 | tf_op jit(solution)/shard_map/ppermute | solution.py:348
  15.5 1.4 %collective-permute-start.9 = (bf16[64,4096]{1,0:T(8,128)(2,1)S(1)}, bf16[64,4096]{1,0:T(8,128)(2,1)S(1)}, u32[]{:S(2)}, u32[]{:S(2)}) collective-permute-start(bf16[64,4096]{1,0:T(8,128)(2,1)S(1)} %collective-permute-done.refs_1_.refs_0_), channel_id=1, source_target_pairs={{0,16},{1,9},{2,18},{3,11},{4,20},{5,13},{6,22},{7,15},{8,24},{9,1... | collective-permute-start | bytes 1572872 | tf_op jit(solution)/shard_map/ppermute | solution.py:348
  17.1 0.8 %collective-permute-done.4 = bf16[64,512]{1,0:T(8,128)(2,1)S(1)} collective-permute-done((bf16[64,512]{1,0:T(8,128)(2,1)S(1)}, bf16[64,512]{1,0:T(8,128)(2,1)S(1)}, u32[]{:S(2)}, u32[]{:S(2)}) %collective-permute-start.4) | collective-permute-done | bytes 65568 | tf_op jit(solution)/shard_map/ppermute | solution.py:367
  18.0 1.5 %collective-permute-done.5.refs_7_.refs_1_ = bf16[4,64,512]{2,1,0:T(8,128)(2,1)S(1)} collective-permute-done((bf16[4,64,512]{2,1,0:T(8,128)(2,1)S(1)}, bf16[4,64,512]{2,1,0:T(8,128)(2,1)S(1)}, u32[]{:S(2)}, u32[]{:S(2)}) %collective-permute-start.5) | collective-permute-done | bytes 262176 | tf_op jit(solution)/shard_map/ppermute | solution.py:380
  19.5 0.8 %key_value_rows.4.refs_5_ = bf16[128,512]{1,0:T(8,128)(2,1)S(1)} custom-call(bf16[64,4096]{1,0:T(8,128)(2,1)S(1)} %collective-permute-done.refs_1_.refs_0_, bf16[64,4096]{1,0:T(8,128)(2,1)S(1)} %collective-permute-done.1.refs_2_.refs_1_, bf16[4096,256]{1,0:T(8,128)(2,1)S(1)} %get-tuple-element.13.refs_1_.refs_2_, ...), custom_call_target="tpu_custom_call" | custom-call | flops 536870912 | bytes 4194304 | tf_op jit(solution)/shard_map/key_value_rows/pallas_call | solution.py:103
  20.4 2.1 %collective-permute-start.6 = (bf16[128,512]{1,0:T(8,128)(2,1)S(1)}, bf16[128,512]{1,0:T(8,128)(2,1)S(1)}, u32[]{:S(2)}, u32[]{:S(2)}) collective-permute-start(bf16[128,512]{1,0:T(8,128)(2,1)S(1)} %key_value_rows.4.refs_5_), channel_id=1, source_target_pairs={{0,2},{1,3},{2,0},{3,1},{4,6},{5,7},{6,4},{7,5},{8,10},{9,11},{10,... | collective-permute-start | bytes 393224 | tf_op jit(solution)/shard_map/ppermute | solution.py:367
  22.4 1.4 %collective-permute-start.7 = (bf16[128,512]{1,0:T(8,128)(2,1)S(1)}, bf16[128,512]{1,0:T(8,128)(2,1)S(1)}, u32[]{:S(2)}, u32[]{:S(2)}) collective-permute-start(bf16[128,512]{1,0:T(8,128)(2,1)S(1)} %key_value_rows.4.refs_5_), channel_id=1, source_target_pairs={{0,6},{1,7},{2,4},{3,5},{4,2},{5,3},{6,0},{7,1},{8,14},{9,15},{10,... | collective-permute-start | bytes 393224 | tf_op jit(solution)/shard_map/ppermute | solution.py:367
  23.8 2.0 %query_rows.2.refs_6_.query_ref = bf16[192,1024]{1,0:T(8,128)(2,1)S(1)} custom-call(bf16[64,4096]{1,0:T(8,128)(2,1)S(1)} %copy-done, bf16[64,4096]{1,0:T(8,128)(2,1)S(1)} %collective-permute-done.refs_1_.refs_0_, bf16[64,4096]{1,0:T(8,128)(2,1)S(1)} %collective-permute-done.1.refs_2_.refs_1_, bf16[4096,1024]{1,0:T(8,128)(2,1)S(1)} %bitcast.15, ...), custom_call_target="tpu_custom_call" | custom-call | flops 1610612736 | bytes 8388608 | tf_op jit(solution)/shard_map/query_rows/pallas_call | solution.py:137
  25.9 0.9 %key_value_rows.5 = bf16[64,512]{1,0:T(8,128)(2,1)S(1)} custom-call(bf16[64,4096]{1,0:T(8,128)(2,1)S(1)} %collective-permute-done.9.refs_0_, bf16[4096,256]{1,0:T(8,128)(2,1)S(1)} %get-tuple-element.13.refs_1_.refs_2_, bf16[4096,256]{1,0:T(8,128)(2,1)S(1)} %get-tuple-element.14.refs_2_.refs_3_, f32[256,128]{1,0:T(8,128)S(1)} %get-tuple-element.22.refs_4_.refs_2_.refs_3_, ...), custom_call_target="tpu_custom_call" | custom-call | flops 268435456 | bytes 4194304 | tf_op jit(solution)/shard_map/key_value_rows/pallas_call | solution.py:103
  26.8 1.3 %collective-permute-start.11 = (bf16[64,512]{1,0:T(8,128)(2,1)S(1)}, bf16[64,512]{1,0:T(8,128)(2,1)S(1)}, u32[]{:S(2)}, u32[]{:S(2)}) collective-permute-start(bf16[64,512]{1,0:T(8,128)(2,1)S(1)} %key_value_rows.5), channel_id=1, source_target_pairs={{0,2},{1,3},{2,0},{3,1},{4,6},{5,7},{6,4},{7,5},{8,10},{9,11},{10,... | collective-permute-start | bytes 196616 | tf_op jit(solution)/shard_map/ppermute | solution.py:367
  28.1 2.6 %collective-permute-start.12 = (bf16[64,512]{1,0:T(8,128)(2,1)S(1)}, bf16[64,512]{1,0:T(8,128)(2,1)S(1)}, u32[]{:S(2)}, u32[]{:S(2)}) collective-permute-start(bf16[64,512]{1,0:T(8,128)(2,1)S(1)} %key_value_rows.5), channel_id=1, source_target_pairs={{0,4},{1,5},{2,6},{3,7},{4,0},{5,1},{6,2},{7,3},{8,12},{9,13},{10,... | collective-permute-start | bytes 196616 | tf_op jit(solution)/shard_map/ppermute | solution.py:367
  30.7 0.6 collective-permute-start.10
  31.6 1.7 %query_rows.3.query_ref = bf16[64,1024]{1,0:T(8,128)(2,1)S(1)} custom-call(bf16[64,4096]{1,0:T(8,128)(2,1)S(1)} %collective-permute-done.9.refs_0_, bf16[4096,1024]{1,0:T(8,128)(2,1)S(1)} %bitcast.15, f32[256,128]{1,0:T(8,128)S(1)} %get-tuple-element.22.refs_4_.refs_2_.refs_3_, f32[256,128]{1,0:T(8,128)S(1)} %get-tuple-element.21.refs_5_.refs_3_.refs_4_), custom_call_target="tpu_custom_call" | custom-call | flops 536870912 | bytes 8388608 | tf_op jit(solution)/shard_map/query_rows/pallas_call | solution.py:137
  33.3 1.6 %collective-permute-done.12 = bf16[64,512]{1,0:T(8,128)(2,1)S(1)} collective-permute-done((bf16[64,512]{1,0:T(8,128)(2,1)S(1)}, bf16[64,512]{1,0:T(8,128)(2,1)S(1)}, u32[]{:S(2)}, u32[]{:S(2)}) %collective-permute-start.12) | collective-permute-done | bytes 65568 | tf_op jit(solution)/shard_map/ppermute | solution.py:367
  34.9 2.0 %collective-permute-done.10 = bf16[64,512]{1,0:T(8,128)(2,1)S(1)} collective-permute-done((bf16[64,512]{1,0:T(8,128)(2,1)S(1)}, bf16[64,512]{1,0:T(8,128)(2,1)S(1)}, u32[]{:S(2)}, u32[]{:S(2)}) %collective-permute-start.10) | collective-permute-done | bytes 65568 | tf_op jit(solution)/shard_map/ppermute | solution.py:367
  36.9 0.7 %collective-permute-done.8 = bf16[128,512]{1,0:T(8,128)(2,1)S(1)} collective-permute-done((bf16[128,512]{1,0:T(8,128)(2,1)S(1)}, bf16[128,512]{1,0:T(8,128)(2,1)S(1)}, u32[]{:S(2)}, u32[]{:S(2)}) %collective-permute-start.8) | collective-permute-done | bytes 131104 | tf_op jit(solution)/shard_map/ppermute | solution.py:367
  37.8 2.3 %collective-permute-done.13.refs_3_ = bf16[4,192,512]{2,1,0:T(8,128)(2,1)S(1)} collective-permute-done((bf16[4,192,512]{2,1,0:T(8,128)(2,1)S(1)}, bf16[4,192,512]{2,1,0:T(8,128)(2,1)S(1)}, u32[]{:S(2)}, u32[]{:S(2)}) %collective-permute-start.13) | collective-permute-done | bytes 786464 | tf_op jit(solution)/shard_map/ppermute | solution.py:380
  40.3 3.3 %attend_project.5 = bf16[64,4096]{1,0:T(8,128)(2,1)S(1)} custom-call(s32[2,16]{1,0:T(2,128)S(1)} %copy-done.1, bf16[64,1024]{1,0:T(8,128)(2,1)S(1)} %query_rows.3.query_ref, bf16[2048,512]{1,0:T(8,128)(2,1)S(1)} %key_value_gather.1.kv_ref, bf16[1024,4096]{1,0:T(8,128)(2,1)S(1)} %bitcast.13), custom_call_target="tpu_custom_call" | custom-call | flops 1073741824 | bytes 8388608 | tf_op jit(solution)/shard_map/attend_project/pallas_call | solution.py:287
  43.6 2.2 %collective-permute-start.15 = (bf16[64,4096]{1,0:T(8,128)(2,1)S(1)}, bf16[64,4096]{1,0:T(8,128)(2,1)S(1)}, u32[]{:S(2)}, u32[]{:S(2)}) collective-permute-start(bf16[64,4096]{1,0:T(8,128)(2,1)S(1)} %attend_project.5), channel_id=1, source_target_pairs={{0,16},{1,9},{2,18},{3,11},{4,20},{5,13},{6,22},{7,15},{8,24},{9,1... | collective-permute-start | bytes 1572872 | tf_op jit(solution)/shard_map/ppermute | solution.py:348
  45.8 5.7 %attend_project.4 = (bf16[64,4096]{1,0:T(8,128)(2,1)S(1)}, bf16[64,4096]{1,0:T(8,128)(2,1)S(1)}) custom-call(s32[2,16]{1,0:T(2,128)S(1)} %copy-done.1, bf16[192,1024]{1,0:T(8,128)(2,1)S(1)} %query_rows.2.refs_6_.query_ref, bf16[2048,512]{1,0:T(8,128)(2,1)S(1)} %key_value_gather.1.kv_ref, bf16[1024,4096]{1,0:T(8,128)(2,1)S(1)} %bitcast.13), custom_call_target="tpu_custom_call" | custom-call | flops 2147483648 | bytes 8388608 | tf_op jit(solution)/shard_map/attend_project/pallas_call | solution.py:287
  51.6 1.4 %collective-permute-done.15 = bf16[64,4096]{1,0:T(8,128)(2,1)S(1)} collective-permute-done((bf16[64,4096]{1,0:T(8,128)(2,1)S(1)}, bf16[64,4096]{1,0:T(8,128)(2,1)S(1)}, u32[]{:S(2)}, u32[]{:S(2)}) %collective-permute-start.15) | collective-permute-done | bytes 524320 | tf_op jit(solution)/shard_map/ppermute | solution.py:348
  53.1 1.5 %collective-permute-start.16 = (bf16[64,4096]{1,0:T(8,128)(2,1)S(1)}, bf16[64,4096]{1,0:T(8,128)(2,1)S(1)}, u32[]{:S(2)}, u32[]{:S(2)}) collective-permute-start(bf16[64,4096]{1,0:T(8,128)(2,1)S(1)} %add_convert_fusion.1), channel_id=1, source_target_pairs={{0,8},{1,17},{2,10},{3,19},{4,12},{5,21},{6,14},{7,23},{8,0},{9,25... | collective-permute-start | bytes 1572872 | tf_op jit(solution)/shard_map/ppermute | solution.py:348
  54.6 4.6 %attend_project.3 = bf16[64,4096]{1,0:T(8,128)(2,1)S(1)} custom-call(s32[2,16]{1,0:T(2,128)S(1)} %copy-done.1, bf16[192,1024]{1,0:T(8,128)(2,1)S(1)} %query_rows.2.refs_6_.query_ref, bf16[2048,512]{1,0:T(8,128)(2,1)S(1)} %key_value_gather.1.kv_ref, bf16[1024,4096]{1,0:T(8,128)(2,1)S(1)} %bitcast.13), custom_call_target="tpu_custom_call" | custom-call | flops 1073741824 | bytes 8388608 | tf_op jit(solution)/shard_map/attend_project/pallas_call | solution.py:287
  59.2 6.9 %collective-permute-done.14 = bf16[64,4096]{1,0:T(8,128)(2,1)S(1)} collective-permute-done((bf16[64,4096]{1,0:T(8,128)(2,1)S(1)}, bf16[64,4096]{1,0:T(8,128)(2,1)S(1)}, u32[]{:S(2)}, u32[]{:S(2)}) %collective-permute-start.14) | collective-permute-done | bytes 524320 | tf_op jit(solution)/shard_map/ppermute | solution.py:348
  66.1 1.0 %add_convert_fusion = bf16[64,4096]{1,0:T(8,128)(2,1)} fusion(bf16[64,4096]{1,0:T(8,128)(2,1)S(1)} %collective-permute-done.16, bf16[64,4096]{1,0:T(8,128)(2,1)S(1)} %collective-permute-done.14, bf16[64,4096]{1,0:T(8,128)(2,1)S(1)} %attend_project.3), kind=kLoop, calls=%fused_computation | loop fusion | flops 1572864 | bytes 2097152 | tf_op jit(solution)/shard_map/convert_element_type | solution.py:321
  (34 shorter events, 1.9 us)
Async XLA Ops:
  0.0 15.5 %collective-permute-start = (bf16[64,4096]{1,0:T(8,128)(2,1)}, bf16[64,4096]{1,0:T(8,128)(2,1)S(1)}, u32[]{:S(2)}, u32[]{:S(2)}) collective-permute-start(bf16[64,4096]{1,0:T(8,128)(2,1)} %refs_0_.5), channel_id=1, source_target_pairs={{0,8},{1,17},{2,10},{3,19},{4,12},{5,21},{6,14},{7,23},{8,0},{9,25... | collective-permute-start | bytes 1572872 | tf_op jit(solution)/shard_map/ppermute | solution.py:348
  2.9 16.6 %collective-permute-start.1 = (bf16[64,4096]{1,0:T(8,128)(2,1)}, bf16[64,4096]{1,0:T(8,128)(2,1)S(1)}, u32[]{:S(2)}, u32[]{:S(2)}) collective-permute-start(bf16[64,4096]{1,0:T(8,128)(2,1)} %refs_0_.5), channel_id=1, source_target_pairs={{0,16},{1,9},{2,18},{3,11},{4,20},{5,13},{6,22},{7,15},{8,24},{9,1... | collective-permute-start | bytes 1572872 | tf_op jit(solution)/shard_map/ppermute | solution.py:348
  5.2 3.0 %copy-start = (bf16[64,4096]{1,0:T(8,128)(2,1)S(1)}, bf16[64,4096]{1,0:T(8,128)(2,1)}, u32[]{:S(2)}) copy-start(bf16[64,4096]{1,0:T(8,128)(2,1)} %refs_0_.5) | copy-start | bytes 1572868
  5.7 18.1 %slice-start.2 = ((s8[8388608]{0:T(1024)(128)(4,1)}), s8[4194304]{0:T(1024)(128)(4,1)S(1)}, s32[]{:S(2)}) async-start(s8[8388608]{0:T(1024)(128)(4,1)} %bitcast.14), calls=%async_computation.2 | async-start | bytes 8388608
  8.1 15.7 %slice-start.3 = ((s8[8388608]{0:T(1024)(128)(4,1)}), s8[4194304]{0:T(1024)(128)(4,1)S(1)}, s32[]{:S(2)}) async-start(s8[8388608]{0:T(1024)(128)(4,1)} %bitcast.14), calls=%async_computation.3 | async-start | bytes 8388608
  9.1 7.8 %collective-permute-start.2 = (bf16[64,512]{1,0:T(8,128)(2,1)S(1)}, bf16[64,512]{1,0:T(8,128)(2,1)S(1)}, u32[]{:S(2)}, u32[]{:S(2)}) collective-permute-start(bf16[64,512]{1,0:T(8,128)(2,1)S(1)} %key_value_rows.3), channel_id=1, source_target_pairs={{0,6},{1,7},{2,4},{3,5},{4,2},{5,3},{6,0},{7,1},{8,14},{9,15},{10,... | collective-permute-start | bytes 196616 | tf_op jit(solution)/shard_map/ppermute | solution.py:367
  12.7 4.4 %collective-permute-start.3 = (bf16[64,512]{1,0:T(8,128)(2,1)S(1)}, bf16[64,512]{1,0:T(8,128)(2,1)S(1)}, u32[]{:S(2)}, u32[]{:S(2)}) collective-permute-start(bf16[64,512]{1,0:T(8,128)(2,1)S(1)} %key_value_rows.3), channel_id=1, source_target_pairs={{0,2},{1,3},{2,0},{3,1},{4,6},{5,7},{6,4},{7,5},{8,10},{9,11},{10,... | collective-permute-start | bytes 196616 | tf_op jit(solution)/shard_map/ppermute | solution.py:367
  12.7 5.2 %collective-permute-start.4 = (bf16[64,512]{1,0:T(8,128)(2,1)S(1)}, bf16[64,512]{1,0:T(8,128)(2,1)S(1)}, u32[]{:S(2)}, u32[]{:S(2)}) collective-permute-start(bf16[64,512]{1,0:T(8,128)(2,1)S(1)} %key_value_rows.3), channel_id=1, source_target_pairs={{0,4},{1,5},{2,6},{3,7},{4,0},{5,1},{6,2},{7,3},{8,12},{9,13},{10,... | collective-permute-start | bytes 196616 | tf_op jit(solution)/shard_map/ppermute | solution.py:367
  15.5 10.4 %collective-permute-start.9 = (bf16[64,4096]{1,0:T(8,128)(2,1)S(1)}, bf16[64,4096]{1,0:T(8,128)(2,1)S(1)}, u32[]{:S(2)}, u32[]{:S(2)}) collective-permute-start(bf16[64,4096]{1,0:T(8,128)(2,1)S(1)} %collective-permute-done.refs_1_.refs_0_), channel_id=1, source_target_pairs={{0,16},{1,9},{2,18},{3,11},{4,20},{5,13},{6,22},{7,15},{8,24},{9,1... | collective-permute-start | bytes 1572872 | tf_op jit(solution)/shard_map/ppermute | solution.py:348
  17.9 1.6 %collective-permute-start.5 = (bf16[4,64,512]{2,1,0:T(8,128)(2,1)S(1)}, bf16[4,64,512]{2,1,0:T(8,128)(2,1)S(1)}, u32[]{:S(2)}, u32[]{:S(2)}) collective-permute-start(bf16[4,64,512]{2,1,0:T(8,128)(2,1)S(1)} %pad_maximum_fusion.1.refs_6_.refs_0_), channel_id=1, source_target_pairs={{0,1},{1,0},{2,3},{3,2},{4,5},{5,4},{6,7},{7,6},{8,9},{9,8},{10,11... | collective-permute-start | bytes 786440 | tf_op jit(solution)/shard_map/ppermute | solution.py:380
  20.4 10.9 %collective-permute-start.6 = (bf16[128,512]{1,0:T(8,128)(2,1)S(1)}, bf16[128,512]{1,0:T(8,128)(2,1)S(1)}, u32[]{:S(2)}, u32[]{:S(2)}) collective-permute-start(bf16[128,512]{1,0:T(8,128)(2,1)S(1)} %key_value_rows.4.refs_5_), channel_id=1, source_target_pairs={{0,2},{1,3},{2,0},{3,1},{4,6},{5,7},{6,4},{7,5},{8,10},{9,11},{10,... | collective-permute-start | bytes 393224 | tf_op jit(solution)/shard_map/ppermute | solution.py:367
  22.4 8.8 %collective-permute-start.7 = (bf16[128,512]{1,0:T(8,128)(2,1)S(1)}, bf16[128,512]{1,0:T(8,128)(2,1)S(1)}, u32[]{:S(2)}, u32[]{:S(2)}) collective-permute-start(bf16[128,512]{1,0:T(8,128)(2,1)S(1)} %key_value_rows.4.refs_5_), channel_id=1, source_target_pairs={{0,6},{1,7},{2,4},{3,5},{4,2},{5,3},{6,0},{7,1},{8,14},{9,15},{10,... | collective-permute-start | bytes 393224 | tf_op jit(solution)/shard_map/ppermute | solution.py:367
  25.8 14.4 %slice-start = ((s8[8388608]{0:T(1024)(128)(4,1)}), s8[4194304]{0:T(1024)(128)(4,1)S(1)}, s32[]{:S(2)}) async-start(s8[8388608]{0:T(1024)(128)(4,1)} %bitcast.12), calls=%async_computation | async-start | bytes 8388608
  26.8 13.5 %slice-start.1 = ((s8[8388608]{0:T(1024)(128)(4,1)}), s8[4194304]{0:T(1024)(128)(4,1)S(1)}, s32[]{:S(2)}) async-start(s8[8388608]{0:T(1024)(128)(4,1)} %bitcast.12), calls=%async_computation.1 | async-start | bytes 8388608
  26.8 6.5 %collective-permute-start.11 = (bf16[64,512]{1,0:T(8,128)(2,1)S(1)}, bf16[64,512]{1,0:T(8,128)(2,1)S(1)}, u32[]{:S(2)}, u32[]{:S(2)}) collective-permute-start(bf16[64,512]{1,0:T(8,128)(2,1)S(1)} %key_value_rows.5), channel_id=1, source_target_pairs={{0,2},{1,3},{2,0},{3,1},{4,6},{5,7},{6,4},{7,5},{8,10},{9,11},{10,... | collective-permute-start | bytes 196616 | tf_op jit(solution)/shard_map/ppermute | solution.py:367
  28.1 6.8 %collective-permute-start.12 = (bf16[64,512]{1,0:T(8,128)(2,1)S(1)}, bf16[64,512]{1,0:T(8,128)(2,1)S(1)}, u32[]{:S(2)}, u32[]{:S(2)}) collective-permute-start(bf16[64,512]{1,0:T(8,128)(2,1)S(1)} %key_value_rows.5), channel_id=1, source_target_pairs={{0,4},{1,5},{2,6},{3,7},{4,0},{5,1},{6,2},{7,3},{8,12},{9,13},{10,... | collective-permute-start | bytes 196616 | tf_op jit(solution)/shard_map/ppermute | solution.py:367
  30.7 6.2 %collective-permute-start.10 = (bf16[64,512]{1,0:T(8,128)(2,1)S(1)}, bf16[64,512]{1,0:T(8,128)(2,1)S(1)}, u32[]{:S(2)}, u32[]{:S(2)}) collective-permute-start(bf16[64,512]{1,0:T(8,128)(2,1)S(1)} %key_value_rows.5), channel_id=1, source_target_pairs={{0,6},{1,7},{2,4},{3,5},{4,2},{5,3},{6,0},{7,1},{8,14},{9,15},{10,... | collective-permute-start | bytes 196616 | tf_op jit(solution)/shard_map/ppermute | solution.py:367
  31.3 6.3 %collective-permute-start.8 = (bf16[128,512]{1,0:T(8,128)(2,1)S(1)}, bf16[128,512]{1,0:T(8,128)(2,1)S(1)}, u32[]{:S(2)}, u32[]{:S(2)}) collective-permute-start(bf16[128,512]{1,0:T(8,128)(2,1)S(1)} %collective-permute-done.7), channel_id=1, source_target_pairs={{0,2},{1,3},{2,0},{3,1},{4,6},{5,7},{6,4},{7,5},{8,10},{9,11},{10,... | collective-permute-start | bytes 393224 | tf_op jit(solution)/shard_map/ppermute | solution.py:367
  37.7 2.6 %copy-start.1 = (s32[2,16]{1,0:T(2,128)S(1)}, s32[2,16]{1,0:T(2,128)}, u32[]{:S(2)}) copy-start(s32[2,16]{1,0:T(2,128)} %mask_ref.5) | copy-start | bytes 388
  37.7 2.4 %collective-permute-start.13 = (bf16[4,192,512]{2,1,0:T(8,128)(2,1)S(1)}, bf16[4,192,512]{2,1,0:T(8,128)(2,1)S(1)}, u32[]{:S(2)}, u32[]{:S(2)}) collective-permute-start(bf16[4,192,512]{2,1,0:T(8,128)(2,1)S(1)} %pad_maximum_fusion.refs_2_), channel_id=1, source_target_pairs={{0,1},{1,0},{2,3},{3,2},{4,5},{5,4},{6,7},{7,6},{8,9},{9,8},{10,11... | collective-permute-start | bytes 2359304 | tf_op jit(solution)/shard_map/ppermute | solution.py:380
  43.6 9.4 %collective-permute-start.15 = (bf16[64,4096]{1,0:T(8,128)(2,1)S(1)}, bf16[64,4096]{1,0:T(8,128)(2,1)S(1)}, u32[]{:S(2)}, u32[]{:S(2)}) collective-permute-start(bf16[64,4096]{1,0:T(8,128)(2,1)S(1)} %attend_project.5), channel_id=1, source_target_pairs={{0,16},{1,9},{2,18},{3,11},{4,20},{5,13},{6,22},{7,15},{8,24},{9,1... | collective-permute-start | bytes 1572872 | tf_op jit(solution)/shard_map/ppermute | solution.py:348
  51.5 14.6 %collective-permute-start.14 = (bf16[64,4096]{1,0:T(8,128)(2,1)S(1)}, bf16[64,4096]{1,0:T(8,128)(2,1)S(1)}, u32[]{:S(2)}, u32[]{:S(2)}) collective-permute-start(bf16[64,4096]{1,0:T(8,128)(2,1)S(1)} %get-tuple-element.18), channel_id=1, source_target_pairs={{0,16},{1,9},{2,18},{3,11},{4,20},{5,13},{6,22},{7,15},{8,24},{9,1... | collective-permute-start | bytes 1572872 | tf_op jit(solution)/shard_map/ppermute | solution.py:348
  53.1 13.0 %collective-permute-start.16 = (bf16[64,4096]{1,0:T(8,128)(2,1)S(1)}, bf16[64,4096]{1,0:T(8,128)(2,1)S(1)}, u32[]{:S(2)}, u32[]{:S(2)}) collective-permute-start(bf16[64,4096]{1,0:T(8,128)(2,1)S(1)} %add_convert_fusion.1), channel_id=1, source_target_pairs={{0,8},{1,17},{2,10},{3,19},{4,12},{5,21},{6,14},{7,23},{8,0},{9,25... | collective-permute-start | bytes 1572872 | tf_op jit(solution)/shard_map/ppermute | solution.py:348

commit v5 on v4

--- a/solution.py
+++ b/solution.py
@@ -225,7 +225,19 @@
                 new_state += [top, sums]
             return tuple(new_state)
 
-        state = lax.fori_loop(1, (count + WIDE - 1) // WIDE, step, step(0, None))
+        def many_steps(step=step, count=count):
+            one, two = step(0, None), step(1, None)
+            state = []
+            for head in range(kv_heads):
+                top = jnp.maximum(one[2 * head], two[2 * head])
+                state += [
+                    top,
+                    one[2 * head + 1] * jnp.exp2(one[2 * head] - top)
+                    + two[2 * head + 1] * jnp.exp2(two[2 * head] - top),
+                ]
+            return lax.fori_loop(2, (count + WIDE - 1) // WIDE, step, tuple(state))
+
+        state = lax.cond(count > WIDE, many_steps, functools.partial(step, 0, None))
         for head in range(kv_heads):
             sums = state[2 * head + 1]
             mixed = (sums[:, :HEAD_WIDTH] / sums[:, HEAD_WIDTH:]).astype(jnp.bfloat16)

time: 67.3 us -> 66.1 us (0.982)
  Pallas kernels: 22.5 us -> 21.7 us
    pallas_call x3, Pallas kernels: 13.6 us -> 12.8 us  [attend(): pl.pallas_call(functools.partial(attend_kernel, slots, held, placed), out...]
where the time goes in v5:
time: 66.1 us; the launch traced here: 65.9 us
  starting transfers between devices  21.9 us (33%)
  Pallas kernels  21.7 us (33%)
  waiting for transfers between devices  19.5 us (30%)
  other arithmetic  2.47 us (4%)
    pallas_call x3, Pallas kernels, attend(): pl.pallas_call(functools.partial(attend_kernel, slots, held, placed), out...  12.8 us
    ppermute x9, starting transfers between devices, across_chips(): lax.ppermute(value, 'blk', [(b, b ^ 2 * by) for b in range(blk_count)])  12.7 us
    ppermute x6, waiting for transfers between devices, send(): return lax.ppermute(value, ('grp', 'blk'), pairs)  10.4 us
    ppermute x6, starting transfers between devices, send(): return lax.ppermute(value, ('grp', 'blk'), pairs)  9.06 us
    ppermute x9, waiting for transfers between devices, across_chips(): lax.ppermute(value, 'blk', [(b, b ^ 2 * by) for b in range(blk_count)])  5.31 us
    ppermute x2, waiting for transfers between devices, with_other_core(): lax.ppermute(held, 'blk', [(b, b ^ 1) for b in range(blk_count)])  3.79 us
    pallas_call x2, Pallas kernels, query_rows(): pl.pallas_call(functools.partial(query_kernel, slots), out_shape=jax.Shap...  3.67 us
    pallas_call x3, Pallas kernels, key_value_rows(): pl.pallas_call(functools.partial(key_value_kernel, len(pieces), slots), o...  2.65 us
  transfers between devices with their start and end apart: 17, of which 10 were waited for; matrix products, arithmetic and copies ran while one was open for 2% of the time, Pallas kernels for 28%

profile of v5, /device:TPU:0, one launch (start us, length us, event | category | flops | bytes accessed | tf_op | source)
XLA Modules:
  0.0 65.9 jit_solution(5487694170107972247)
XLA Ops:
  0.0 2.9 %collective-permute-start = (bf16[64,4096]{1,0:T(8,128)(2,1)}, bf16[64,4096]{1,0:T(8,128)(2,1)S(1)}, u32[]{:S(2)}, u32[]{:S(2)}) collective-permute-start(bf16[64,4096]{1,0:T(8,128)(2,1)} %refs_0_.5), channel_id=1, source_target_pairs={{0,8},{1,17},{2,10},{3,19},{4,12},{5,21},{6,14},{7,23},{8,0},{9,25... | collective-permute-start | bytes 1572872 | tf_op jit(solution)/shard_map/ppermute | solution.py:360
  2.9 1.5 %collective-permute-start.1 = (bf16[64,4096]{1,0:T(8,128)(2,1)}, bf16[64,4096]{1,0:T(8,128)(2,1)S(1)}, u32[]{:S(2)}, u32[]{:S(2)}) collective-permute-start(bf16[64,4096]{1,0:T(8,128)(2,1)} %refs_0_.5), channel_id=1, source_target_pairs={{0,16},{1,9},{2,18},{3,11},{4,20},{5,13},{6,22},{7,15},{8,24},{9,1... | collective-permute-start | bytes 1572872 | tf_op jit(solution)/shard_map/ppermute | solution.py:360
  4.5 0.7 %convert_element_type.31 = f32[256]{0:T(256)S(1)} convert(s32[256]{0:T(256)} %param.13) | non-fusion elementwise | flops 256 | bytes 2048 | tf_op jit(solution)/shard_map/convert_element_type | solution.py:325
  5.7 2.4 %preload.1 = (bf16[4096,256]{1,0:T(8,128)(2,1)S(1)}, bf16[4096,256]{1,0:T(8,128)(2,1)S(1)}) custom-call(bf16[4096,256]{1,0:T(8,128)(2,1)} %refs_0_.4, bf16[4096,256]{1,0:T(8,128)(2,1)} %refs_1_.2, f32[256,128]{1,0:T(8,128)S(1)} %get-tuple-element.22.refs_4_.refs_2_.refs_3_, f32[256,128]{1,0:T(8,128)S(1)} %get-tuple-element.21.refs_5_.refs_3_.refs_4_), custom_call_target="tpu_custom_call" | custom-call | tf_op jit(solution)/shard_map/preload/pallas_call | solution.py:46
  8.1 0.9 %key_value_rows.3 = bf16[64,512]{1,0:T(8,128)(2,1)S(1)} custom-call(bf16[64,4096]{1,0:T(8,128)(2,1)S(1)} %copy-done, bf16[4096,256]{1,0:T(8,128)(2,1)S(1)} %get-tuple-element.13.refs_1_.refs_2_, bf16[4096,256]{1,0:T(8,128)(2,1)S(1)} %get-tuple-element.14.refs_2_.refs_3_, f32[256,128]{1,0:T(8,128)S(1)} %get-tuple-element.22.refs_4_.refs_2_.refs_3_, ...), custom_call_target="tpu_custom_call" | custom-call | flops 268435456 | bytes 4194304 | tf_op jit(solution)/shard_map/key_value_rows/pallas_call | solution.py:103
  9.1 3.7 %collective-permute-start.2 = (bf16[64,512]{1,0:T(8,128)(2,1)S(1)}, bf16[64,512]{1,0:T(8,128)(2,1)S(1)}, u32[]{:S(2)}, u32[]{:S(2)}) collective-permute-start(bf16[64,512]{1,0:T(8,128)(2,1)S(1)} %key_value_rows.3), channel_id=1, source_target_pairs={{0,6},{1,7},{2,4},{3,5},{4,2},{5,3},{6,0},{7,1},{8,14},{9,15},{10,... | collective-permute-start | bytes 196616 | tf_op jit(solution)/shard_map/ppermute | solution.py:379
  12.7 0.8 %collective-permute-start.4 = (bf16[64,512]{1,0:T(8,128)(2,1)S(1)}, bf16[64,512]{1,0:T(8,128)(2,1)S(1)}, u32[]{:S(2)}, u32[]{:S(2)}) collective-permute-start(bf16[64,512]{1,0:T(8,128)(2,1)S(1)} %key_value_rows.3), channel_id=1, source_target_pairs={{0,4},{1,5},{2,6},{3,7},{4,0},{5,1},{6,2},{7,3},{8,12},{9,13},{10,... | collective-permute-start | bytes 196616 | tf_op jit(solution)/shard_map/ppermute | solution.py:379
  13.5 1.9 %collective-permute-done.refs_1_.refs_0_ = bf16[64,4096]{1,0:T(8,128)(2,1)S(1)} collective-permute-done((bf16[64,4096]{1,0:T(8,128)(2,1)}, bf16[64,4096]{1,0:T(8,128)(2,1)S(1)}, u32[]{:S(2)}, u32[]{:S(2)}) %collective-permute-start) | collective-permute-done | bytes 524320 | tf_op jit(solution)/shard_map/ppermute | solution.py:360
  15.5 1.4 %collective-permute-start.9 = (bf16[64,4096]{1,0:T(8,128)(2,1)S(1)}, bf16[64,4096]{1,0:T(8,128)(2,1)S(1)}, u32[]{:S(2)}, u32[]{:S(2)}) collective-permute-start(bf16[64,4096]{1,0:T(8,128)(2,1)S(1)} %collective-permute-done.refs_1_.refs_0_), channel_id=1, source_target_pairs={{0,16},{1,9},{2,18},{3,11},{4,20},{5,13},{6,22},{7,15},{8,24},{9,1... | collective-permute-start | bytes 1572872 | tf_op jit(solution)/shard_map/ppermute | solution.py:360
  17.1 0.8 %collective-permute-done.4 = bf16[64,512]{1,0:T(8,128)(2,1)S(1)} collective-permute-done((bf16[64,512]{1,0:T(8,128)(2,1)S(1)}, bf16[64,512]{1,0:T(8,128)(2,1)S(1)}, u32[]{:S(2)}, u32[]{:S(2)}) %collective-permute-start.4) | collective-permute-done | bytes 65568 | tf_op jit(solution)/shard_map/ppermute | solution.py:379
  18.0 1.5 %collective-permute-done.5.refs_7_.refs_1_ = bf16[4,64,512]{2,1,0:T(8,128)(2,1)S(1)} collective-permute-done((bf16[4,64,512]{2,1,0:T(8,128)(2,1)S(1)}, bf16[4,64,512]{2,1,0:T(8,128)(2,1)S(1)}, u32[]{:S(2)}, u32[]{:S(2)}) %collective-permute-start.5) | collective-permute-done | bytes 262176 | tf_op jit(solution)/shard_map/ppermute | solution.py:392
  19.5 0.8 %key_value_rows.4.refs_5_ = bf16[128,512]{1,0:T(8,128)(2,1)S(1)} custom-call(bf16[64,4096]{1,0:T(8,128)(2,1)S(1)} %collective-permute-done.refs_1_.refs_0_, bf16[64,4096]{1,0:T(8,128)(2,1)S(1)} %collective-permute-done.1.refs_2_.refs_1_, bf16[4096,256]{1,0:T(8,128)(2,1)S(1)} %get-tuple-element.13.refs_1_.refs_2_, ...), custom_call_target="tpu_custom_call" | custom-call | flops 536870912 | bytes 4194304 | tf_op jit(solution)/shard_map/key_value_rows/pallas_call | solution.py:103
  20.4 2.1 %collective-permute-start.6 = (bf16[128,512]{1,0:T(8,128)(2,1)S(1)}, bf16[128,512]{1,0:T(8,128)(2,1)S(1)}, u32[]{:S(2)}, u32[]{:S(2)}) collective-permute-start(bf16[128,512]{1,0:T(8,128)(2,1)S(1)} %key_value_rows.4.refs_5_), channel_id=1, source_target_pairs={{0,2},{1,3},{2,0},{3,1},{4,6},{5,7},{6,4},{7,5},{8,10},{9,11},{10,... | collective-permute-start | bytes 393224 | tf_op jit(solution)/shard_map/ppermute | solution.py:379
  22.4 1.4 %collective-permute-start.7 = (bf16[128,512]{1,0:T(8,128)(2,1)S(1)}, bf16[128,512]{1,0:T(8,128)(2,1)S(1)}, u32[]{:S(2)}, u32[]{:S(2)}) collective-permute-start(bf16[128,512]{1,0:T(8,128)(2,1)S(1)} %key_value_rows.4.refs_5_), channel_id=1, source_target_pairs={{0,6},{1,7},{2,4},{3,5},{4,2},{5,3},{6,0},{7,1},{8,14},{9,15},{10,... | collective-permute-start | bytes 393224 | tf_op jit(solution)/shard_map/ppermute | solution.py:379
  23.8 2.0 %query_rows.2.refs_6_.query_ref = bf16[192,1024]{1,0:T(8,128)(2,1)S(1)} custom-call(bf16[64,4096]{1,0:T(8,128)(2,1)S(1)} %copy-done, bf16[64,4096]{1,0:T(8,128)(2,1)S(1)} %collective-permute-done.refs_1_.refs_0_, bf16[64,4096]{1,0:T(8,128)(2,1)S(1)} %collective-permute-done.1.refs_2_.refs_1_, bf16[4096,1024]{1,0:T(8,128)(2,1)S(1)} %bitcast.15, ...), custom_call_target="tpu_custom_call" | custom-call | flops 1610612736 | bytes 8388608 | tf_op jit(solution)/shard_map/query_rows/pallas_call | solution.py:137
  25.9 0.9 %key_value_rows.5 = bf16[64,512]{1,0:T(8,128)(2,1)S(1)} custom-call(bf16[64,4096]{1,0:T(8,128)(2,1)S(1)} %collective-permute-done.9.refs_0_, bf16[4096,256]{1,0:T(8,128)(2,1)S(1)} %get-tuple-element.13.refs_1_.refs_2_, bf16[4096,256]{1,0:T(8,128)(2,1)S(1)} %get-tuple-element.14.refs_2_.refs_3_, f32[256,128]{1,0:T(8,128)S(1)} %get-tuple-element.22.refs_4_.refs_2_.refs_3_, ...), custom_call_target="tpu_custom_call" | custom-call | flops 268435456 | bytes 4194304 | tf_op jit(solution)/shard_map/key_value_rows/pallas_call | solution.py:103
  26.8 1.3 %collective-permute-start.11 = (bf16[64,512]{1,0:T(8,128)(2,1)S(1)}, bf16[64,512]{1,0:T(8,128)(2,1)S(1)}, u32[]{:S(2)}, u32[]{:S(2)}) collective-permute-start(bf16[64,512]{1,0:T(8,128)(2,1)S(1)} %key_value_rows.5), channel_id=1, source_target_pairs={{0,2},{1,3},{2,0},{3,1},{4,6},{5,7},{6,4},{7,5},{8,10},{9,11},{10,... | collective-permute-start | bytes 196616 | tf_op jit(solution)/shard_map/ppermute | solution.py:379
  28.1 2.6 %collective-permute-start.12 = (bf16[64,512]{1,0:T(8,128)(2,1)S(1)}, bf16[64,512]{1,0:T(8,128)(2,1)S(1)}, u32[]{:S(2)}, u32[]{:S(2)}) collective-permute-start(bf16[64,512]{1,0:T(8,128)(2,1)S(1)} %key_value_rows.5), channel_id=1, source_target_pairs={{0,4},{1,5},{2,6},{3,7},{4,0},{5,1},{6,2},{7,3},{8,12},{9,13},{10,... | collective-permute-start | bytes 196616 | tf_op jit(solution)/shard_map/ppermute | solution.py:379
  30.7 0.6 collective-permute-start.10
  31.6 1.7 %query_rows.3.query_ref = bf16[64,1024]{1,0:T(8,128)(2,1)S(1)} custom-call(bf16[64,4096]{1,0:T(8,128)(2,1)S(1)} %collective-permute-done.9.refs_0_, bf16[4096,1024]{1,0:T(8,128)(2,1)S(1)} %bitcast.15, f32[256,128]{1,0:T(8,128)S(1)} %get-tuple-element.22.refs_4_.refs_2_.refs_3_, f32[256,128]{1,0:T(8,128)S(1)} %get-tuple-element.21.refs_5_.refs_3_.refs_4_), custom_call_target="tpu_custom_call" | custom-call | flops 536870912 | bytes 8388608 | tf_op jit(solution)/shard_map/query_rows/pallas_call | solution.py:137
  33.3 1.6 %collective-permute-done.12 = bf16[64,512]{1,0:T(8,128)(2,1)S(1)} collective-permute-done((bf16[64,512]{1,0:T(8,128)(2,1)S(1)}, bf16[64,512]{1,0:T(8,128)(2,1)S(1)}, u32[]{:S(2)}, u32[]{:S(2)}) %collective-permute-start.12) | collective-permute-done | bytes 65568 | tf_op jit(solution)/shard_map/ppermute | solution.py:379
  34.9 2.0 %collective-permute-done.10 = bf16[64,512]{1,0:T(8,128)(2,1)S(1)} collective-permute-done((bf16[64,512]{1,0:T(8,128)(2,1)S(1)}, bf16[64,512]{1,0:T(8,128)(2,1)S(1)}, u32[]{:S(2)}, u32[]{:S(2)}) %collective-permute-start.10) | collective-permute-done | bytes 65568 | tf_op jit(solution)/shard_map/ppermute | solution.py:379
  36.9 0.7 %collective-permute-done.8 = bf16[128,512]{1,0:T(8,128)(2,1)S(1)} collective-permute-done((bf16[128,512]{1,0:T(8,128)(2,1)S(1)}, bf16[128,512]{1,0:T(8,128)(2,1)S(1)}, u32[]{:S(2)}, u32[]{:S(2)}) %collective-permute-start.8) | collective-permute-done | bytes 131104 | tf_op jit(solution)/shard_map/ppermute | solution.py:379
  37.8 2.3 %collective-permute-done.13.refs_3_ = bf16[4,192,512]{2,1,0:T(8,128)(2,1)S(1)} collective-permute-done((bf16[4,192,512]{2,1,0:T(8,128)(2,1)S(1)}, bf16[4,192,512]{2,1,0:T(8,128)(2,1)S(1)}, u32[]{:S(2)}, u32[]{:S(2)}) %collective-permute-start.13) | collective-permute-done | bytes 786464 | tf_op jit(solution)/shard_map/ppermute | solution.py:392
  40.3 3.4 %attend_project.5 = bf16[64,4096]{1,0:T(8,128)(2,1)S(1)} custom-call(s32[2,16]{1,0:T(2,128)S(1)} %copy-done.1, bf16[64,1024]{1,0:T(8,128)(2,1)S(1)} %query_rows.3.query_ref, bf16[2048,512]{1,0:T(8,128)(2,1)S(1)} %key_value_gather.1.kv_ref, bf16[1024,4096]{1,0:T(8,128)(2,1)S(1)} %bitcast.13), custom_call_target="tpu_custom_call" | custom-call | flops 1073741824 | bytes 8388608 | tf_op jit(solution)/shard_map/attend_project/pallas_call | solution.py:299
  43.6 1.6 %collective-permute-start.15 = (bf16[64,4096]{1,0:T(8,128)(2,1)S(1)}, bf16[64,4096]{1,0:T(8,128)(2,1)S(1)}, u32[]{:S(2)}, u32[]{:S(2)}) collective-permute-start(bf16[64,4096]{1,0:T(8,128)(2,1)S(1)} %attend_project.5), channel_id=1, source_target_pairs={{0,16},{1,9},{2,18},{3,11},{4,20},{5,13},{6,22},{7,15},{8,24},{9,1... | collective-permute-start | bytes 1572872 | tf_op jit(solution)/shard_map/ppermute | solution.py:360
  45.2 5.4 %attend_project.4 = (bf16[64,4096]{1,0:T(8,128)(2,1)S(1)}, bf16[64,4096]{1,0:T(8,128)(2,1)S(1)}) custom-call(s32[2,16]{1,0:T(2,128)S(1)} %copy-done.1, bf16[192,1024]{1,0:T(8,128)(2,1)S(1)} %query_rows.2.refs_6_.query_ref, bf16[2048,512]{1,0:T(8,128)(2,1)S(1)} %key_value_gather.1.kv_ref, bf16[1024,4096]{1,0:T(8,128)(2,1)S(1)} %bitcast.13), custom_call_target="tpu_custom_call" | custom-call | flops 2147483648 | bytes 8388608 | tf_op jit(solution)/shard_map/attend_project/pallas_call | solution.py:299
  51.1 1.8 %collective-permute-done.15 = bf16[64,4096]{1,0:T(8,128)(2,1)S(1)} collective-permute-done((bf16[64,4096]{1,0:T(8,128)(2,1)S(1)}, bf16[64,4096]{1,0:T(8,128)(2,1)S(1)}, u32[]{:S(2)}, u32[]{:S(2)}) %collective-permute-start.15) | collective-permute-done | bytes 524320 | tf_op jit(solution)/shard_map/ppermute | solution.py:360
  53.0 1.2 %collective-permute-start.16 = (bf16[64,4096]{1,0:T(8,128)(2,1)S(1)}, bf16[64,4096]{1,0:T(8,128)(2,1)S(1)}, u32[]{:S(2)}, u32[]{:S(2)}) collective-permute-start(bf16[64,4096]{1,0:T(8,128)(2,1)S(1)} %add_convert_fusion.1), channel_id=1, source_target_pairs={{0,8},{1,17},{2,10},{3,19},{4,12},{5,21},{6,14},{7,23},{8,0},{9,25... | collective-permute-start | bytes 1572872 | tf_op jit(solution)/shard_map/ppermute | solution.py:360
  54.3 4.0 %attend_project.3 = bf16[64,4096]{1,0:T(8,128)(2,1)S(1)} custom-call(s32[2,16]{1,0:T(2,128)S(1)} %copy-done.1, bf16[192,1024]{1,0:T(8,128)(2,1)S(1)} %query_rows.2.refs_6_.query_ref, bf16[2048,512]{1,0:T(8,128)(2,1)S(1)} %key_value_gather.1.kv_ref, bf16[1024,4096]{1,0:T(8,128)(2,1)S(1)} %bitcast.13), custom_call_target="tpu_custom_call" | custom-call | flops 1073741824 | bytes 8388608 | tf_op jit(solution)/shard_map/attend_project/pallas_call | solution.py:299
  58.3 6.6 %collective-permute-done.14 = bf16[64,4096]{1,0:T(8,128)(2,1)S(1)} collective-permute-done((bf16[64,4096]{1,0:T(8,128)(2,1)S(1)}, bf16[64,4096]{1,0:T(8,128)(2,1)S(1)}, u32[]{:S(2)}, u32[]{:S(2)}) %collective-permute-start.14) | collective-permute-done | bytes 524320 | tf_op jit(solution)/shard_map/ppermute | solution.py:360
  64.9 1.0 %add_convert_fusion = bf16[64,4096]{1,0:T(8,128)(2,1)} fusion(bf16[64,4096]{1,0:T(8,128)(2,1)S(1)} %collective-permute-done.16, bf16[64,4096]{1,0:T(8,128)(2,1)S(1)} %collective-permute-done.14, bf16[64,4096]{1,0:T(8,128)(2,1)S(1)} %attend_project.3), kind=kLoop, calls=%fused_computation | loop fusion | flops 1572864 | bytes 2097152 | tf_op jit(solution)/shard_map/convert_element_type | solution.py:333
  (34 shorter events, 2.2 us)
Async XLA Ops:
  0.0 15.5 %collective-permute-start = (bf16[64,4096]{1,0:T(8,128)(2,1)}, bf16[64,4096]{1,0:T(8,128)(2,1)S(1)}, u32[]{:S(2)}, u32[]{:S(2)}) collective-permute-start(bf16[64,4096]{1,0:T(8,128)(2,1)} %refs_0_.5), channel_id=1, source_target_pairs={{0,8},{1,17},{2,10},{3,19},{4,12},{5,21},{6,14},{7,23},{8,0},{9,25... | collective-permute-start | bytes 1572872 | tf_op jit(solution)/shard_map/ppermute | solution.py:360
  2.9 16.6 %collective-permute-start.1 = (bf16[64,4096]{1,0:T(8,128)(2,1)}, bf16[64,4096]{1,0:T(8,128)(2,1)S(1)}, u32[]{:S(2)}, u32[]{:S(2)}) collective-permute-start(bf16[64,4096]{1,0:T(8,128)(2,1)} %refs_0_.5), channel_id=1, source_target_pairs={{0,16},{1,9},{2,18},{3,11},{4,20},{5,13},{6,22},{7,15},{8,24},{9,1... | collective-permute-start | bytes 1572872 | tf_op jit(solution)/shard_map/ppermute | solution.py:360
  5.2 3.0 %copy-start = (bf16[64,4096]{1,0:T(8,128)(2,1)S(1)}, bf16[64,4096]{1,0:T(8,128)(2,1)}, u32[]{:S(2)}) copy-start(bf16[64,4096]{1,0:T(8,128)(2,1)} %refs_0_.5) | copy-start | bytes 1572868
  5.7 18.1 %slice-start.2 = ((s8[8388608]{0:T(1024)(128)(4,1)}), s8[4194304]{0:T(1024)(128)(4,1)S(1)}, s32[]{:S(2)}) async-start(s8[8388608]{0:T(1024)(128)(4,1)} %bitcast.14), calls=%async_computation.2 | async-start | bytes 8388608
  8.1 15.7 %slice-start.3 = ((s8[8388608]{0:T(1024)(128)(4,1)}), s8[4194304]{0:T(1024)(128)(4,1)S(1)}, s32[]{:S(2)}) async-start(s8[8388608]{0:T(1024)(128)(4,1)} %bitcast.14), calls=%async_computation.3 | async-start | bytes 8388608
  9.1 7.8 %collective-permute-start.2 = (bf16[64,512]{1,0:T(8,128)(2,1)S(1)}, bf16[64,512]{1,0:T(8,128)(2,1)S(1)}, u32[]{:S(2)}, u32[]{:S(2)}) collective-permute-start(bf16[64,512]{1,0:T(8,128)(2,1)S(1)} %key_value_rows.3), channel_id=1, source_target_pairs={{0,6},{1,7},{2,4},{3,5},{4,2},{5,3},{6,0},{7,1},{8,14},{9,15},{10,... | collective-permute-start | bytes 196616 | tf_op jit(solution)/shard_map/ppermute | solution.py:379
  12.7 4.4 %collective-permute-start.3 = (bf16[64,512]{1,0:T(8,128)(2,1)S(1)}, bf16[64,512]{1,0:T(8,128)(2,1)S(1)}, u32[]{:S(2)}, u32[]{:S(2)}) collective-permute-start(bf16[64,512]{1,0:T(8,128)(2,1)S(1)} %key_value_rows.3), channel_id=1, source_target_pairs={{0,2},{1,3},{2,0},{3,1},{4,6},{5,7},{6,4},{7,5},{8,10},{9,11},{10,... | collective-permute-start | bytes 196616 | tf_op jit(solution)/shard_map/ppermute | solution.py:379
  12.7 5.2 %collective-permute-start.4 = (bf16[64,512]{1,0:T(8,128)(2,1)S(1)}, bf16[64,512]{1,0:T(8,128)(2,1)S(1)}, u32[]{:S(2)}, u32[]{:S(2)}) collective-permute-start(bf16[64,512]{1,0:T(8,128)(2,1)S(1)} %key_value_rows.3), channel_id=1, source_target_pairs={{0,4},{1,5},{2,6},{3,7},{4,0},{5,1},{6,2},{7,3},{8,12},{9,13},{10,... | collective-permute-start | bytes 196616 | tf_op jit(solution)/shard_map/ppermute | solution.py:379
  15.5 10.4 %collective-permute-start.9 = (bf16[64,4096]{1,0:T(8,128)(2,1)S(1)}, bf16[64,4096]{1,0:T(8,128)(2,1)S(1)}, u32[]{:S(2)}, u32[]{:S(2)}) collective-permute-start(bf16[64,4096]{1,0:T(8,128)(2,1)S(1)} %collective-permute-done.refs_1_.refs_0_), channel_id=1, source_target_pairs={{0,16},{1,9},{2,18},{3,11},{4,20},{5,13},{6,22},{7,15},{8,24},{9,1... | collective-permute-start | bytes 1572872 | tf_op jit(solution)/shard_map/ppermute | solution.py:360
  17.9 1.6 %collective-permute-start.5 = (bf16[4,64,512]{2,1,0:T(8,128)(2,1)S(1)}, bf16[4,64,512]{2,1,0:T(8,128)(2,1)S(1)}, u32[]{:S(2)}, u32[]{:S(2)}) collective-permute-start(bf16[4,64,512]{2,1,0:T(8,128)(2,1)S(1)} %pad_maximum_fusion.1.refs_6_.refs_0_), channel_id=1, source_target_pairs={{0,1},{1,0},{2,3},{3,2},{4,5},{5,4},{6,7},{7,6},{8,9},{9,8},{10,11... | collective-permute-start | bytes 786440 | tf_op jit(solution)/shard_map/ppermute | solution.py:392
  20.4 10.9 %collective-permute-start.6 = (bf16[128,512]{1,0:T(8,128)(2,1)S(1)}, bf16[128,512]{1,0:T(8,128)(2,1)S(1)}, u32[]{:S(2)}, u32[]{:S(2)}) collective-permute-start(bf16[128,512]{1,0:T(8,128)(2,1)S(1)} %key_value_rows.4.refs_5_), channel_id=1, source_target_pairs={{0,2},{1,3},{2,0},{3,1},{4,6},{5,7},{6,4},{7,5},{8,10},{9,11},{10,... | collective-permute-start | bytes 393224 | tf_op jit(solution)/shard_map/ppermute | solution.py:379
  22.4 8.8 %collective-permute-start.7 = (bf16[128,512]{1,0:T(8,128)(2,1)S(1)}, bf16[128,512]{1,0:T(8,128)(2,1)S(1)}, u32[]{:S(2)}, u32[]{:S(2)}) collective-permute-start(bf16[128,512]{1,0:T(8,128)(2,1)S(1)} %key_value_rows.4.refs_5_), channel_id=1, source_target_pairs={{0,6},{1,7},{2,4},{3,5},{4,2},{5,3},{6,0},{7,1},{8,14},{9,15},{10,... | collective-permute-start | bytes 393224 | tf_op jit(solution)/shard_map/ppermute | solution.py:379
  25.8 14.4 %slice-start = ((s8[8388608]{0:T(1024)(128)(4,1)}), s8[4194304]{0:T(1024)(128)(4,1)S(1)}, s32[]{:S(2)}) async-start(s8[8388608]{0:T(1024)(128)(4,1)} %bitcast.12), calls=%async_computation | async-start | bytes 8388608
  26.8 13.5 %slice-start.1 = ((s8[8388608]{0:T(1024)(128)(4,1)}), s8[4194304]{0:T(1024)(128)(4,1)S(1)}, s32[]{:S(2)}) async-start(s8[8388608]{0:T(1024)(128)(4,1)} %bitcast.12), calls=%async_computation.1 | async-start | bytes 8388608
  26.8 6.5 %collective-permute-start.11 = (bf16[64,512]{1,0:T(8,128)(2,1)S(1)}, bf16[64,512]{1,0:T(8,128)(2,1)S(1)}, u32[]{:S(2)}, u32[]{:S(2)}) collective-permute-start(bf16[64,512]{1,0:T(8,128)(2,1)S(1)} %key_value_rows.5), channel_id=1, source_target_pairs={{0,2},{1,3},{2,0},{3,1},{4,6},{5,7},{6,4},{7,5},{8,10},{9,11},{10,... | collective-permute-start | bytes 196616 | tf_op jit(solution)/shard_map/ppermute | solution.py:379
  28.1 6.8 %collective-permute-start.12 = (bf16[64,512]{1,0:T(8,128)(2,1)S(1)}, bf16[64,512]{1,0:T(8,128)(2,1)S(1)}, u32[]{:S(2)}, u32[]{:S(2)}) collective-permute-start(bf16[64,512]{1,0:T(8,128)(2,1)S(1)} %key_value_rows.5), channel_id=1, source_target_pairs={{0,4},{1,5},{2,6},{3,7},{4,0},{5,1},{6,2},{7,3},{8,12},{9,13},{10,... | collective-permute-start | bytes 196616 | tf_op jit(solution)/shard_map/ppermute | solution.py:379
  30.7 6.2 %collective-permute-start.10 = (bf16[64,512]{1,0:T(8,128)(2,1)S(1)}, bf16[64,512]{1,0:T(8,128)(2,1)S(1)}, u32[]{:S(2)}, u32[]{:S(2)}) collective-permute-start(bf16[64,512]{1,0:T(8,128)(2,1)S(1)} %key_value_rows.5), channel_id=1, source_target_pairs={{0,6},{1,7},{2,4},{3,5},{4,2},{5,3},{6,0},{7,1},{8,14},{9,15},{10,... | collective-permute-start | bytes 196616 | tf_op jit(solution)/shard_map/ppermute | solution.py:379
  31.3 6.3 %collective-permute-start.8 = (bf16[128,512]{1,0:T(8,128)(2,1)S(1)}, bf16[128,512]{1,0:T(8,128)(2,1)S(1)}, u32[]{:S(2)}, u32[]{:S(2)}) collective-permute-start(bf16[128,512]{1,0:T(8,128)(2,1)S(1)} %collective-permute-done.7), channel_id=1, source_target_pairs={{0,2},{1,3},{2,0},{3,1},{4,6},{5,7},{6,4},{7,5},{8,10},{9,11},{10,... | collective-permute-start | bytes 393224 | tf_op jit(solution)/shard_map/ppermute | solution.py:379
  37.7 2.6 %copy-start.1 = (s32[2,16]{1,0:T(2,128)S(1)}, s32[2,16]{1,0:T(2,128)}, u32[]{:S(2)}) copy-start(s32[2,16]{1,0:T(2,128)} %mask_ref.5) | copy-start | bytes 388
  37.7 2.4 %collective-permute-start.13 = (bf16[4,192,512]{2,1,0:T(8,128)(2,1)S(1)}, bf16[4,192,512]{2,1,0:T(8,128)(2,1)S(1)}, u32[]{:S(2)}, u32[]{:S(2)}) collective-permute-start(bf16[4,192,512]{2,1,0:T(8,128)(2,1)S(1)} %pad_maximum_fusion.refs_2_), channel_id=1, source_target_pairs={{0,1},{1,0},{2,3},{3,2},{4,5},{5,4},{6,7},{7,6},{8,9},{9,8},{10,11... | collective-permute-start | bytes 2359304 | tf_op jit(solution)/shard_map/ppermute | solution.py:392
  43.6 9.2 %collective-permute-start.15 = (bf16[64,4096]{1,0:T(8,128)(2,1)S(1)}, bf16[64,4096]{1,0:T(8,128)(2,1)S(1)}, u32[]{:S(2)}, u32[]{:S(2)}) collective-permute-start(bf16[64,4096]{1,0:T(8,128)(2,1)S(1)} %attend_project.5), channel_id=1, source_target_pairs={{0,16},{1,9},{2,18},{3,11},{4,20},{5,13},{6,22},{7,15},{8,24},{9,1... | collective-permute-start | bytes 1572872 | tf_op jit(solution)/shard_map/ppermute | solution.py:360
  50.7 14.3 %collective-permute-start.14 = (bf16[64,4096]{1,0:T(8,128)(2,1)S(1)}, bf16[64,4096]{1,0:T(8,128)(2,1)S(1)}, u32[]{:S(2)}, u32[]{:S(2)}) collective-permute-start(bf16[64,4096]{1,0:T(8,128)(2,1)S(1)} %get-tuple-element.18), channel_id=1, source_target_pairs={{0,16},{1,9},{2,18},{3,11},{4,20},{5,13},{6,22},{7,15},{8,24},{9,1... | collective-permute-start | bytes 1572872 | tf_op jit(solution)/shard_map/ppermute | solution.py:360
  53.0 11.9 %collective-permute-start.16 = (bf16[64,4096]{1,0:T(8,128)(2,1)S(1)}, bf16[64,4096]{1,0:T(8,128)(2,1)S(1)}, u32[]{:S(2)}, u32[]{:S(2)}) collective-permute-start(bf16[64,4096]{1,0:T(8,128)(2,1)S(1)} %add_convert_fusion.1), channel_id=1, source_target_pairs={{0,8},{1,17},{2,10},{3,19},{4,12},{5,21},{6,14},{7,23},{8,0},{9,25... | collective-permute-start | bytes 1572872 | tf_op jit(solution)/shard_map/ppermute | solution.py:360

commit v6 on v5

--- a/solution.py
+++ b/solution.py
@@ -410,8 +410,9 @@
 
     (term_across,) = terms((3,))
     sent_across = send(term_across, 2)
-    term_first, term_second = terms((1, 2))
+    (term_second,) = terms((2,))
     sent_second = send(term_second, 2)
+    (term_first,) = terms((1,))
     sent_first = send(add(term_first, sent_across), 1)
     (term_own,) = terms((0,))
     return add(term_own, sent_second, sent_first)

time: 66.1 us -> 64.9 us (0.982)
  waiting for transfers between devices: 19.5 us -> 15 us
  Pallas kernels: 21.7 us -> 24 us
  starting transfers between devices: 21.9 us -> 23 us
    ppermute x6, waiting for transfers between devices: 10.4 us -> 5.93 us  [send(): return lax.ppermute(value, ('grp', 'blk'), pairs)]
    pallas_call x3 -> x4, Pallas kernels: 12.8 us -> 15.1 us  [attend(): pl.pallas_call(functools.partial(attend_kernel, slots, held, placed), out...]
    ppermute x6, starting transfers between devices: 9.06 us -> 10.1 us  [send(): return lax.ppermute(value, ('grp', 'blk'), pairs)]
  transfers between devices with their start and end apart: 17 -> 17, of which waited for: 10 -> 10; matrix products, arithmetic and copies ran while one was open for 2% -> 2% of each run, Pallas kernels for 28% -> 32%
where the time goes in v6:
time: 64.9 us; the launch traced here: 64.7 us
  Pallas kernels  24 us (37%)
  starting transfers between devices  23 us (35%)
  waiting for transfers between devices  15 us (23%)
  other arithmetic  2.47 us (4%)
    pallas_call x4, Pallas kernels, attend(): pl.pallas_call(functools.partial(attend_kernel, slots, held, placed), out...  15.1 us
    ppermute x9, starting transfers between devices, across_chips(): lax.ppermute(value, 'blk', [(b, b ^ 2 * by) for b in range(blk_count)])  12.7 us
    ppermute x6, starting transfers between devices, send(): return lax.ppermute(value, ('grp', 'blk'), pairs)  10.1 us
    ppermute x6, waiting for transfers between devices, send(): return lax.ppermute(value, ('grp', 'blk'), pairs)  5.93 us
    ppermute x9, waiting for transfers between devices, across_chips(): lax.ppermute(value, 'blk', [(b, b ^ 2 * by) for b in range(blk_count)])  5.31 us
    ppermute x2, waiting for transfers between devices, with_other_core(): lax.ppermute(held, 'blk', [(b, b ^ 1) for b in range(blk_count)])  3.79 us
    pallas_call x2, Pallas kernels, query_rows(): pl.pallas_call(functools.partial(query_kernel, slots), out_shape=jax.Shap...  3.67 us
    pallas_call x3, Pallas kernels, key_value_rows(): pl.pallas_call(functools.partial(key_value_kernel, len(pieces), slots), o...  2.65 us
  transfers between devices with their start and end apart: 17, of which 10 were waited for; matrix products, arithmetic and copies ran while one was open for 2% of the time, Pallas kernels for 32%

profile of v6, /device:TPU:0, one launch (start us, length us, event | category | flops | bytes accessed | tf_op | source)
XLA Modules:
  0.0 64.7 jit_solution(12965408682351544741)
XLA Ops:
  0.0 2.9 %collective-permute-start = (bf16[64,4096]{1,0:T(8,128)(2,1)}, bf16[64,4096]{1,0:T(8,128)(2,1)S(1)}, u32[]{:S(2)}, u32[]{:S(2)}) collective-permute-start(bf16[64,4096]{1,0:T(8,128)(2,1)} %refs_0_.5), channel_id=1, source_target_pairs={{0,8},{1,17},{2,10},{3,19},{4,12},{5,21},{6,14},{7,23},{8,0},{9,25... | collective-permute-start | bytes 1572872 | tf_op jit(solution)/shard_map/ppermute | solution.py:360
  2.9 1.5 %collective-permute-start.1 = (bf16[64,4096]{1,0:T(8,128)(2,1)}, bf16[64,4096]{1,0:T(8,128)(2,1)S(1)}, u32[]{:S(2)}, u32[]{:S(2)}) collective-permute-start(bf16[64,4096]{1,0:T(8,128)(2,1)} %refs_0_.5), channel_id=1, source_target_pairs={{0,16},{1,9},{2,18},{3,11},{4,20},{5,13},{6,22},{7,15},{8,24},{9,1... | collective-permute-start | bytes 1572872 | tf_op jit(solution)/shard_map/ppermute | solution.py:360
  5.7 2.4 %preload.1 = (bf16[4096,256]{1,0:T(8,128)(2,1)S(1)}, bf16[4096,256]{1,0:T(8,128)(2,1)S(1)}) custom-call(bf16[4096,256]{1,0:T(8,128)(2,1)} %refs_0_.4, bf16[4096,256]{1,0:T(8,128)(2,1)} %refs_1_.2, f32[256,128]{1,0:T(8,128)S(1)} %get-tuple-element.18.refs_4_.refs_2_.refs_3_, f32[256,128]{1,0:T(8,128)S(1)} %get-tuple-element.17.refs_5_.refs_3_.refs_4_), custom_call_target="tpu_custom_call" | custom-call | tf_op jit(solution)/shard_map/preload/pallas_call | solution.py:46
  8.1 0.9 %key_value_rows.3 = bf16[64,512]{1,0:T(8,128)(2,1)S(1)} custom-call(bf16[64,4096]{1,0:T(8,128)(2,1)S(1)} %copy-done, bf16[4096,256]{1,0:T(8,128)(2,1)S(1)} %get-tuple-element.11.refs_1_.refs_2_, bf16[4096,256]{1,0:T(8,128)(2,1)S(1)} %get-tuple-element.12.refs_2_.refs_3_, f32[256,128]{1,0:T(8,128)S(1)} %get-tuple-element.18.refs_4_.refs_2_.refs_3_, ...), custom_call_target="tpu_custom_call" | custom-call | flops 268435456 | bytes 4194304 | tf_op jit(solution)/shard_map/key_value_rows/pallas_call | solution.py:103
  9.1 3.7 %collective-permute-start.2 = (bf16[64,512]{1,0:T(8,128)(2,1)S(1)}, bf16[64,512]{1,0:T(8,128)(2,1)S(1)}, u32[]{:S(2)}, u32[]{:S(2)}) collective-permute-start(bf16[64,512]{1,0:T(8,128)(2,1)S(1)} %key_value_rows.3), channel_id=1, source_target_pairs={{0,6},{1,7},{2,4},{3,5},{4,2},{5,3},{6,0},{7,1},{8,14},{9,15},{10,... | collective-permute-start | bytes 196616 | tf_op jit(solution)/shard_map/ppermute | solution.py:379
  12.7 0.8 %collective-permute-start.4 = (bf16[64,512]{1,0:T(8,128)(2,1)S(1)}, bf16[64,512]{1,0:T(8,128)(2,1)S(1)}, u32[]{:S(2)}, u32[]{:S(2)}) collective-permute-start(bf16[64,512]{1,0:T(8,128)(2,1)S(1)} %key_value_rows.3), channel_id=1, source_target_pairs={{0,4},{1,5},{2,6},{3,7},{4,0},{5,1},{6,2},{7,3},{8,12},{9,13},{10,... | collective-permute-start | bytes 196616 | tf_op jit(solution)/shard_map/ppermute | solution.py:379
  13.5 1.9 %collective-permute-done.refs_1_.refs_0_ = bf16[64,4096]{1,0:T(8,128)(2,1)S(1)} collective-permute-done((bf16[64,4096]{1,0:T(8,128)(2,1)}, bf16[64,4096]{1,0:T(8,128)(2,1)S(1)}, u32[]{:S(2)}, u32[]{:S(2)}) %collective-permute-start) | collective-permute-done | bytes 524320 | tf_op jit(solution)/shard_map/ppermute | solution.py:360
  15.5 1.4 %collective-permute-start.9 = (bf16[64,4096]{1,0:T(8,128)(2,1)S(1)}, bf16[64,4096]{1,0:T(8,128)(2,1)S(1)}, u32[]{:S(2)}, u32[]{:S(2)}) collective-permute-start(bf16[64,4096]{1,0:T(8,128)(2,1)S(1)} %collective-permute-done.refs_1_.refs_0_), channel_id=1, source_target_pairs={{0,16},{1,9},{2,18},{3,11},{4,20},{5,13},{6,22},{7,15},{8,24},{9,1... | collective-permute-start | bytes 1572872 | tf_op jit(solution)/shard_map/ppermute | solution.py:360
  17.1 0.8 %collective-permute-done.4 = bf16[64,512]{1,0:T(8,128)(2,1)S(1)} collective-permute-done((bf16[64,512]{1,0:T(8,128)(2,1)S(1)}, bf16[64,512]{1,0:T(8,128)(2,1)S(1)}, u32[]{:S(2)}, u32[]{:S(2)}) %collective-permute-start.4) | collective-permute-done | bytes 65568 | tf_op jit(solution)/shard_map/ppermute | solution.py:379
  18.0 1.5 %collective-permute-done.5.refs_7_.refs_1_ = bf16[4,64,512]{2,1,0:T(8,128)(2,1)S(1)} collective-permute-done((bf16[4,64,512]{2,1,0:T(8,128)(2,1)S(1)}, bf16[4,64,512]{2,1,0:T(8,128)(2,1)S(1)}, u32[]{:S(2)}, u32[]{:S(2)}) %collective-permute-start.5) | collective-permute-done | bytes 262176 | tf_op jit(solution)/shard_map/ppermute | solution.py:392
  19.5 0.8 %key_value_rows.4.refs_5_ = bf16[128,512]{1,0:T(8,128)(2,1)S(1)} custom-call(bf16[64,4096]{1,0:T(8,128)(2,1)S(1)} %collective-permute-done.refs_1_.refs_0_, bf16[64,4096]{1,0:T(8,128)(2,1)S(1)} %collective-permute-done.1.refs_2_.refs_1_, bf16[4096,256]{1,0:T(8,128)(2,1)S(1)} %get-tuple-element.11.refs_1_.refs_2_, ...), custom_call_target="tpu_custom_call" | custom-call | flops 536870912 | bytes 4194304 | tf_op jit(solution)/shard_map/key_value_rows/pallas_call | solution.py:103
  20.4 2.1 %collective-permute-start.6 = (bf16[128,512]{1,0:T(8,128)(2,1)S(1)}, bf16[128,512]{1,0:T(8,128)(2,1)S(1)}, u32[]{:S(2)}, u32[]{:S(2)}) collective-permute-start(bf16[128,512]{1,0:T(8,128)(2,1)S(1)} %key_value_rows.4.refs_5_), channel_id=1, source_target_pairs={{0,2},{1,3},{2,0},{3,1},{4,6},{5,7},{6,4},{7,5},{8,10},{9,11},{10,... | collective-permute-start | bytes 393224 | tf_op jit(solution)/shard_map/ppermute | solution.py:379
  22.4 1.4 %collective-permute-start.7 = (bf16[128,512]{1,0:T(8,128)(2,1)S(1)}, bf16[128,512]{1,0:T(8,128)(2,1)S(1)}, u32[]{:S(2)}, u32[]{:S(2)}) collective-permute-start(bf16[128,512]{1,0:T(8,128)(2,1)S(1)} %key_value_rows.4.refs_5_), channel_id=1, source_target_pairs={{0,6},{1,7},{2,4},{3,5},{4,2},{5,3},{6,0},{7,1},{8,14},{9,15},{10,... | collective-permute-start | bytes 393224 | tf_op jit(solution)/shard_map/ppermute | solution.py:379
  23.8 2.0 %query_rows.2.refs_6_.query_ref = bf16[192,1024]{1,0:T(8,128)(2,1)S(1)} custom-call(bf16[64,4096]{1,0:T(8,128)(2,1)S(1)} %copy-done, bf16[64,4096]{1,0:T(8,128)(2,1)S(1)} %collective-permute-done.refs_1_.refs_0_, bf16[64,4096]{1,0:T(8,128)(2,1)S(1)} %collective-permute-done.1.refs_2_.refs_1_, bf16[4096,1024]{1,0:T(8,128)(2,1)S(1)} %bitcast.15, ...), custom_call_target="tpu_custom_call" | custom-call | flops 1610612736 | bytes 8388608 | tf_op jit(solution)/shard_map/query_rows/pallas_call | solution.py:137
  25.9 0.9 %key_value_rows.5 = bf16[64,512]{1,0:T(8,128)(2,1)S(1)} custom-call(bf16[64,4096]{1,0:T(8,128)(2,1)S(1)} %collective-permute-done.9.refs_0_, bf16[4096,256]{1,0:T(8,128)(2,1)S(1)} %get-tuple-element.11.refs_1_.refs_2_, bf16[4096,256]{1,0:T(8,128)(2,1)S(1)} %get-tuple-element.12.refs_2_.refs_3_, f32[256,128]{1,0:T(8,128)S(1)} %get-tuple-element.18.refs_4_.refs_2_.refs_3_, ...), custom_call_target="tpu_custom_call" | custom-call | flops 268435456 | bytes 4194304 | tf_op jit(solution)/shard_map/key_value_rows/pallas_call | solution.py:103
  26.8 1.3 %collective-permute-start.11 = (bf16[64,512]{1,0:T(8,128)(2,1)S(1)}, bf16[64,512]{1,0:T(8,128)(2,1)S(1)}, u32[]{:S(2)}, u32[]{:S(2)}) collective-permute-start(bf16[64,512]{1,0:T(8,128)(2,1)S(1)} %key_value_rows.5), channel_id=1, source_target_pairs={{0,2},{1,3},{2,0},{3,1},{4,6},{5,7},{6,4},{7,5},{8,10},{9,11},{10,... | collective-permute-start | bytes 196616 | tf_op jit(solution)/shard_map/ppermute | solution.py:379
  28.1 2.6 %collective-permute-start.12 = (bf16[64,512]{1,0:T(8,128)(2,1)S(1)}, bf16[64,512]{1,0:T(8,128)(2,1)S(1)}, u32[]{:S(2)}, u32[]{:S(2)}) collective-permute-start(bf16[64,512]{1,0:T(8,128)(2,1)S(1)} %key_value_rows.5), channel_id=1, source_target_pairs={{0,4},{1,5},{2,6},{3,7},{4,0},{5,1},{6,2},{7,3},{8,12},{9,13},{10,... | collective-permute-start | bytes 196616 | tf_op jit(solution)/shard_map/ppermute | solution.py:379
  31.6 1.7 %query_rows.3.query_ref = bf16[64,1024]{1,0:T(8,128)(2,1)S(1)} custom-call(bf16[64,4096]{1,0:T(8,128)(2,1)S(1)} %collective-permute-done.9.refs_0_, bf16[4096,1024]{1,0:T(8,128)(2,1)S(1)} %bitcast.15, f32[256,128]{1,0:T(8,128)S(1)} %get-tuple-element.18.refs_4_.refs_2_.refs_3_, f32[256,128]{1,0:T(8,128)S(1)} %get-tuple-element.17.refs_5_.refs_3_.refs_4_), custom_call_target="tpu_custom_call" | custom-call | flops 536870912 | bytes 8388608 | tf_op jit(solution)/shard_map/query_rows/pallas_call | solution.py:137
  33.3 1.6 %collective-permute-done.12 = bf16[64,512]{1,0:T(8,128)(2,1)S(1)} collective-permute-done((bf16[64,512]{1,0:T(8,128)(2,1)S(1)}, bf16[64,512]{1,0:T(8,128)(2,1)S(1)}, u32[]{:S(2)}, u32[]{:S(2)}) %collective-permute-start.12) | collective-permute-done | bytes 65568 | tf_op jit(solution)/shard_map/ppermute | solution.py:379
  34.9 2.0 %collective-permute-done.10 = bf16[64,512]{1,0:T(8,128)(2,1)S(1)} collective-permute-done((bf16[64,512]{1,0:T(8,128)(2,1)S(1)}, bf16[64,512]{1,0:T(8,128)(2,1)S(1)}, u32[]{:S(2)}, u32[]{:S(2)}) %collective-permute-start.10) | collective-permute-done | bytes 65568 | tf_op jit(solution)/shard_map/ppermute | solution.py:379
  36.9 0.7 %collective-permute-done.8 = bf16[128,512]{1,0:T(8,128)(2,1)S(1)} collective-permute-done((bf16[128,512]{1,0:T(8,128)(2,1)S(1)}, bf16[128,512]{1,0:T(8,128)(2,1)S(1)}, u32[]{:S(2)}, u32[]{:S(2)}) %collective-permute-start.8) | collective-permute-done | bytes 131104 | tf_op jit(solution)/shard_map/ppermute | solution.py:379
  37.8 2.3 %collective-permute-done.13.refs_3_ = bf16[4,192,512]{2,1,0:T(8,128)(2,1)S(1)} collective-permute-done((bf16[4,192,512]{2,1,0:T(8,128)(2,1)S(1)}, bf16[4,192,512]{2,1,0:T(8,128)(2,1)S(1)}, u32[]{:S(2)}, u32[]{:S(2)}) %collective-permute-start.13) | collective-permute-done | bytes 786464 | tf_op jit(solution)/shard_map/ppermute | solution.py:392
  40.3 3.4 %attend_project.7 = bf16[64,4096]{1,0:T(8,128)(2,1)S(1)} custom-call(s32[2,16]{1,0:T(2,128)S(1)} %copy-done.1, bf16[64,1024]{1,0:T(8,128)(2,1)S(1)} %query_rows.3.query_ref, bf16[2048,512]{1,0:T(8,128)(2,1)S(1)} %key_value_gather.1.kv_ref, bf16[1024,4096]{1,0:T(8,128)(2,1)S(1)} %bitcast.13), custom_call_target="tpu_custom_call" | custom-call | flops 1073741824 | bytes 8388608 | tf_op jit(solution)/shard_map/attend_project/pallas_call | solution.py:299
  43.6 1.6 %collective-permute-start.15 = (bf16[64,4096]{1,0:T(8,128)(2,1)S(1)}, bf16[64,4096]{1,0:T(8,128)(2,1)S(1)}, u32[]{:S(2)}, u32[]{:S(2)}) collective-permute-start(bf16[64,4096]{1,0:T(8,128)(2,1)S(1)} %attend_project.7), channel_id=1, source_target_pairs={{0,16},{1,9},{2,18},{3,11},{4,20},{5,13},{6,22},{7,15},{8,24},{9,1... | collective-permute-start | bytes 1572872 | tf_op jit(solution)/shard_map/ppermute | solution.py:360
  45.2 3.6 %attend_project.5 = bf16[64,4096]{1,0:T(8,128)(2,1)S(1)} custom-call(s32[2,16]{1,0:T(2,128)S(1)} %copy-done.1, bf16[192,1024]{1,0:T(8,128)(2,1)S(1)} %query_rows.2.refs_6_.query_ref, bf16[2048,512]{1,0:T(8,128)(2,1)S(1)} %key_value_gather.1.kv_ref, bf16[1024,4096]{1,0:T(8,128)(2,1)S(1)} %bitcast.13), custom_call_target="tpu_custom_call" | custom-call | flops 1073741824 | bytes 8388608 | tf_op jit(solution)/shard_map/attend_project/pallas_call | solution.py:299
  48.8 1.4 %collective-permute-start.14 = (bf16[64,4096]{1,0:T(8,128)(2,1)S(1)}, bf16[64,4096]{1,0:T(8,128)(2,1)S(1)}, u32[]{:S(2)}, u32[]{:S(2)}) collective-permute-start(bf16[64,4096]{1,0:T(8,128)(2,1)S(1)} %attend_project.5), channel_id=1, source_target_pairs={{0,16},{1,9},{2,18},{3,11},{4,20},{5,13},{6,22},{7,15},{8,24},{9,1... | collective-permute-start | bytes 1572872 | tf_op jit(solution)/shard_map/ppermute | solution.py:360
  50.3 4.1 %attend_project.6 = bf16[64,4096]{1,0:T(8,128)(2,1)S(1)} custom-call(s32[2,16]{1,0:T(2,128)S(1)} %copy-done.1, bf16[192,1024]{1,0:T(8,128)(2,1)S(1)} %query_rows.2.refs_6_.query_ref, bf16[2048,512]{1,0:T(8,128)(2,1)S(1)} %key_value_gather.1.kv_ref, bf16[1024,4096]{1,0:T(8,128)(2,1)S(1)} %bitcast.13), custom_call_target="tpu_custom_call" | custom-call | flops 1073741824 | bytes 8388608 | tf_op jit(solution)/shard_map/attend_project/pallas_call | solution.py:299
  54.5 1.2 %collective-permute-start.16 = (bf16[64,4096]{1,0:T(8,128)(2,1)S(1)}, bf16[64,4096]{1,0:T(8,128)(2,1)S(1)}, u32[]{:S(2)}, u32[]{:S(2)}) collective-permute-start(bf16[64,4096]{1,0:T(8,128)(2,1)S(1)} %add_convert_fusion.1), channel_id=1, source_target_pairs={{0,8},{1,17},{2,10},{3,19},{4,12},{5,21},{6,14},{7,23},{8,0},{9,25... | collective-permute-start | bytes 1572872 | tf_op jit(solution)/shard_map/ppermute | solution.py:360
  55.7 4.0 %attend_project.4 = bf16[64,4096]{1,0:T(8,128)(2,1)S(1)} custom-call(s32[2,16]{1,0:T(2,128)S(1)} %copy-done.1, bf16[192,1024]{1,0:T(8,128)(2,1)S(1)} %query_rows.2.refs_6_.query_ref, bf16[2048,512]{1,0:T(8,128)(2,1)S(1)} %key_value_gather.1.kv_ref, bf16[1024,4096]{1,0:T(8,128)(2,1)S(1)} %bitcast.13), custom_call_target="tpu_custom_call" | custom-call | flops 1073741824 | bytes 8388608 | tf_op jit(solution)/shard_map/attend_project/pallas_call | solution.py:299
  59.7 2.0 %collective-permute-done.14 = bf16[64,4096]{1,0:T(8,128)(2,1)S(1)} collective-permute-done((bf16[64,4096]{1,0:T(8,128)(2,1)S(1)}, bf16[64,4096]{1,0:T(8,128)(2,1)S(1)}, u32[]{:S(2)}, u32[]{:S(2)}) %collective-permute-start.14) | collective-permute-done | bytes 524320 | tf_op jit(solution)/shard_map/ppermute | solution.py:360
  61.8 1.9 %collective-permute-done.16 = bf16[64,4096]{1,0:T(8,128)(2,1)S(1)} collective-permute-done((bf16[64,4096]{1,0:T(8,128)(2,1)S(1)}, bf16[64,4096]{1,0:T(8,128)(2,1)S(1)}, u32[]{:S(2)}, u32[]{:S(2)}) %collective-permute-start.16) | collective-permute-done | bytes 524320 | tf_op jit(solution)/shard_map/ppermute | solution.py:360
  63.7 1.0 %add_convert_fusion = bf16[64,4096]{1,0:T(8,128)(2,1)} fusion(bf16[64,4096]{1,0:T(8,128)(2,1)S(1)} %collective-permute-done.16, bf16[64,4096]{1,0:T(8,128)(2,1)S(1)} %collective-permute-done.14, bf16[64,4096]{1,0:T(8,128)(2,1)S(1)} %attend_project.4), kind=kLoop, calls=%fused_computation | loop fusion | flops 1572864 | bytes 2097152 | tf_op jit(solution)/shard_map/convert_element_type | solution.py:333
  (35 shorter events, 3.1 us)
Async XLA Ops:
  0.0 15.5 %collective-permute-start = (bf16[64,4096]{1,0:T(8,128)(2,1)}, bf16[64,4096]{1,0:T(8,128)(2,1)S(1)}, u32[]{:S(2)}, u32[]{:S(2)}) collective-permute-start(bf16[64,4096]{1,0:T(8,128)(2,1)} %refs_0_.5), channel_id=1, source_target_pairs={{0,8},{1,17},{2,10},{3,19},{4,12},{5,21},{6,14},{7,23},{8,0},{9,25... | collective-permute-start | bytes 1572872 | tf_op jit(solution)/shard_map/ppermute | solution.py:360
  2.9 16.6 %collective-permute-start.1 = (bf16[64,4096]{1,0:T(8,128)(2,1)}, bf16[64,4096]{1,0:T(8,128)(2,1)S(1)}, u32[]{:S(2)}, u32[]{:S(2)}) collective-permute-start(bf16[64,4096]{1,0:T(8,128)(2,1)} %refs_0_.5), channel_id=1, source_target_pairs={{0,16},{1,9},{2,18},{3,11},{4,20},{5,13},{6,22},{7,15},{8,24},{9,1... | collective-permute-start | bytes 1572872 | tf_op jit(solution)/shard_map/ppermute | solution.py:360
  5.2 3.0 %copy-start = (bf16[64,4096]{1,0:T(8,128)(2,1)S(1)}, bf16[64,4096]{1,0:T(8,128)(2,1)}, u32[]{:S(2)}) copy-start(bf16[64,4096]{1,0:T(8,128)(2,1)} %refs_0_.5) | copy-start | bytes 1572868
  5.7 18.1 %slice-start.2 = ((s8[8388608]{0:T(1024)(128)(4,1)}), s8[4194304]{0:T(1024)(128)(4,1)S(1)}, s32[]{:S(2)}) async-start(s8[8388608]{0:T(1024)(128)(4,1)} %bitcast.14), calls=%async_computation.2 | async-start | bytes 8388608
  8.1 15.7 %slice-start.3 = ((s8[8388608]{0:T(1024)(128)(4,1)}), s8[4194304]{0:T(1024)(128)(4,1)S(1)}, s32[]{:S(2)}) async-start(s8[8388608]{0:T(1024)(128)(4,1)} %bitcast.14), calls=%async_computation.3 | async-start | bytes 8388608
  9.1 7.8 %collective-permute-start.2 = (bf16[64,512]{1,0:T(8,128)(2,1)S(1)}, bf16[64,512]{1,0:T(8,128)(2,1)S(1)}, u32[]{:S(2)}, u32[]{:S(2)}) collective-permute-start(bf16[64,512]{1,0:T(8,128)(2,1)S(1)} %key_value_rows.3), channel_id=1, source_target_pairs={{0,6},{1,7},{2,4},{3,5},{4,2},{5,3},{6,0},{7,1},{8,14},{9,15},{10,... | collective-permute-start | bytes 196616 | tf_op jit(solution)/shard_map/ppermute | solution.py:379
  12.7 4.4 %collective-permute-start.3 = (bf16[64,512]{1,0:T(8,128)(2,1)S(1)}, bf16[64,512]{1,0:T(8,128)(2,1)S(1)}, u32[]{:S(2)}, u32[]{:S(2)}) collective-permute-start(bf16[64,512]{1,0:T(8,128)(2,1)S(1)} %key_value_rows.3), channel_id=1, source_target_pairs={{0,2},{1,3},{2,0},{3,1},{4,6},{5,7},{6,4},{7,5},{8,10},{9,11},{10,... | collective-permute-start | bytes 196616 | tf_op jit(solution)/shard_map/ppermute | solution.py:379
  12.7 5.2 %collective-permute-start.4 = (bf16[64,512]{1,0:T(8,128)(2,1)S(1)}, bf16[64,512]{1,0:T(8,128)(2,1)S(1)}, u32[]{:S(2)}, u32[]{:S(2)}) collective-permute-start(bf16[64,512]{1,0:T(8,128)(2,1)S(1)} %key_value_rows.3), channel_id=1, source_target_pairs={{0,4},{1,5},{2,6},{3,7},{4,0},{5,1},{6,2},{7,3},{8,12},{9,13},{10,... | collective-permute-start | bytes 196616 | tf_op jit(solution)/shard_map/ppermute | solution.py:379
  15.5 10.4 %collective-permute-start.9 = (bf16[64,4096]{1,0:T(8,128)(2,1)S(1)}, bf16[64,4096]{1,0:T(8,128)(2,1)S(1)}, u32[]{:S(2)}, u32[]{:S(2)}) collective-permute-start(bf16[64,4096]{1,0:T(8,128)(2,1)S(1)} %collective-permute-done.refs_1_.refs_0_), channel_id=1, source_target_pairs={{0,16},{1,9},{2,18},{3,11},{4,20},{5,13},{6,22},{7,15},{8,24},{9,1... | collective-permute-start | bytes 1572872 | tf_op jit(solution)/shard_map/ppermute | solution.py:360
  17.9 1.6 %collective-permute-start.5 = (bf16[4,64,512]{2,1,0:T(8,128)(2,1)S(1)}, bf16[4,64,512]{2,1,0:T(8,128)(2,1)S(1)}, u32[]{:S(2)}, u32[]{:S(2)}) collective-permute-start(bf16[4,64,512]{2,1,0:T(8,128)(2,1)S(1)} %pad_maximum_fusion.1.refs_6_.refs_0_), channel_id=1, source_target_pairs={{0,1},{1,0},{2,3},{3,2},{4,5},{5,4},{6,7},{7,6},{8,9},{9,8},{10,11... | collective-permute-start | bytes 786440 | tf_op jit(solution)/shard_map/ppermute | solution.py:392
  20.4 10.9 %collective-permute-start.6 = (bf16[128,512]{1,0:T(8,128)(2,1)S(1)}, bf16[128,512]{1,0:T(8,128)(2,1)S(1)}, u32[]{:S(2)}, u32[]{:S(2)}) collective-permute-start(bf16[128,512]{1,0:T(8,128)(2,1)S(1)} %key_value_rows.4.refs_5_), channel_id=1, source_target_pairs={{0,2},{1,3},{2,0},{3,1},{4,6},{5,7},{6,4},{7,5},{8,10},{9,11},{10,... | collective-permute-start | bytes 393224 | tf_op jit(solution)/shard_map/ppermute | solution.py:379
  22.4 8.8 %collective-permute-start.7 = (bf16[128,512]{1,0:T(8,128)(2,1)S(1)}, bf16[128,512]{1,0:T(8,128)(2,1)S(1)}, u32[]{:S(2)}, u32[]{:S(2)}) collective-permute-start(bf16[128,512]{1,0:T(8,128)(2,1)S(1)} %key_value_rows.4.refs_5_), channel_id=1, source_target_pairs={{0,6},{1,7},{2,4},{3,5},{4,2},{5,3},{6,0},{7,1},{8,14},{9,15},{10,... | collective-permute-start | bytes 393224 | tf_op jit(solution)/shard_map/ppermute | solution.py:379
  25.8 14.4 %slice-start = ((s8[8388608]{0:T(1024)(128)(4,1)}), s8[4194304]{0:T(1024)(128)(4,1)S(1)}, s32[]{:S(2)}) async-start(s8[8388608]{0:T(1024)(128)(4,1)} %bitcast.12), calls=%async_computation | async-start | bytes 8388608
  26.8 13.5 %slice-start.1 = ((s8[8388608]{0:T(1024)(128)(4,1)}), s8[4194304]{0:T(1024)(128)(4,1)S(1)}, s32[]{:S(2)}) async-start(s8[8388608]{0:T(1024)(128)(4,1)} %bitcast.12), calls=%async_computation.1 | async-start | bytes 8388608
  26.8 6.5 %collective-permute-start.11 = (bf16[64,512]{1,0:T(8,128)(2,1)S(1)}, bf16[64,512]{1,0:T(8,128)(2,1)S(1)}, u32[]{:S(2)}, u32[]{:S(2)}) collective-permute-start(bf16[64,512]{1,0:T(8,128)(2,1)S(1)} %key_value_rows.5), channel_id=1, source_target_pairs={{0,2},{1,3},{2,0},{3,1},{4,6},{5,7},{6,4},{7,5},{8,10},{9,11},{10,... | collective-permute-start | bytes 196616 | tf_op jit(solution)/shard_map/ppermute | solution.py:379
  28.1 6.8 %collective-permute-start.12 = (bf16[64,512]{1,0:T(8,128)(2,1)S(1)}, bf16[64,512]{1,0:T(8,128)(2,1)S(1)}, u32[]{:S(2)}, u32[]{:S(2)}) collective-permute-start(bf16[64,512]{1,0:T(8,128)(2,1)S(1)} %key_value_rows.5), channel_id=1, source_target_pairs={{0,4},{1,5},{2,6},{3,7},{4,0},{5,1},{6,2},{7,3},{8,12},{9,13},{10,... | collective-permute-start | bytes 196616 | tf_op jit(solution)/shard_map/ppermute | solution.py:379
  30.7 6.2 %collective-permute-start.10 = (bf16[64,512]{1,0:T(8,128)(2,1)S(1)}, bf16[64,512]{1,0:T(8,128)(2,1)S(1)}, u32[]{:S(2)}, u32[]{:S(2)}) collective-permute-start(bf16[64,512]{1,0:T(8,128)(2,1)S(1)} %key_value_rows.5), channel_id=1, source_target_pairs={{0,6},{1,7},{2,4},{3,5},{4,2},{5,3},{6,0},{7,1},{8,14},{9,15},{10,... | collective-permute-start | bytes 196616 | tf_op jit(solution)/shard_map/ppermute | solution.py:379
  31.3 6.3 %collective-permute-start.8 = (bf16[128,512]{1,0:T(8,128)(2,1)S(1)}, bf16[128,512]{1,0:T(8,128)(2,1)S(1)}, u32[]{:S(2)}, u32[]{:S(2)}) collective-permute-start(bf16[128,512]{1,0:T(8,128)(2,1)S(1)} %collective-permute-done.7), channel_id=1, source_target_pairs={{0,2},{1,3},{2,0},{3,1},{4,6},{5,7},{6,4},{7,5},{8,10},{9,11},{10,... | collective-permute-start | bytes 393224 | tf_op jit(solution)/shard_map/ppermute | solution.py:379
  37.7 2.6 %copy-start.1 = (s32[2,16]{1,0:T(2,128)S(1)}, s32[2,16]{1,0:T(2,128)}, u32[]{:S(2)}) copy-start(s32[2,16]{1,0:T(2,128)} %mask_ref.7) | copy-start | bytes 388
  37.7 2.4 %collective-permute-start.13 = (bf16[4,192,512]{2,1,0:T(8,128)(2,1)S(1)}, bf16[4,192,512]{2,1,0:T(8,128)(2,1)S(1)}, u32[]{:S(2)}, u32[]{:S(2)}) collective-permute-start(bf16[4,192,512]{2,1,0:T(8,128)(2,1)S(1)} %pad_maximum_fusion.refs_2_), channel_id=1, source_target_pairs={{0,1},{1,0},{2,3},{3,2},{4,5},{5,4},{6,7},{7,6},{8,9},{9,8},{10,11... | collective-permute-start | bytes 2359304 | tf_op jit(solution)/shard_map/ppermute | solution.py:392
  43.6 10.7 %collective-permute-start.15 = (bf16[64,4096]{1,0:T(8,128)(2,1)S(1)}, bf16[64,4096]{1,0:T(8,128)(2,1)S(1)}, u32[]{:S(2)}, u32[]{:S(2)}) collective-permute-start(bf16[64,4096]{1,0:T(8,128)(2,1)S(1)} %attend_project.7), channel_id=1, source_target_pairs={{0,16},{1,9},{2,18},{3,11},{4,20},{5,13},{6,22},{7,15},{8,24},{9,1... | collective-permute-start | bytes 1572872 | tf_op jit(solution)/shard_map/ppermute | solution.py:360
  48.8 12.9 %collective-permute-start.14 = (bf16[64,4096]{1,0:T(8,128)(2,1)S(1)}, bf16[64,4096]{1,0:T(8,128)(2,1)S(1)}, u32[]{:S(2)}, u32[]{:S(2)}) collective-permute-start(bf16[64,4096]{1,0:T(8,128)(2,1)S(1)} %attend_project.5), channel_id=1, source_target_pairs={{0,16},{1,9},{2,18},{3,11},{4,20},{5,13},{6,22},{7,15},{8,24},{9,1... | collective-permute-start | bytes 1572872 | tf_op jit(solution)/shard_map/ppermute | solution.py:360
  54.5 9.2 %collective-permute-start.16 = (bf16[64,4096]{1,0:T(8,128)(2,1)S(1)}, bf16[64,4096]{1,0:T(8,128)(2,1)S(1)}, u32[]{:S(2)}, u32[]{:S(2)}) collective-permute-start(bf16[64,4096]{1,0:T(8,128)(2,1)S(1)} %add_convert_fusion.1), channel_id=1, source_target_pairs={{0,8},{1,17},{2,10},{3,19},{4,12},{5,21},{6,14},{7,23},{8,0},{9,25... | collective-permute-start | bytes 1572872 | tf_op jit(solution)/shard_map/ppermute | solution.py:360

commit v7 on v6

--- a/solution.py
+++ b/solution.py
@@ -14,6 +14,7 @@
 NEG_FILL = -1e30
 QUERY_COLS = 1024
 WIDE = 8
+MOST = 7
 SURE = 6
 QUERY_FACTOR = HEAD_WIDTH**-0.5 * math.log2(math.e)
 ANY = pl.BlockSpec(memory_space=pl.ANY)
@@ -182,10 +183,10 @@
         ]
         ones = jnp.ones((WIDE * block, HEAD_WIDTH), jnp.bfloat16)
 
-        def step(index, state, queries=queries, count=count):
+        def step(index, state, queries=queries, count=count, width=WIDE):
             first = index * WIDE
             starts = [
-                pl.multiple_of(live_ref[first + wide] * block, block) for wide in range(WIDE)
+                pl.multiple_of(live_ref[first + wide] * block, block) for wide in range(width)
             ]
             new_state = []
             for head, query in enumerate(queries):
@@ -207,7 +208,7 @@
                     + [
                         scores[:, wide * block : (wide + 1) * block]
                         + jnp.where(first + wide < count, 0.0, NEG_FILL)
-                        for wide in range(SURE, WIDE)
+                        for wide in range(SURE, width)
                     ],
                     axis=1,
                 )
@@ -217,7 +218,7 @@
                 weights = jnp.exp2(scores - top).astype(jnp.bfloat16)
                 sums = jnp.dot(
                     weights,
-                    jnp.concatenate([values, ones], axis=1),
+                    jnp.concatenate([values, ones[: width * block]], axis=1),
                     preferred_element_type=jnp.float32,
                 )
                 if state is not None:
@@ -237,7 +238,7 @@
                 ]
             return lax.fori_loop(2, (count + WIDE - 1) // WIDE, step, tuple(state))
 
-        state = lax.cond(count > WIDE, many_steps, functools.partial(step, 0, None))
+        state = lax.cond(count > MOST, many_steps, functools.partial(step, 0, None, width=MOST))
         for head in range(kv_heads):
             sums = state[2 * head + 1]
             mixed = (sums[:, :HEAD_WIDTH] / sums[:, HEAD_WIDTH:]).astype(jnp.bfloat16)

time: 64.9 us -> 64.7 us (level)
  transfers between devices with their start and end apart: 17 -> 17, of which waited for: 10 -> 10; matrix products, arithmetic and copies ran while one was open for 2% -> 2% of each run, Pallas kernels for 32% -> 31%
where the time goes in v7:
time: 64.7 us; the launch traced here: 64.5 us
  Pallas kernels  23.6 us (36%)
  starting transfers between devices  23.1 us (36%)
  waiting for transfers between devices  15 us (23%)
  other arithmetic  2.47 us (4%)
    pallas_call x4, Pallas kernels, attend(): pl.pallas_call(functools.partial(attend_kernel, slots, held, placed), out...  14.7 us
    ppermute x9, starting transfers between devices, across_chips(): lax.ppermute(value, 'blk', [(b, b ^ 2 * by) for b in range(blk_count)])  12.7 us
    ppermute x6, starting transfers between devices, send(): return lax.ppermute(value, ('grp', 'blk'), pairs)  10.3 us
    ppermute x6, waiting for transfers between devices, send(): return lax.ppermute(value, ('grp', 'blk'), pairs)  5.91 us
    ppermute x9, waiting for transfers between devices, across_chips(): lax.ppermute(value, 'blk', [(b, b ^ 2 * by) for b in range(blk_count)])  5.31 us
    ppermute x2, waiting for transfers between devices, with_other_core(): lax.ppermute(held, 'blk', [(b, b ^ 1) for b in range(blk_count)])  3.79 us
    pallas_call x2, Pallas kernels, query_rows(): pl.pallas_call(functools.partial(query_kernel, slots), out_shape=jax.Shap...  3.67 us
    pallas_call x3, Pallas kernels, key_value_rows(): pl.pallas_call(functools.partial(key_value_kernel, len(pieces), slots), o...  2.65 us
  transfers between devices with their start and end apart: 17, of which 10 were waited for; matrix products, arithmetic and copies ran while one was open for 2% of the time, Pallas kernels for 31%

profile of v7, /device:TPU:0, one launch (start us, length us, event | category | flops | bytes accessed | tf_op | source)
XLA Modules:
  0.0 64.5 jit_solution(17134091993636935426)
XLA Ops:
  0.0 2.9 %collective-permute-start = (bf16[64,4096]{1,0:T(8,128)(2,1)}, bf16[64,4096]{1,0:T(8,128)(2,1)S(1)}, u32[]{:S(2)}, u32[]{:S(2)}) collective-permute-start(bf16[64,4096]{1,0:T(8,128)(2,1)} %refs_0_.5), channel_id=1, source_target_pairs={{0,8},{1,17},{2,10},{3,19},{4,12},{5,21},{6,14},{7,23},{8,0},{9,25... | collective-permute-start | bytes 1572872 | tf_op jit(solution)/shard_map/ppermute | solution.py:361
  2.9 1.5 %collective-permute-start.1 = (bf16[64,4096]{1,0:T(8,128)(2,1)}, bf16[64,4096]{1,0:T(8,128)(2,1)S(1)}, u32[]{:S(2)}, u32[]{:S(2)}) collective-permute-start(bf16[64,4096]{1,0:T(8,128)(2,1)} %refs_0_.5), channel_id=1, source_target_pairs={{0,16},{1,9},{2,18},{3,11},{4,20},{5,13},{6,22},{7,15},{8,24},{9,1... | collective-permute-start | bytes 1572872 | tf_op jit(solution)/shard_map/ppermute | solution.py:361
  5.7 2.4 %preload.1 = (bf16[4096,256]{1,0:T(8,128)(2,1)S(1)}, bf16[4096,256]{1,0:T(8,128)(2,1)S(1)}) custom-call(bf16[4096,256]{1,0:T(8,128)(2,1)} %refs_0_.4, bf16[4096,256]{1,0:T(8,128)(2,1)} %refs_1_.2, f32[256,128]{1,0:T(8,128)S(1)} %get-tuple-element.18.refs_4_.refs_2_.refs_3_, f32[256,128]{1,0:T(8,128)S(1)} %get-tuple-element.17.refs_5_.refs_3_.refs_4_), custom_call_target="tpu_custom_call" | custom-call | tf_op jit(solution)/shard_map/preload/pallas_call | solution.py:47
  8.1 0.9 %key_value_rows.3 = bf16[64,512]{1,0:T(8,128)(2,1)S(1)} custom-call(bf16[64,4096]{1,0:T(8,128)(2,1)S(1)} %copy-done, bf16[4096,256]{1,0:T(8,128)(2,1)S(1)} %get-tuple-element.11.refs_1_.refs_2_, bf16[4096,256]{1,0:T(8,128)(2,1)S(1)} %get-tuple-element.12.refs_2_.refs_3_, f32[256,128]{1,0:T(8,128)S(1)} %get-tuple-element.18.refs_4_.refs_2_.refs_3_, ...), custom_call_target="tpu_custom_call" | custom-call | flops 268435456 | bytes 4194304 | tf_op jit(solution)/shard_map/key_value_rows/pallas_call | solution.py:104
  9.1 3.7 %collective-permute-start.2 = (bf16[64,512]{1,0:T(8,128)(2,1)S(1)}, bf16[64,512]{1,0:T(8,128)(2,1)S(1)}, u32[]{:S(2)}, u32[]{:S(2)}) collective-permute-start(bf16[64,512]{1,0:T(8,128)(2,1)S(1)} %key_value_rows.3), channel_id=1, source_target_pairs={{0,6},{1,7},{2,4},{3,5},{4,2},{5,3},{6,0},{7,1},{8,14},{9,15},{10,... | collective-permute-start | bytes 196616 | tf_op jit(solution)/shard_map/ppermute | solution.py:380
  12.7 0.8 %collective-permute-start.4 = (bf16[64,512]{1,0:T(8,128)(2,1)S(1)}, bf16[64,512]{1,0:T(8,128)(2,1)S(1)}, u32[]{:S(2)}, u32[]{:S(2)}) collective-permute-start(bf16[64,512]{1,0:T(8,128)(2,1)S(1)} %key_value_rows.3), channel_id=1, source_target_pairs={{0,4},{1,5},{2,6},{3,7},{4,0},{5,1},{6,2},{7,3},{8,12},{9,13},{10,... | collective-permute-start | bytes 196616 | tf_op jit(solution)/shard_map/ppermute | solution.py:380
  13.5 1.9 %collective-permute-done.refs_1_.refs_0_ = bf16[64,4096]{1,0:T(8,128)(2,1)S(1)} collective-permute-done((bf16[64,4096]{1,0:T(8,128)(2,1)}, bf16[64,4096]{1,0:T(8,128)(2,1)S(1)}, u32[]{:S(2)}, u32[]{:S(2)}) %collective-permute-start) | collective-permute-done | bytes 524320 | tf_op jit(solution)/shard_map/ppermute | solution.py:361
  15.5 1.4 %collective-permute-start.9 = (bf16[64,4096]{1,0:T(8,128)(2,1)S(1)}, bf16[64,4096]{1,0:T(8,128)(2,1)S(1)}, u32[]{:S(2)}, u32[]{:S(2)}) collective-permute-start(bf16[64,4096]{1,0:T(8,128)(2,1)S(1)} %collective-permute-done.refs_1_.refs_0_), channel_id=1, source_target_pairs={{0,16},{1,9},{2,18},{3,11},{4,20},{5,13},{6,22},{7,15},{8,24},{9,1... | collective-permute-start | bytes 1572872 | tf_op jit(solution)/shard_map/ppermute | solution.py:361
  17.1 0.8 %collective-permute-done.4 = bf16[64,512]{1,0:T(8,128)(2,1)S(1)} collective-permute-done((bf16[64,512]{1,0:T(8,128)(2,1)S(1)}, bf16[64,512]{1,0:T(8,128)(2,1)S(1)}, u32[]{:S(2)}, u32[]{:S(2)}) %collective-permute-start.4) | collective-permute-done | bytes 65568 | tf_op jit(solution)/shard_map/ppermute | solution.py:380
  18.0 1.5 %collective-permute-done.5.refs_7_.refs_1_ = bf16[4,64,512]{2,1,0:T(8,128)(2,1)S(1)} collective-permute-done((bf16[4,64,512]{2,1,0:T(8,128)(2,1)S(1)}, bf16[4,64,512]{2,1,0:T(8,128)(2,1)S(1)}, u32[]{:S(2)}, u32[]{:S(2)}) %collective-permute-start.5) | collective-permute-done | bytes 262176 | tf_op jit(solution)/shard_map/ppermute | solution.py:393
  19.5 0.8 %key_value_rows.4.refs_5_ = bf16[128,512]{1,0:T(8,128)(2,1)S(1)} custom-call(bf16[64,4096]{1,0:T(8,128)(2,1)S(1)} %collective-permute-done.refs_1_.refs_0_, bf16[64,4096]{1,0:T(8,128)(2,1)S(1)} %collective-permute-done.1.refs_2_.refs_1_, bf16[4096,256]{1,0:T(8,128)(2,1)S(1)} %get-tuple-element.11.refs_1_.refs_2_, ...), custom_call_target="tpu_custom_call" | custom-call | flops 536870912 | bytes 4194304 | tf_op jit(solution)/shard_map/key_value_rows/pallas_call | solution.py:104
  20.4 2.1 %collective-permute-start.6 = (bf16[128,512]{1,0:T(8,128)(2,1)S(1)}, bf16[128,512]{1,0:T(8,128)(2,1)S(1)}, u32[]{:S(2)}, u32[]{:S(2)}) collective-permute-start(bf16[128,512]{1,0:T(8,128)(2,1)S(1)} %key_value_rows.4.refs_5_), channel_id=1, source_target_pairs={{0,2},{1,3},{2,0},{3,1},{4,6},{5,7},{6,4},{7,5},{8,10},{9,11},{10,... | collective-permute-start | bytes 393224 | tf_op jit(solution)/shard_map/ppermute | solution.py:380
  22.4 1.4 %collective-permute-start.7 = (bf16[128,512]{1,0:T(8,128)(2,1)S(1)}, bf16[128,512]{1,0:T(8,128)(2,1)S(1)}, u32[]{:S(2)}, u32[]{:S(2)}) collective-permute-start(bf16[128,512]{1,0:T(8,128)(2,1)S(1)} %key_value_rows.4.refs_5_), channel_id=1, source_target_pairs={{0,6},{1,7},{2,4},{3,5},{4,2},{5,3},{6,0},{7,1},{8,14},{9,15},{10,... | collective-permute-start | bytes 393224 | tf_op jit(solution)/shard_map/ppermute | solution.py:380
  23.8 2.0 %query_rows.2.refs_6_.query_ref = bf16[192,1024]{1,0:T(8,128)(2,1)S(1)} custom-call(bf16[64,4096]{1,0:T(8,128)(2,1)S(1)} %copy-done, bf16[64,4096]{1,0:T(8,128)(2,1)S(1)} %collective-permute-done.refs_1_.refs_0_, bf16[64,4096]{1,0:T(8,128)(2,1)S(1)} %collective-permute-done.1.refs_2_.refs_1_, bf16[4096,1024]{1,0:T(8,128)(2,1)S(1)} %bitcast.15, ...), custom_call_target="tpu_custom_call" | custom-call | flops 1610612736 | bytes 8388608 | tf_op jit(solution)/shard_map/query_rows/pallas_call | solution.py:138
  25.9 0.9 %key_value_rows.5 = bf16[64,512]{1,0:T(8,128)(2,1)S(1)} custom-call(bf16[64,4096]{1,0:T(8,128)(2,1)S(1)} %collective-permute-done.9.refs_0_, bf16[4096,256]{1,0:T(8,128)(2,1)S(1)} %get-tuple-element.11.refs_1_.refs_2_, bf16[4096,256]{1,0:T(8,128)(2,1)S(1)} %get-tuple-element.12.refs_2_.refs_3_, f32[256,128]{1,0:T(8,128)S(1)} %get-tuple-element.18.refs_4_.refs_2_.refs_3_, ...), custom_call_target="tpu_custom_call" | custom-call | flops 268435456 | bytes 4194304 | tf_op jit(solution)/shard_map/key_value_rows/pallas_call | solution.py:104
  26.8 1.3 %collective-permute-start.11 = (bf16[64,512]{1,0:T(8,128)(2,1)S(1)}, bf16[64,512]{1,0:T(8,128)(2,1)S(1)}, u32[]{:S(2)}, u32[]{:S(2)}) collective-permute-start(bf16[64,512]{1,0:T(8,128)(2,1)S(1)} %key_value_rows.5), channel_id=1, source_target_pairs={{0,2},{1,3},{2,0},{3,1},{4,6},{5,7},{6,4},{7,5},{8,10},{9,11},{10,... | collective-permute-start | bytes 196616 | tf_op jit(solution)/shard_map/ppermute | solution.py:380
  28.1 2.6 %collective-permute-start.12 = (bf16[64,512]{1,0:T(8,128)(2,1)S(1)}, bf16[64,512]{1,0:T(8,128)(2,1)S(1)}, u32[]{:S(2)}, u32[]{:S(2)}) collective-permute-start(bf16[64,512]{1,0:T(8,128)(2,1)S(1)} %key_value_rows.5), channel_id=1, source_target_pairs={{0,4},{1,5},{2,6},{3,7},{4,0},{5,1},{6,2},{7,3},{8,12},{9,13},{10,... | collective-permute-start | bytes 196616 | tf_op jit(solution)/shard_map/ppermute | solution.py:380
  31.6 1.7 %query_rows.3.query_ref = bf16[64,1024]{1,0:T(8,128)(2,1)S(1)} custom-call(bf16[64,4096]{1,0:T(8,128)(2,1)S(1)} %collective-permute-done.9.refs_0_, bf16[4096,1024]{1,0:T(8,128)(2,1)S(1)} %bitcast.15, f32[256,128]{1,0:T(8,128)S(1)} %get-tuple-element.18.refs_4_.refs_2_.refs_3_, f32[256,128]{1,0:T(8,128)S(1)} %get-tuple-element.17.refs_5_.refs_3_.refs_4_), custom_call_target="tpu_custom_call" | custom-call | flops 536870912 | bytes 8388608 | tf_op jit(solution)/shard_map/query_rows/pallas_call | solution.py:138
  33.3 1.6 %collective-permute-done.12 = bf16[64,512]{1,0:T(8,128)(2,1)S(1)} collective-permute-done((bf16[64,512]{1,0:T(8,128)(2,1)S(1)}, bf16[64,512]{1,0:T(8,128)(2,1)S(1)}, u32[]{:S(2)}, u32[]{:S(2)}) %collective-permute-start.12) | collective-permute-done | bytes 65568 | tf_op jit(solution)/shard_map/ppermute | solution.py:380
  34.9 2.0 %collective-permute-done.10 = bf16[64,512]{1,0:T(8,128)(2,1)S(1)} collective-permute-done((bf16[64,512]{1,0:T(8,128)(2,1)S(1)}, bf16[64,512]{1,0:T(8,128)(2,1)S(1)}, u32[]{:S(2)}, u32[]{:S(2)}) %collective-permute-start.10) | collective-permute-done | bytes 65568 | tf_op jit(solution)/shard_map/ppermute | solution.py:380
  36.9 0.7 %collective-permute-done.8 = bf16[128,512]{1,0:T(8,128)(2,1)S(1)} collective-permute-done((bf16[128,512]{1,0:T(8,128)(2,1)S(1)}, bf16[128,512]{1,0:T(8,128)(2,1)S(1)}, u32[]{:S(2)}, u32[]{:S(2)}) %collective-permute-start.8) | collective-permute-done | bytes 131104 | tf_op jit(solution)/shard_map/ppermute | solution.py:380
  37.8 2.3 %collective-permute-done.13.refs_3_ = bf16[4,192,512]{2,1,0:T(8,128)(2,1)S(1)} collective-permute-done((bf16[4,192,512]{2,1,0:T(8,128)(2,1)S(1)}, bf16[4,192,512]{2,1,0:T(8,128)(2,1)S(1)}, u32[]{:S(2)}, u32[]{:S(2)}) %collective-permute-start.13) | collective-permute-done | bytes 786464 | tf_op jit(solution)/shard_map/ppermute | solution.py:393
  40.3 3.2 %attend_project.7 = bf16[64,4096]{1,0:T(8,128)(2,1)S(1)} custom-call(s32[2,16]{1,0:T(2,128)S(1)} %copy-done.1, bf16[64,1024]{1,0:T(8,128)(2,1)S(1)} %query_rows.3.query_ref, bf16[2048,512]{1,0:T(8,128)(2,1)S(1)} %key_value_gather.1.kv_ref, bf16[1024,4096]{1,0:T(8,128)(2,1)S(1)} %bitcast.13), custom_call_target="tpu_custom_call" | custom-call | flops 1073741824 | bytes 8388608 | tf_op jit(solution)/shard_map/attend_project/pallas_call | solution.py:300
  43.5 1.8 %collective-permute-start.15 = (bf16[64,4096]{1,0:T(8,128)(2,1)S(1)}, bf16[64,4096]{1,0:T(8,128)(2,1)S(1)}, u32[]{:S(2)}, u32[]{:S(2)}) collective-permute-start(bf16[64,4096]{1,0:T(8,128)(2,1)S(1)} %attend_project.7), channel_id=1, source_target_pairs={{0,16},{1,9},{2,18},{3,11},{4,20},{5,13},{6,22},{7,15},{8,24},{9,1... | collective-permute-start | bytes 1572872 | tf_op jit(solution)/shard_map/ppermute | solution.py:361
  45.2 3.4 %attend_project.5 = bf16[64,4096]{1,0:T(8,128)(2,1)S(1)} custom-call(s32[2,16]{1,0:T(2,128)S(1)} %copy-done.1, bf16[192,1024]{1,0:T(8,128)(2,1)S(1)} %query_rows.2.refs_6_.query_ref, bf16[2048,512]{1,0:T(8,128)(2,1)S(1)} %key_value_gather.1.kv_ref, bf16[1024,4096]{1,0:T(8,128)(2,1)S(1)} %bitcast.13), custom_call_target="tpu_custom_call" | custom-call | flops 1073741824 | bytes 8388608 | tf_op jit(solution)/shard_map/attend_project/pallas_call | solution.py:300
  48.7 1.4 %collective-permute-start.14 = (bf16[64,4096]{1,0:T(8,128)(2,1)S(1)}, bf16[64,4096]{1,0:T(8,128)(2,1)S(1)}, u32[]{:S(2)}, u32[]{:S(2)}) collective-permute-start(bf16[64,4096]{1,0:T(8,128)(2,1)S(1)} %attend_project.5), channel_id=1, source_target_pairs={{0,16},{1,9},{2,18},{3,11},{4,20},{5,13},{6,22},{7,15},{8,24},{9,1... | collective-permute-start | bytes 1572872 | tf_op jit(solution)/shard_map/ppermute | solution.py:361
  50.1 4.1 %attend_project.6 = bf16[64,4096]{1,0:T(8,128)(2,1)S(1)} custom-call(s32[2,16]{1,0:T(2,128)S(1)} %copy-done.1, bf16[192,1024]{1,0:T(8,128)(2,1)S(1)} %query_rows.2.refs_6_.query_ref, bf16[2048,512]{1,0:T(8,128)(2,1)S(1)} %key_value_gather.1.kv_ref, bf16[1024,4096]{1,0:T(8,128)(2,1)S(1)} %bitcast.13), custom_call_target="tpu_custom_call" | custom-call | flops 1073741824 | bytes 8388608 | tf_op jit(solution)/shard_map/attend_project/pallas_call | solution.py:300
  54.3 1.2 %collective-permute-start.16 = (bf16[64,4096]{1,0:T(8,128)(2,1)S(1)}, bf16[64,4096]{1,0:T(8,128)(2,1)S(1)}, u32[]{:S(2)}, u32[]{:S(2)}) collective-permute-start(bf16[64,4096]{1,0:T(8,128)(2,1)S(1)} %add_convert_fusion.1), channel_id=1, source_target_pairs={{0,8},{1,17},{2,10},{3,19},{4,12},{5,21},{6,14},{7,23},{8,0},{9,25... | collective-permute-start | bytes 1572872 | tf_op jit(solution)/shard_map/ppermute | solution.py:361
  55.5 4.1 %attend_project.4 = bf16[64,4096]{1,0:T(8,128)(2,1)S(1)} custom-call(s32[2,16]{1,0:T(2,128)S(1)} %copy-done.1, bf16[192,1024]{1,0:T(8,128)(2,1)S(1)} %query_rows.2.refs_6_.query_ref, bf16[2048,512]{1,0:T(8,128)(2,1)S(1)} %key_value_gather.1.kv_ref, bf16[1024,4096]{1,0:T(8,128)(2,1)S(1)} %bitcast.13), custom_call_target="tpu_custom_call" | custom-call | flops 1073741824 | bytes 8388608 | tf_op jit(solution)/shard_map/attend_project/pallas_call | solution.py:300
  59.6 2.4 %collective-permute-done.14 = bf16[64,4096]{1,0:T(8,128)(2,1)S(1)} collective-permute-done((bf16[64,4096]{1,0:T(8,128)(2,1)S(1)}, bf16[64,4096]{1,0:T(8,128)(2,1)S(1)}, u32[]{:S(2)}, u32[]{:S(2)}) %collective-permute-start.14) | collective-permute-done | bytes 524320 | tf_op jit(solution)/shard_map/ppermute | solution.py:361
  61.9 1.6 %collective-permute-done.16 = bf16[64,4096]{1,0:T(8,128)(2,1)S(1)} collective-permute-done((bf16[64,4096]{1,0:T(8,128)(2,1)S(1)}, bf16[64,4096]{1,0:T(8,128)(2,1)S(1)}, u32[]{:S(2)}, u32[]{:S(2)}) %collective-permute-start.16) | collective-permute-done | bytes 524320 | tf_op jit(solution)/shard_map/ppermute | solution.py:361
  63.5 1.0 %add_convert_fusion = bf16[64,4096]{1,0:T(8,128)(2,1)} fusion(bf16[64,4096]{1,0:T(8,128)(2,1)S(1)} %collective-permute-done.16, bf16[64,4096]{1,0:T(8,128)(2,1)S(1)} %collective-permute-done.14, bf16[64,4096]{1,0:T(8,128)(2,1)S(1)} %attend_project.4), kind=kLoop, calls=%fused_computation | loop fusion | flops 1572864 | bytes 2097152 | tf_op jit(solution)/shard_map/convert_element_type | solution.py:334
  (35 shorter events, 3.1 us)
Async XLA Ops:
  0.0 15.5 %collective-permute-start = (bf16[64,4096]{1,0:T(8,128)(2,1)}, bf16[64,4096]{1,0:T(8,128)(2,1)S(1)}, u32[]{:S(2)}, u32[]{:S(2)}) collective-permute-start(bf16[64,4096]{1,0:T(8,128)(2,1)} %refs_0_.5), channel_id=1, source_target_pairs={{0,8},{1,17},{2,10},{3,19},{4,12},{5,21},{6,14},{7,23},{8,0},{9,25... | collective-permute-start | bytes 1572872 | tf_op jit(solution)/shard_map/ppermute | solution.py:361
  2.9 16.6 %collective-permute-start.1 = (bf16[64,4096]{1,0:T(8,128)(2,1)}, bf16[64,4096]{1,0:T(8,128)(2,1)S(1)}, u32[]{:S(2)}, u32[]{:S(2)}) collective-permute-start(bf16[64,4096]{1,0:T(8,128)(2,1)} %refs_0_.5), channel_id=1, source_target_pairs={{0,16},{1,9},{2,18},{3,11},{4,20},{5,13},{6,22},{7,15},{8,24},{9,1... | collective-permute-start | bytes 1572872 | tf_op jit(solution)/shard_map/ppermute | solution.py:361
  5.2 3.0 %copy-start = (bf16[64,4096]{1,0:T(8,128)(2,1)S(1)}, bf16[64,4096]{1,0:T(8,128)(2,1)}, u32[]{:S(2)}) copy-start(bf16[64,4096]{1,0:T(8,128)(2,1)} %refs_0_.5) | copy-start | bytes 1572868
  5.7 18.1 %slice-start.2 = ((s8[8388608]{0:T(1024)(128)(4,1)}), s8[4194304]{0:T(1024)(128)(4,1)S(1)}, s32[]{:S(2)}) async-start(s8[8388608]{0:T(1024)(128)(4,1)} %bitcast.14), calls=%async_computation.2 | async-start | bytes 8388608
  8.1 15.7 %slice-start.3 = ((s8[8388608]{0:T(1024)(128)(4,1)}), s8[4194304]{0:T(1024)(128)(4,1)S(1)}, s32[]{:S(2)}) async-start(s8[8388608]{0:T(1024)(128)(4,1)} %bitcast.14), calls=%async_computation.3 | async-start | bytes 8388608
  9.1 7.8 %collective-permute-start.2 = (bf16[64,512]{1,0:T(8,128)(2,1)S(1)}, bf16[64,512]{1,0:T(8,128)(2,1)S(1)}, u32[]{:S(2)}, u32[]{:S(2)}) collective-permute-start(bf16[64,512]{1,0:T(8,128)(2,1)S(1)} %key_value_rows.3), channel_id=1, source_target_pairs={{0,6},{1,7},{2,4},{3,5},{4,2},{5,3},{6,0},{7,1},{8,14},{9,15},{10,... | collective-permute-start | bytes 196616 | tf_op jit(solution)/shard_map/ppermute | solution.py:380
  12.7 4.4 %collective-permute-start.3 = (bf16[64,512]{1,0:T(8,128)(2,1)S(1)}, bf16[64,512]{1,0:T(8,128)(2,1)S(1)}, u32[]{:S(2)}, u32[]{:S(2)}) collective-permute-start(bf16[64,512]{1,0:T(8,128)(2,1)S(1)} %key_value_rows.3), channel_id=1, source_target_pairs={{0,2},{1,3},{2,0},{3,1},{4,6},{5,7},{6,4},{7,5},{8,10},{9,11},{10,... | collective-permute-start | bytes 196616 | tf_op jit(solution)/shard_map/ppermute | solution.py:380
  12.7 5.2 %collective-permute-start.4 = (bf16[64,512]{1,0:T(8,128)(2,1)S(1)}, bf16[64,512]{1,0:T(8,128)(2,1)S(1)}, u32[]{:S(2)}, u32[]{:S(2)}) collective-permute-start(bf16[64,512]{1,0:T(8,128)(2,1)S(1)} %key_value_rows.3), channel_id=1, source_target_pairs={{0,4},{1,5},{2,6},{3,7},{4,0},{5,1},{6,2},{7,3},{8,12},{9,13},{10,... | collective-permute-start | bytes 196616 | tf_op jit(solution)/shard_map/ppermute | solution.py:380
  15.5 10.4 %collective-permute-start.9 = (bf16[64,4096]{1,0:T(8,128)(2,1)S(1)}, bf16[64,4096]{1,0:T(8,128)(2,1)S(1)}, u32[]{:S(2)}, u32[]{:S(2)}) collective-permute-start(bf16[64,4096]{1,0:T(8,128)(2,1)S(1)} %collective-permute-done.refs_1_.refs_0_), channel_id=1, source_target_pairs={{0,16},{1,9},{2,18},{3,11},{4,20},{5,13},{6,22},{7,15},{8,24},{9,1... | collective-permute-start | bytes 1572872 | tf_op jit(solution)/shard_map/ppermute | solution.py:361
  17.9 1.6 %collective-permute-start.5 = (bf16[4,64,512]{2,1,0:T(8,128)(2,1)S(1)}, bf16[4,64,512]{2,1,0:T(8,128)(2,1)S(1)}, u32[]{:S(2)}, u32[]{:S(2)}) collective-permute-start(bf16[4,64,512]{2,1,0:T(8,128)(2,1)S(1)} %pad_maximum_fusion.1.refs_6_.refs_0_), channel_id=1, source_target_pairs={{0,1},{1,0},{2,3},{3,2},{4,5},{5,4},{6,7},{7,6},{8,9},{9,8},{10,11... | collective-permute-start | bytes 786440 | tf_op jit(solution)/shard_map/ppermute | solution.py:393
  20.4 10.9 %collective-permute-start.6 = (bf16[128,512]{1,0:T(8,128)(2,1)S(1)}, bf16[128,512]{1,0:T(8,128)(2,1)S(1)}, u32[]{:S(2)}, u32[]{:S(2)}) collective-permute-start(bf16[128,512]{1,0:T(8,128)(2,1)S(1)} %key_value_rows.4.refs_5_), channel_id=1, source_target_pairs={{0,2},{1,3},{2,0},{3,1},{4,6},{5,7},{6,4},{7,5},{8,10},{9,11},{10,... | collective-permute-start | bytes 393224 | tf_op jit(solution)/shard_map/ppermute | solution.py:380
  22.4 8.8 %collective-permute-start.7 = (bf16[128,512]{1,0:T(8,128)(2,1)S(1)}, bf16[128,512]{1,0:T(8,128)(2,1)S(1)}, u32[]{:S(2)}, u32[]{:S(2)}) collective-permute-start(bf16[128,512]{1,0:T(8,128)(2,1)S(1)} %key_value_rows.4.refs_5_), channel_id=1, source_target_pairs={{0,6},{1,7},{2,4},{3,5},{4,2},{5,3},{6,0},{7,1},{8,14},{9,15},{10,... | collective-permute-start | bytes 393224 | tf_op jit(solution)/shard_map/ppermute | solution.py:380
  25.8 14.4 %slice-start = ((s8[8388608]{0:T(1024)(128)(4,1)}), s8[4194304]{0:T(1024)(128)(4,1)S(1)}, s32[]{:S(2)}) async-start(s8[8388608]{0:T(1024)(128)(4,1)} %bitcast.12), calls=%async_computation | async-start | bytes 8388608
  26.8 13.5 %slice-start.1 = ((s8[8388608]{0:T(1024)(128)(4,1)}), s8[4194304]{0:T(1024)(128)(4,1)S(1)}, s32[]{:S(2)}) async-start(s8[8388608]{0:T(1024)(128)(4,1)} %bitcast.12), calls=%async_computation.1 | async-start | bytes 8388608
  26.8 6.5 %collective-permute-start.11 = (bf16[64,512]{1,0:T(8,128)(2,1)S(1)}, bf16[64,512]{1,0:T(8,128)(2,1)S(1)}, u32[]{:S(2)}, u32[]{:S(2)}) collective-permute-start(bf16[64,512]{1,0:T(8,128)(2,1)S(1)} %key_value_rows.5), channel_id=1, source_target_pairs={{0,2},{1,3},{2,0},{3,1},{4,6},{5,7},{6,4},{7,5},{8,10},{9,11},{10,... | collective-permute-start | bytes 196616 | tf_op jit(solution)/shard_map/ppermute | solution.py:380
  28.1 6.8 %collective-permute-start.12 = (bf16[64,512]{1,0:T(8,128)(2,1)S(1)}, bf16[64,512]{1,0:T(8,128)(2,1)S(1)}, u32[]{:S(2)}, u32[]{:S(2)}) collective-permute-start(bf16[64,512]{1,0:T(8,128)(2,1)S(1)} %key_value_rows.5), channel_id=1, source_target_pairs={{0,4},{1,5},{2,6},{3,7},{4,0},{5,1},{6,2},{7,3},{8,12},{9,13},{10,... | collective-permute-start | bytes 196616 | tf_op jit(solution)/shard_map/ppermute | solution.py:380
  30.7 6.2 %collective-permute-start.10 = (bf16[64,512]{1,0:T(8,128)(2,1)S(1)}, bf16[64,512]{1,0:T(8,128)(2,1)S(1)}, u32[]{:S(2)}, u32[]{:S(2)}) collective-permute-start(bf16[64,512]{1,0:T(8,128)(2,1)S(1)} %key_value_rows.5), channel_id=1, source_target_pairs={{0,6},{1,7},{2,4},{3,5},{4,2},{5,3},{6,0},{7,1},{8,14},{9,15},{10,... | collective-permute-start | bytes 196616 | tf_op jit(solution)/shard_map/ppermute | solution.py:380
  31.3 6.3 %collective-permute-start.8 = (bf16[128,512]{1,0:T(8,128)(2,1)S(1)}, bf16[128,512]{1,0:T(8,128)(2,1)S(1)}, u32[]{:S(2)}, u32[]{:S(2)}) collective-permute-start(bf16[128,512]{1,0:T(8,128)(2,1)S(1)} %collective-permute-done.7), channel_id=1, source_target_pairs={{0,2},{1,3},{2,0},{3,1},{4,6},{5,7},{6,4},{7,5},{8,10},{9,11},{10,... | collective-permute-start | bytes 393224 | tf_op jit(solution)/shard_map/ppermute | solution.py:380
  37.7 2.6 %copy-start.1 = (s32[2,16]{1,0:T(2,128)S(1)}, s32[2,16]{1,0:T(2,128)}, u32[]{:S(2)}) copy-start(s32[2,16]{1,0:T(2,128)} %mask_ref.7) | copy-start | bytes 388
  37.7 2.4 %collective-permute-start.13 = (bf16[4,192,512]{2,1,0:T(8,128)(2,1)S(1)}, bf16[4,192,512]{2,1,0:T(8,128)(2,1)S(1)}, u32[]{:S(2)}, u32[]{:S(2)}) collective-permute-start(bf16[4,192,512]{2,1,0:T(8,128)(2,1)S(1)} %pad_maximum_fusion.refs_2_), channel_id=1, source_target_pairs={{0,1},{1,0},{2,3},{3,2},{4,5},{5,4},{6,7},{7,6},{8,9},{9,8},{10,11... | collective-permute-start | bytes 2359304 | tf_op jit(solution)/shard_map/ppermute | solution.py:393
  43.5 10.7 %collective-permute-start.15 = (bf16[64,4096]{1,0:T(8,128)(2,1)S(1)}, bf16[64,4096]{1,0:T(8,128)(2,1)S(1)}, u32[]{:S(2)}, u32[]{:S(2)}) collective-permute-start(bf16[64,4096]{1,0:T(8,128)(2,1)S(1)} %attend_project.7), channel_id=1, source_target_pairs={{0,16},{1,9},{2,18},{3,11},{4,20},{5,13},{6,22},{7,15},{8,24},{9,1... | collective-permute-start | bytes 1572872 | tf_op jit(solution)/shard_map/ppermute | solution.py:361
  48.7 13.3 %collective-permute-start.14 = (bf16[64,4096]{1,0:T(8,128)(2,1)S(1)}, bf16[64,4096]{1,0:T(8,128)(2,1)S(1)}, u32[]{:S(2)}, u32[]{:S(2)}) collective-permute-start(bf16[64,4096]{1,0:T(8,128)(2,1)S(1)} %attend_project.5), channel_id=1, source_target_pairs={{0,16},{1,9},{2,18},{3,11},{4,20},{5,13},{6,22},{7,15},{8,24},{9,1... | collective-permute-start | bytes 1572872 | tf_op jit(solution)/shard_map/ppermute | solution.py:361
  54.3 9.2 %collective-permute-start.16 = (bf16[64,4096]{1,0:T(8,128)(2,1)S(1)}, bf16[64,4096]{1,0:T(8,128)(2,1)S(1)}, u32[]{:S(2)}, u32[]{:S(2)}) collective-permute-start(bf16[64,4096]{1,0:T(8,128)(2,1)S(1)} %add_convert_fusion.1), channel_id=1, source_target_pairs={{0,8},{1,17},{2,10},{3,19},{4,12},{5,21},{6,14},{7,23},{8,0},{9,25... | collective-permute-start | bytes 1572872 | tf_op jit(solution)/shard_map/ppermute | solution.py:361

commit v8 on v7

--- a/solution.py
+++ b/solution.py
@@ -181,7 +181,7 @@
             )
             for head in range(kv_heads)
         ]
-        ones = jnp.ones((WIDE * block, HEAD_WIDTH), jnp.bfloat16)
+        ones = jnp.ones((2 * WIDE * block, HEAD_WIDTH), jnp.bfloat16)
 
         def step(index, state, queries=queries, count=count, width=WIDE):
             first = index * WIDE
@@ -227,16 +227,8 @@
             return tuple(new_state)
 
         def many_steps(step=step, count=count):
-            one, two = step(0, None), step(1, None)
-            state = []
-            for head in range(kv_heads):
-                top = jnp.maximum(one[2 * head], two[2 * head])
-                state += [
-                    top,
-                    one[2 * head + 1] * jnp.exp2(one[2 * head] - top)
-                    + two[2 * head + 1] * jnp.exp2(two[2 * head] - top),
-                ]
-            return lax.fori_loop(2, (count + WIDE - 1) // WIDE, step, tuple(state))
+            state = step(0, None, width=2 * WIDE)
+            return lax.fori_loop(2, (count + WIDE - 1) // WIDE, step, state)
 
         state = lax.cond(count > MOST, many_steps, functools.partial(step, 0, None, width=MOST))
         for head in range(kv_heads):

time: 64.7 us -> 65.2 us (level)
  transfers between devices with their start and end apart: 17 -> 17, of which waited for: 10 -> 10; matrix products, arithmetic and copies ran while one was open for 2% -> 2% of each run, Pallas kernels for 31% -> 32%
where the time goes in v8:
time: 65.2 us; the launch traced here: 65 us
  Pallas kernels  24.1 us (37%)
  starting transfers between devices  23.6 us (36%)
  waiting for transfers between devices  14.6 us (22%)
  other arithmetic  2.47 us (4%)
    pallas_call x4, Pallas kernels, attend(): pl.pallas_call(functools.partial(attend_kernel, slots, held, placed), out...  15.2 us
    ppermute x9, starting transfers between devices, across_chips(): lax.ppermute(value, 'blk', [(b, b ^ 2 * by) for b in range(blk_count)])  12.7 us
    ppermute x6, starting transfers between devices, send(): return lax.ppermute(value, ('grp', 'blk'), pairs)  10.7 us
    ppermute x6, waiting for transfers between devices, send(): return lax.ppermute(value, ('grp', 'blk'), pairs)  5.47 us
    ppermute x9, waiting for transfers between devices, across_chips(): lax.ppermute(value, 'blk', [(b, b ^ 2 * by) for b in range(blk_count)])  5.31 us
    ppermute x2, waiting for transfers between devices, with_other_core(): lax.ppermute(held, 'blk', [(b, b ^ 1) for b in range(blk_count)])  3.79 us
    pallas_call x2, Pallas kernels, query_rows(): pl.pallas_call(functools.partial(query_kernel, slots), out_shape=jax.Shap...  3.67 us
    pallas_call x3, Pallas kernels, key_value_rows(): pl.pallas_call(functools.partial(key_value_kernel, len(pieces), slots), o...  2.65 us
  transfers between devices with their start and end apart: 17, of which 10 were waited for; matrix products, arithmetic and copies ran while one was open for 2% of the time, Pallas kernels for 32%

profile of v8, /device:TPU:0, one launch (start us, length us, event | category | flops | bytes accessed | tf_op | source)
XLA Modules:
  0.0 65.0 jit_solution(3196352698801463356)
XLA Ops:
  0.0 2.9 %collective-permute-start = (bf16[64,4096]{1,0:T(8,128)(2,1)}, bf16[64,4096]{1,0:T(8,128)(2,1)S(1)}, u32[]{:S(2)}, u32[]{:S(2)}) collective-permute-start(bf16[64,4096]{1,0:T(8,128)(2,1)} %refs_0_.5), channel_id=1, source_target_pairs={{0,8},{1,17},{2,10},{3,19},{4,12},{5,21},{6,14},{7,23},{8,0},{9,25... | collective-permute-start | bytes 1572872 | tf_op jit(solution)/shard_map/ppermute | solution.py:353
  2.9 1.5 %collective-permute-start.1 = (bf16[64,4096]{1,0:T(8,128)(2,1)}, bf16[64,4096]{1,0:T(8,128)(2,1)S(1)}, u32[]{:S(2)}, u32[]{:S(2)}) collective-permute-start(bf16[64,4096]{1,0:T(8,128)(2,1)} %refs_0_.5), channel_id=1, source_target_pairs={{0,16},{1,9},{2,18},{3,11},{4,20},{5,13},{6,22},{7,15},{8,24},{9,1... | collective-permute-start | bytes 1572872 | tf_op jit(solution)/shard_map/ppermute | solution.py:353
  5.7 2.4 %preload.1 = (bf16[4096,256]{1,0:T(8,128)(2,1)S(1)}, bf16[4096,256]{1,0:T(8,128)(2,1)S(1)}) custom-call(bf16[4096,256]{1,0:T(8,128)(2,1)} %refs_0_.4, bf16[4096,256]{1,0:T(8,128)(2,1)} %refs_1_.2, f32[256,128]{1,0:T(8,128)S(1)} %get-tuple-element.18.refs_4_.refs_2_.refs_3_, f32[256,128]{1,0:T(8,128)S(1)} %get-tuple-element.17.refs_5_.refs_3_.refs_4_), custom_call_target="tpu_custom_call" | custom-call | tf_op jit(solution)/shard_map/preload/pallas_call | solution.py:47
  8.1 0.9 %key_value_rows.3 = bf16[64,512]{1,0:T(8,128)(2,1)S(1)} custom-call(bf16[64,4096]{1,0:T(8,128)(2,1)S(1)} %copy-done, bf16[4096,256]{1,0:T(8,128)(2,1)S(1)} %get-tuple-element.11.refs_1_.refs_2_, bf16[4096,256]{1,0:T(8,128)(2,1)S(1)} %get-tuple-element.12.refs_2_.refs_3_, f32[256,128]{1,0:T(8,128)S(1)} %get-tuple-element.18.refs_4_.refs_2_.refs_3_, ...), custom_call_target="tpu_custom_call" | custom-call | flops 268435456 | bytes 4194304 | tf_op jit(solution)/shard_map/key_value_rows/pallas_call | solution.py:104
  9.1 3.7 %collective-permute-start.2 = (bf16[64,512]{1,0:T(8,128)(2,1)S(1)}, bf16[64,512]{1,0:T(8,128)(2,1)S(1)}, u32[]{:S(2)}, u32[]{:S(2)}) collective-permute-start(bf16[64,512]{1,0:T(8,128)(2,1)S(1)} %key_value_rows.3), channel_id=1, source_target_pairs={{0,6},{1,7},{2,4},{3,5},{4,2},{5,3},{6,0},{7,1},{8,14},{9,15},{10,... | collective-permute-start | bytes 196616 | tf_op jit(solution)/shard_map/ppermute | solution.py:372
  12.7 0.8 %collective-permute-start.4 = (bf16[64,512]{1,0:T(8,128)(2,1)S(1)}, bf16[64,512]{1,0:T(8,128)(2,1)S(1)}, u32[]{:S(2)}, u32[]{:S(2)}) collective-permute-start(bf16[64,512]{1,0:T(8,128)(2,1)S(1)} %key_value_rows.3), channel_id=1, source_target_pairs={{0,4},{1,5},{2,6},{3,7},{4,0},{5,1},{6,2},{7,3},{8,12},{9,13},{10,... | collective-permute-start | bytes 196616 | tf_op jit(solution)/shard_map/ppermute | solution.py:372
  13.5 1.9 %collective-permute-done.refs_1_.refs_0_ = bf16[64,4096]{1,0:T(8,128)(2,1)S(1)} collective-permute-done((bf16[64,4096]{1,0:T(8,128)(2,1)}, bf16[64,4096]{1,0:T(8,128)(2,1)S(1)}, u32[]{:S(2)}, u32[]{:S(2)}) %collective-permute-start) | collective-permute-done | bytes 524320 | tf_op jit(solution)/shard_map/ppermute | solution.py:353
  15.5 1.4 %collective-permute-start.9 = (bf16[64,4096]{1,0:T(8,128)(2,1)S(1)}, bf16[64,4096]{1,0:T(8,128)(2,1)S(1)}, u32[]{:S(2)}, u32[]{:S(2)}) collective-permute-start(bf16[64,4096]{1,0:T(8,128)(2,1)S(1)} %collective-permute-done.refs_1_.refs_0_), channel_id=1, source_target_pairs={{0,16},{1,9},{2,18},{3,11},{4,20},{5,13},{6,22},{7,15},{8,24},{9,1... | collective-permute-start | bytes 1572872 | tf_op jit(solution)/shard_map/ppermute | solution.py:353
  17.1 0.8 %collective-permute-done.4 = bf16[64,512]{1,0:T(8,128)(2,1)S(1)} collective-permute-done((bf16[64,512]{1,0:T(8,128)(2,1)S(1)}, bf16[64,512]{1,0:T(8,128)(2,1)S(1)}, u32[]{:S(2)}, u32[]{:S(2)}) %collective-permute-start.4) | collective-permute-done | bytes 65568 | tf_op jit(solution)/shard_map/ppermute | solution.py:372
  18.0 1.5 %collective-permute-done.5.refs_7_.refs_1_ = bf16[4,64,512]{2,1,0:T(8,128)(2,1)S(1)} collective-permute-done((bf16[4,64,512]{2,1,0:T(8,128)(2,1)S(1)}, bf16[4,64,512]{2,1,0:T(8,128)(2,1)S(1)}, u32[]{:S(2)}, u32[]{:S(2)}) %collective-permute-start.5) | collective-permute-done | bytes 262176 | tf_op jit(solution)/shard_map/ppermute | solution.py:385
  19.5 0.8 %key_value_rows.4.refs_5_ = bf16[128,512]{1,0:T(8,128)(2,1)S(1)} custom-call(bf16[64,4096]{1,0:T(8,128)(2,1)S(1)} %collective-permute-done.refs_1_.refs_0_, bf16[64,4096]{1,0:T(8,128)(2,1)S(1)} %collective-permute-done.1.refs_2_.refs_1_, bf16[4096,256]{1,0:T(8,128)(2,1)S(1)} %get-tuple-element.11.refs_1_.refs_2_, ...), custom_call_target="tpu_custom_call" | custom-call | flops 536870912 | bytes 4194304 | tf_op jit(solution)/shard_map/key_value_rows/pallas_call | solution.py:104
  20.4 2.1 %collective-permute-start.6 = (bf16[128,512]{1,0:T(8,128)(2,1)S(1)}, bf16[128,512]{1,0:T(8,128)(2,1)S(1)}, u32[]{:S(2)}, u32[]{:S(2)}) collective-permute-start(bf16[128,512]{1,0:T(8,128)(2,1)S(1)} %key_value_rows.4.refs_5_), channel_id=1, source_target_pairs={{0,2},{1,3},{2,0},{3,1},{4,6},{5,7},{6,4},{7,5},{8,10},{9,11},{10,... | collective-permute-start | bytes 393224 | tf_op jit(solution)/shard_map/ppermute | solution.py:372
  22.4 1.4 %collective-permute-start.7 = (bf16[128,512]{1,0:T(8,128)(2,1)S(1)}, bf16[128,512]{1,0:T(8,128)(2,1)S(1)}, u32[]{:S(2)}, u32[]{:S(2)}) collective-permute-start(bf16[128,512]{1,0:T(8,128)(2,1)S(1)} %key_value_rows.4.refs_5_), channel_id=1, source_target_pairs={{0,6},{1,7},{2,4},{3,5},{4,2},{5,3},{6,0},{7,1},{8,14},{9,15},{10,... | collective-permute-start | bytes 393224 | tf_op jit(solution)/shard_map/ppermute | solution.py:372
  23.8 2.0 %query_rows.2.refs_6_.query_ref = bf16[192,1024]{1,0:T(8,128)(2,1)S(1)} custom-call(bf16[64,4096]{1,0:T(8,128)(2,1)S(1)} %copy-done, bf16[64,4096]{1,0:T(8,128)(2,1)S(1)} %collective-permute-done.refs_1_.refs_0_, bf16[64,4096]{1,0:T(8,128)(2,1)S(1)} %collective-permute-done.1.refs_2_.refs_1_, bf16[4096,1024]{1,0:T(8,128)(2,1)S(1)} %bitcast.15, ...), custom_call_target="tpu_custom_call" | custom-call | flops 1610612736 | bytes 8388608 | tf_op jit(solution)/shard_map/query_rows/pallas_call | solution.py:138
  25.9 0.9 %key_value_rows.5 = bf16[64,512]{1,0:T(8,128)(2,1)S(1)} custom-call(bf16[64,4096]{1,0:T(8,128)(2,1)S(1)} %collective-permute-done.9.refs_0_, bf16[4096,256]{1,0:T(8,128)(2,1)S(1)} %get-tuple-element.11.refs_1_.refs_2_, bf16[4096,256]{1,0:T(8,128)(2,1)S(1)} %get-tuple-element.12.refs_2_.refs_3_, f32[256,128]{1,0:T(8,128)S(1)} %get-tuple-element.18.refs_4_.refs_2_.refs_3_, ...), custom_call_target="tpu_custom_call" | custom-call | flops 268435456 | bytes 4194304 | tf_op jit(solution)/shard_map/key_value_rows/pallas_call | solution.py:104
  26.8 1.3 %collective-permute-start.11 = (bf16[64,512]{1,0:T(8,128)(2,1)S(1)}, bf16[64,512]{1,0:T(8,128)(2,1)S(1)}, u32[]{:S(2)}, u32[]{:S(2)}) collective-permute-start(bf16[64,512]{1,0:T(8,128)(2,1)S(1)} %key_value_rows.5), channel_id=1, source_target_pairs={{0,2},{1,3},{2,0},{3,1},{4,6},{5,7},{6,4},{7,5},{8,10},{9,11},{10,... | collective-permute-start | bytes 196616 | tf_op jit(solution)/shard_map/ppermute | solution.py:372
  28.1 2.6 %collective-permute-start.12 = (bf16[64,512]{1,0:T(8,128)(2,1)S(1)}, bf16[64,512]{1,0:T(8,128)(2,1)S(1)}, u32[]{:S(2)}, u32[]{:S(2)}) collective-permute-start(bf16[64,512]{1,0:T(8,128)(2,1)S(1)} %key_value_rows.5), channel_id=1, source_target_pairs={{0,4},{1,5},{2,6},{3,7},{4,0},{5,1},{6,2},{7,3},{8,12},{9,13},{10,... | collective-permute-start | bytes 196616 | tf_op jit(solution)/shard_map/ppermute | solution.py:372
  31.6 1.7 %query_rows.3.query_ref = bf16[64,1024]{1,0:T(8,128)(2,1)S(1)} custom-call(bf16[64,4096]{1,0:T(8,128)(2,1)S(1)} %collective-permute-done.9.refs_0_, bf16[4096,1024]{1,0:T(8,128)(2,1)S(1)} %bitcast.15, f32[256,128]{1,0:T(8,128)S(1)} %get-tuple-element.18.refs_4_.refs_2_.refs_3_, f32[256,128]{1,0:T(8,128)S(1)} %get-tuple-element.17.refs_5_.refs_3_.refs_4_), custom_call_target="tpu_custom_call" | custom-call | flops 536870912 | bytes 8388608 | tf_op jit(solution)/shard_map/query_rows/pallas_call | solution.py:138
  33.3 1.6 %collective-permute-done.12 = bf16[64,512]{1,0:T(8,128)(2,1)S(1)} collective-permute-done((bf16[64,512]{1,0:T(8,128)(2,1)S(1)}, bf16[64,512]{1,0:T(8,128)(2,1)S(1)}, u32[]{:S(2)}, u32[]{:S(2)}) %collective-permute-start.12) | collective-permute-done | bytes 65568 | tf_op jit(solution)/shard_map/ppermute | solution.py:372
  34.9 2.0 %collective-permute-done.10 = bf16[64,512]{1,0:T(8,128)(2,1)S(1)} collective-permute-done((bf16[64,512]{1,0:T(8,128)(2,1)S(1)}, bf16[64,512]{1,0:T(8,128)(2,1)S(1)}, u32[]{:S(2)}, u32[]{:S(2)}) %collective-permute-start.10) | collective-permute-done | bytes 65568 | tf_op jit(solution)/shard_map/ppermute | solution.py:372
  36.9 0.7 %collective-permute-done.8 = bf16[128,512]{1,0:T(8,128)(2,1)S(1)} collective-permute-done((bf16[128,512]{1,0:T(8,128)(2,1)S(1)}, bf16[128,512]{1,0:T(8,128)(2,1)S(1)}, u32[]{:S(2)}, u32[]{:S(2)}) %collective-permute-start.8) | collective-permute-done | bytes 131104 | tf_op jit(solution)/shard_map/ppermute | solution.py:372
  37.8 2.3 %collective-permute-done.13.refs_3_ = bf16[4,192,512]{2,1,0:T(8,128)(2,1)S(1)} collective-permute-done((bf16[4,192,512]{2,1,0:T(8,128)(2,1)S(1)}, bf16[4,192,512]{2,1,0:T(8,128)(2,1)S(1)}, u32[]{:S(2)}, u32[]{:S(2)}) %collective-permute-start.13) | collective-permute-done | bytes 786464 | tf_op jit(solution)/shard_map/ppermute | solution.py:385
  40.3 3.2 %attend_project.7 = bf16[64,4096]{1,0:T(8,128)(2,1)S(1)} custom-call(s32[2,16]{1,0:T(2,128)S(1)} %copy-done.1, bf16[64,1024]{1,0:T(8,128)(2,1)S(1)} %query_rows.3.query_ref, bf16[2048,512]{1,0:T(8,128)(2,1)S(1)} %key_value_gather.1.kv_ref, bf16[1024,4096]{1,0:T(8,128)(2,1)S(1)} %bitcast.13), custom_call_target="tpu_custom_call" | custom-call | flops 1073741824 | bytes 8388608 | tf_op jit(solution)/shard_map/attend_project/pallas_call | solution.py:292
  43.5 2.0 %collective-permute-start.15 = (bf16[64,4096]{1,0:T(8,128)(2,1)S(1)}, bf16[64,4096]{1,0:T(8,128)(2,1)S(1)}, u32[]{:S(2)}, u32[]{:S(2)}) collective-permute-start(bf16[64,4096]{1,0:T(8,128)(2,1)S(1)} %attend_project.7), channel_id=1, source_target_pairs={{0,16},{1,9},{2,18},{3,11},{4,20},{5,13},{6,22},{7,15},{8,24},{9,1... | collective-permute-start | bytes 1572872 | tf_op jit(solution)/shard_map/ppermute | solution.py:353
  45.5 3.4 %attend_project.5 = bf16[64,4096]{1,0:T(8,128)(2,1)S(1)} custom-call(s32[2,16]{1,0:T(2,128)S(1)} %copy-done.1, bf16[192,1024]{1,0:T(8,128)(2,1)S(1)} %query_rows.2.refs_6_.query_ref, bf16[2048,512]{1,0:T(8,128)(2,1)S(1)} %key_value_gather.1.kv_ref, bf16[1024,4096]{1,0:T(8,128)(2,1)S(1)} %bitcast.13), custom_call_target="tpu_custom_call" | custom-call | flops 1073741824 | bytes 8388608 | tf_op jit(solution)/shard_map/attend_project/pallas_call | solution.py:292
  48.9 1.4 %collective-permute-start.14 = (bf16[64,4096]{1,0:T(8,128)(2,1)S(1)}, bf16[64,4096]{1,0:T(8,128)(2,1)S(1)}, u32[]{:S(2)}, u32[]{:S(2)}) collective-permute-start(bf16[64,4096]{1,0:T(8,128)(2,1)S(1)} %attend_project.5), channel_id=1, source_target_pairs={{0,16},{1,9},{2,18},{3,11},{4,20},{5,13},{6,22},{7,15},{8,24},{9,1... | collective-permute-start | bytes 1572872 | tf_op jit(solution)/shard_map/ppermute | solution.py:353
  50.3 4.3 %attend_project.6 = bf16[64,4096]{1,0:T(8,128)(2,1)S(1)} custom-call(s32[2,16]{1,0:T(2,128)S(1)} %copy-done.1, bf16[192,1024]{1,0:T(8,128)(2,1)S(1)} %query_rows.2.refs_6_.query_ref, bf16[2048,512]{1,0:T(8,128)(2,1)S(1)} %key_value_gather.1.kv_ref, bf16[1024,4096]{1,0:T(8,128)(2,1)S(1)} %bitcast.13), custom_call_target="tpu_custom_call" | custom-call | flops 1073741824 | bytes 8388608 | tf_op jit(solution)/shard_map/attend_project/pallas_call | solution.py:292
  54.8 1.4 %collective-permute-start.16 = (bf16[64,4096]{1,0:T(8,128)(2,1)S(1)}, bf16[64,4096]{1,0:T(8,128)(2,1)S(1)}, u32[]{:S(2)}, u32[]{:S(2)}) collective-permute-start(bf16[64,4096]{1,0:T(8,128)(2,1)S(1)} %add_convert_fusion.1), channel_id=1, source_target_pairs={{0,8},{1,17},{2,10},{3,19},{4,12},{5,21},{6,14},{7,23},{8,0},{9,25... | collective-permute-start | bytes 1572872 | tf_op jit(solution)/shard_map/ppermute | solution.py:353
  56.2 4.3 %attend_project.4 = bf16[64,4096]{1,0:T(8,128)(2,1)S(1)} custom-call(s32[2,16]{1,0:T(2,128)S(1)} %copy-done.1, bf16[192,1024]{1,0:T(8,128)(2,1)S(1)} %query_rows.2.refs_6_.query_ref, bf16[2048,512]{1,0:T(8,128)(2,1)S(1)} %key_value_gather.1.kv_ref, bf16[1024,4096]{1,0:T(8,128)(2,1)S(1)} %bitcast.13), custom_call_target="tpu_custom_call" | custom-call | flops 1073741824 | bytes 8388608 | tf_op jit(solution)/shard_map/attend_project/pallas_call | solution.py:292
  60.5 1.9 %collective-permute-done.14 = bf16[64,4096]{1,0:T(8,128)(2,1)S(1)} collective-permute-done((bf16[64,4096]{1,0:T(8,128)(2,1)S(1)}, bf16[64,4096]{1,0:T(8,128)(2,1)S(1)}, u32[]{:S(2)}, u32[]{:S(2)}) %collective-permute-start.14) | collective-permute-done | bytes 524320 | tf_op jit(solution)/shard_map/ppermute | solution.py:353
  62.4 1.6 %collective-permute-done.16 = bf16[64,4096]{1,0:T(8,128)(2,1)S(1)} collective-permute-done((bf16[64,4096]{1,0:T(8,128)(2,1)S(1)}, bf16[64,4096]{1,0:T(8,128)(2,1)S(1)}, u32[]{:S(2)}, u32[]{:S(2)}) %collective-permute-start.16) | collective-permute-done | bytes 524320 | tf_op jit(solution)/shard_map/ppermute | solution.py:353
  64.0 1.0 %add_convert_fusion = bf16[64,4096]{1,0:T(8,128)(2,1)} fusion(bf16[64,4096]{1,0:T(8,128)(2,1)S(1)} %collective-permute-done.16, bf16[64,4096]{1,0:T(8,128)(2,1)S(1)} %collective-permute-done.14, bf16[64,4096]{1,0:T(8,128)(2,1)S(1)} %attend_project.4), kind=kLoop, calls=%fused_computation | loop fusion | flops 1572864 | bytes 2097152 | tf_op jit(solution)/shard_map/convert_element_type | solution.py:326
  (35 shorter events, 3.1 us)
Async XLA Ops:
  0.0 15.5 %collective-permute-start = (bf16[64,4096]{1,0:T(8,128)(2,1)}, bf16[64,4096]{1,0:T(8,128)(2,1)S(1)}, u32[]{:S(2)}, u32[]{:S(2)}) collective-permute-start(bf16[64,4096]{1,0:T(8,128)(2,1)} %refs_0_.5), channel_id=1, source_target_pairs={{0,8},{1,17},{2,10},{3,19},{4,12},{5,21},{6,14},{7,23},{8,0},{9,25... | collective-permute-start | bytes 1572872 | tf_op jit(solution)/shard_map/ppermute | solution.py:353
  2.9 16.6 %collective-permute-start.1 = (bf16[64,4096]{1,0:T(8,128)(2,1)}, bf16[64,4096]{1,0:T(8,128)(2,1)S(1)}, u32[]{:S(2)}, u32[]{:S(2)}) collective-permute-start(bf16[64,4096]{1,0:T(8,128)(2,1)} %refs_0_.5), channel_id=1, source_target_pairs={{0,16},{1,9},{2,18},{3,11},{4,20},{5,13},{6,22},{7,15},{8,24},{9,1... | collective-permute-start | bytes 1572872 | tf_op jit(solution)/shard_map/ppermute | solution.py:353
  5.2 3.0 %copy-start = (bf16[64,4096]{1,0:T(8,128)(2,1)S(1)}, bf16[64,4096]{1,0:T(8,128)(2,1)}, u32[]{:S(2)}) copy-start(bf16[64,4096]{1,0:T(8,128)(2,1)} %refs_0_.5) | copy-start | bytes 1572868
  5.7 18.1 %slice-start.2 = ((s8[8388608]{0:T(1024)(128)(4,1)}), s8[4194304]{0:T(1024)(128)(4,1)S(1)}, s32[]{:S(2)}) async-start(s8[8388608]{0:T(1024)(128)(4,1)} %bitcast.14), calls=%async_computation.2 | async-start | bytes 8388608
  8.1 15.7 %slice-start.3 = ((s8[8388608]{0:T(1024)(128)(4,1)}), s8[4194304]{0:T(1024)(128)(4,1)S(1)}, s32[]{:S(2)}) async-start(s8[8388608]{0:T(1024)(128)(4,1)} %bitcast.14), calls=%async_computation.3 | async-start | bytes 8388608
  9.1 7.8 %collective-permute-start.2 = (bf16[64,512]{1,0:T(8,128)(2,1)S(1)}, bf16[64,512]{1,0:T(8,128)(2,1)S(1)}, u32[]{:S(2)}, u32[]{:S(2)}) collective-permute-start(bf16[64,512]{1,0:T(8,128)(2,1)S(1)} %key_value_rows.3), channel_id=1, source_target_pairs={{0,6},{1,7},{2,4},{3,5},{4,2},{5,3},{6,0},{7,1},{8,14},{9,15},{10,... | collective-permute-start | bytes 196616 | tf_op jit(solution)/shard_map/ppermute | solution.py:372
  12.7 4.4 %collective-permute-start.3 = (bf16[64,512]{1,0:T(8,128)(2,1)S(1)}, bf16[64,512]{1,0:T(8,128)(2,1)S(1)}, u32[]{:S(2)}, u32[]{:S(2)}) collective-permute-start(bf16[64,512]{1,0:T(8,128)(2,1)S(1)} %key_value_rows.3), channel_id=1, source_target_pairs={{0,2},{1,3},{2,0},{3,1},{4,6},{5,7},{6,4},{7,5},{8,10},{9,11},{10,... | collective-permute-start | bytes 196616 | tf_op jit(solution)/shard_map/ppermute | solution.py:372
  12.7 5.2 %collective-permute-start.4 = (bf16[64,512]{1,0:T(8,128)(2,1)S(1)}, bf16[64,512]{1,0:T(8,128)(2,1)S(1)}, u32[]{:S(2)}, u32[]{:S(2)}) collective-permute-start(bf16[64,512]{1,0:T(8,128)(2,1)S(1)} %key_value_rows.3), channel_id=1, source_target_pairs={{0,4},{1,5},{2,6},{3,7},{4,0},{5,1},{6,2},{7,3},{8,12},{9,13},{10,... | collective-permute-start | bytes 196616 | tf_op jit(solution)/shard_map/ppermute | solution.py:372
  15.5 10.4 %collective-permute-start.9 = (bf16[64,4096]{1,0:T(8,128)(2,1)S(1)}, bf16[64,4096]{1,0:T(8,128)(2,1)S(1)}, u32[]{:S(2)}, u32[]{:S(2)}) collective-permute-start(bf16[64,4096]{1,0:T(8,128)(2,1)S(1)} %collective-permute-done.refs_1_.refs_0_), channel_id=1, source_target_pairs={{0,16},{1,9},{2,18},{3,11},{4,20},{5,13},{6,22},{7,15},{8,24},{9,1... | collective-permute-start | bytes 1572872 | tf_op jit(solution)/shard_map/ppermute | solution.py:353
  17.9 1.6 %collective-permute-start.5 = (bf16[4,64,512]{2,1,0:T(8,128)(2,1)S(1)}, bf16[4,64,512]{2,1,0:T(8,128)(2,1)S(1)}, u32[]{:S(2)}, u32[]{:S(2)}) collective-permute-start(bf16[4,64,512]{2,1,0:T(8,128)(2,1)S(1)} %pad_maximum_fusion.1.refs_6_.refs_0_), channel_id=1, source_target_pairs={{0,1},{1,0},{2,3},{3,2},{4,5},{5,4},{6,7},{7,6},{8,9},{9,8},{10,11... | collective-permute-start | bytes 786440 | tf_op jit(solution)/shard_map/ppermute | solution.py:385
  20.4 10.9 %collective-permute-start.6 = (bf16[128,512]{1,0:T(8,128)(2,1)S(1)}, bf16[128,512]{1,0:T(8,128)(2,1)S(1)}, u32[]{:S(2)}, u32[]{:S(2)}) collective-permute-start(bf16[128,512]{1,0:T(8,128)(2,1)S(1)} %key_value_rows.4.refs_5_), channel_id=1, source_target_pairs={{0,2},{1,3},{2,0},{3,1},{4,6},{5,7},{6,4},{7,5},{8,10},{9,11},{10,... | collective-permute-start | bytes 393224 | tf_op jit(solution)/shard_map/ppermute | solution.py:372
  22.4 8.8 %collective-permute-start.7 = (bf16[128,512]{1,0:T(8,128)(2,1)S(1)}, bf16[128,512]{1,0:T(8,128)(2,1)S(1)}, u32[]{:S(2)}, u32[]{:S(2)}) collective-permute-start(bf16[128,512]{1,0:T(8,128)(2,1)S(1)} %key_value_rows.4.refs_5_), channel_id=1, source_target_pairs={{0,6},{1,7},{2,4},{3,5},{4,2},{5,3},{6,0},{7,1},{8,14},{9,15},{10,... | collective-permute-start | bytes 393224 | tf_op jit(solution)/shard_map/ppermute | solution.py:372
  25.8 14.4 %slice-start = ((s8[8388608]{0:T(1024)(128)(4,1)}), s8[4194304]{0:T(1024)(128)(4,1)S(1)}, s32[]{:S(2)}) async-start(s8[8388608]{0:T(1024)(128)(4,1)} %bitcast.12), calls=%async_computation | async-start | bytes 8388608
  26.8 13.5 %slice-start.1 = ((s8[8388608]{0:T(1024)(128)(4,1)}), s8[4194304]{0:T(1024)(128)(4,1)S(1)}, s32[]{:S(2)}) async-start(s8[8388608]{0:T(1024)(128)(4,1)} %bitcast.12), calls=%async_computation.1 | async-start | bytes 8388608
  26.8 6.5 %collective-permute-start.11 = (bf16[64,512]{1,0:T(8,128)(2,1)S(1)}, bf16[64,512]{1,0:T(8,128)(2,1)S(1)}, u32[]{:S(2)}, u32[]{:S(2)}) collective-permute-start(bf16[64,512]{1,0:T(8,128)(2,1)S(1)} %key_value_rows.5), channel_id=1, source_target_pairs={{0,2},{1,3},{2,0},{3,1},{4,6},{5,7},{6,4},{7,5},{8,10},{9,11},{10,... | collective-permute-start | bytes 196616 | tf_op jit(solution)/shard_map/ppermute | solution.py:372
  28.1 6.8 %collective-permute-start.12 = (bf16[64,512]{1,0:T(8,128)(2,1)S(1)}, bf16[64,512]{1,0:T(8,128)(2,1)S(1)}, u32[]{:S(2)}, u32[]{:S(2)}) collective-permute-start(bf16[64,512]{1,0:T(8,128)(2,1)S(1)} %key_value_rows.5), channel_id=1, source_target_pairs={{0,4},{1,5},{2,6},{3,7},{4,0},{5,1},{6,2},{7,3},{8,12},{9,13},{10,... | collective-permute-start | bytes 196616 | tf_op jit(solution)/shard_map/ppermute | solution.py:372
  30.7 6.2 %collective-permute-start.10 = (bf16[64,512]{1,0:T(8,128)(2,1)S(1)}, bf16[64,512]{1,0:T(8,128)(2,1)S(1)}, u32[]{:S(2)}, u32[]{:S(2)}) collective-permute-start(bf16[64,512]{1,0:T(8,128)(2,1)S(1)} %key_value_rows.5), channel_id=1, source_target_pairs={{0,6},{1,7},{2,4},{3,5},{4,2},{5,3},{6,0},{7,1},{8,14},{9,15},{10,... | collective-permute-start | bytes 196616 | tf_op jit(solution)/shard_map/ppermute | solution.py:372
  31.3 6.3 %collective-permute-start.8 = (bf16[128,512]{1,0:T(8,128)(2,1)S(1)}, bf16[128,512]{1,0:T(8,128)(2,1)S(1)}, u32[]{:S(2)}, u32[]{:S(2)}) collective-permute-start(bf16[128,512]{1,0:T(8,128)(2,1)S(1)} %collective-permute-done.7), channel_id=1, source_target_pairs={{0,2},{1,3},{2,0},{3,1},{4,6},{5,7},{6,4},{7,5},{8,10},{9,11},{10,... | collective-permute-start | bytes 393224 | tf_op jit(solution)/shard_map/ppermute | solution.py:372
  37.7 2.6 %copy-start.1 = (s32[2,16]{1,0:T(2,128)S(1)}, s32[2,16]{1,0:T(2,128)}, u32[]{:S(2)}) copy-start(s32[2,16]{1,0:T(2,128)} %mask_ref.7) | copy-start | bytes 388
  37.7 2.4 %collective-permute-start.13 = (bf16[4,192,512]{2,1,0:T(8,128)(2,1)S(1)}, bf16[4,192,512]{2,1,0:T(8,128)(2,1)S(1)}, u32[]{:S(2)}, u32[]{:S(2)}) collective-permute-start(bf16[4,192,512]{2,1,0:T(8,128)(2,1)S(1)} %pad_maximum_fusion.refs_2_), channel_id=1, source_target_pairs={{0,1},{1,0},{2,3},{3,2},{4,5},{5,4},{6,7},{7,6},{8,9},{9,8},{10,11... | collective-permute-start | bytes 2359304 | tf_op jit(solution)/shard_map/ppermute | solution.py:385
  43.5 11.2 %collective-permute-start.15 = (bf16[64,4096]{1,0:T(8,128)(2,1)S(1)}, bf16[64,4096]{1,0:T(8,128)(2,1)S(1)}, u32[]{:S(2)}, u32[]{:S(2)}) collective-permute-start(bf16[64,4096]{1,0:T(8,128)(2,1)S(1)} %attend_project.7), channel_id=1, source_target_pairs={{0,16},{1,9},{2,18},{3,11},{4,20},{5,13},{6,22},{7,15},{8,24},{9,1... | collective-permute-start | bytes 1572872 | tf_op jit(solution)/shard_map/ppermute | solution.py:353
  48.9 13.5 %collective-permute-start.14 = (bf16[64,4096]{1,0:T(8,128)(2,1)S(1)}, bf16[64,4096]{1,0:T(8,128)(2,1)S(1)}, u32[]{:S(2)}, u32[]{:S(2)}) collective-permute-start(bf16[64,4096]{1,0:T(8,128)(2,1)S(1)} %attend_project.5), channel_id=1, source_target_pairs={{0,16},{1,9},{2,18},{3,11},{4,20},{5,13},{6,22},{7,15},{8,24},{9,1... | collective-permute-start | bytes 1572872 | tf_op jit(solution)/shard_map/ppermute | solution.py:353
  54.8 9.2 %collective-permute-start.16 = (bf16[64,4096]{1,0:T(8,128)(2,1)S(1)}, bf16[64,4096]{1,0:T(8,128)(2,1)S(1)}, u32[]{:S(2)}, u32[]{:S(2)}) collective-permute-start(bf16[64,4096]{1,0:T(8,128)(2,1)S(1)} %add_convert_fusion.1), channel_id=1, source_target_pairs={{0,8},{1,17},{2,10},{3,19},{4,12},{5,21},{6,14},{7,23},{8,0},{9,25... | collective-permute-start | bytes 1572872 | tf_op jit(solution)/shard_map/ppermute | solution.py:353
